TPU v7x, 512 devices: a whole 4x4x16 slice. The times are simulated.
512 devices in a mesh: dp: 4 (over y), seq: 16 (over x, z_hi, core), head: 8 (over z_lo).
Axes of the slice: x: 4, y: 4, z: 16 (z_hi: 2, z_lo: 8; z = z_hi * 8 + z_lo), core: 2. Of those that a mesh axis runs over, the one named last changes fastest.
Arguments:
- projected: bfloat16 [4, 4096, 4, 1024], P('dp', ('seq', 'head')), may hold values from -6 to 6
- cotangent: bfloat16 [4, 4096, 1024], P('dp', ('seq', 'head')), may hold values from -6 to 6
- out_weight: bfloat16 [1024, 1024], P('head'), may hold values from -0.1875 to 0.1875
- time_bias: float32 [8, 16], P('head'), may hold values from -1.5 to 1.5
- block_lists: int32 [4, 32, 24], P('dp'), may hold values from -1 to 31, as said below
- stamps: int32 [4, 4096], P('dp'), may hold values from 0 to 6144, as said below
Outputs:
- layer_out: bfloat16 [4, 4096, 1024], P('dp', ('seq', 'head'))
- input_grads: bfloat16 [4, 4096, 4, 1024], P('dp', ('seq', 'head'))
- weight_grad: float32 [1024, 1024], P('head')
- bias_grad: float32 [8, 16], P('head')
Inputs may be any that keep to these rules, and one draw needn't show every extreme that they name: `block_lists`: entry 0 of row r is r itself; the next n - 1 entries are distinct blocks below r; the remaining entries are -1; n runs from 1 to 24, and in every history some row has all 24 entries. `stamps`: never falls along a history and rises by at most 3 from one action to the next; the first action of each history has stamp 0 and the last one the largest stamp.
All inputs are finite; a program needn't handle non-finite values.
Results may differ from a plain program's by a relative error of at most 0.0057.
Values may be sent and summed in bfloat16 or wider, within the bound.
No kernel may reach another device: no remote copies, remote signals or barrier semaphores. Data moves between devices by JAX's collectives and lax.ppermute only.
A program may use at most 64 MiB of HBM per device.

v0:
```python
import jax
import jax.numpy as jnp
from jax import lax
from jax.sharding import PartitionSpec as P

HEADS = 8
HEAD_DIM = 128
D = 1024
BLOCK = 128
BUCKETS = 16


eps = 1e-05


def bucketize(spread, bucket_count):
    spread = jnp.maximum(spread, 0)
    powers = 2 ** jnp.arange(bucket_count - 1, dtype=jnp.int32)
    return jnp.sum((spread[None] >= powers[:, None, None]).astype(jnp.int32), axis=0)


def tile_scores(query_tile, key_tile, query_start, key_start, stamps_row, time_bias, listed):
    score_scale = HEAD_DIM ** (-0.5)
    scores = (
        jnp.einsum("qhd,khd->hqk", query_tile, key_tile, preferred_element_type=jnp.float32)
        * score_scale
    )
    within = jnp.arange(BLOCK, dtype=jnp.int32)
    query_stamps = lax.dynamic_slice_in_dim(stamps_row, query_start, BLOCK)
    key_stamps = lax.dynamic_slice_in_dim(stamps_row, key_start, BLOCK)
    buckets = bucketize(query_stamps[:, None] - key_stamps[None, :], BUCKETS)
    onehot = (buckets[None] == jnp.arange(BUCKETS, dtype=jnp.int32)[:, None, None]).astype(
        jnp.float32
    )
    scores = scores + jnp.einsum("cqk,hc->hqk", onehot, time_bias, precision=lax.Precision.HIGHEST)
    allowed = (key_start + within)[None, :] <= (query_start + within)[:, None]
    counts = (BLOCK * (listed - 1) + within + 1).astype(jnp.float32)
    return (scores, allowed, onehot, counts)


def tile_grads(
    query_tile,
    grad_tile,
    key_tile,
    value_tile,
    query_start,
    key_start,
    stamps_row,
    time_bias,
    listed,
):
    scores, allowed, onehot, counts = tile_scores(
        query_tile, key_tile, query_start, key_start, stamps_row, time_bias, listed
    )
    weights = (jnp.where(allowed[None], jax.nn.silu(scores), 0.0) / counts[None, :, None]).astype(
        jnp.bfloat16
    )
    sigmoid = jax.nn.sigmoid(scores)
    prob_grad = jnp.einsum(
        "qhd,khd->hqk", grad_tile, value_tile, preferred_element_type=jnp.float32
    )
    score_grad = (
        jnp.where(allowed[None], prob_grad * sigmoid * (1.0 + scores * (1.0 - sigmoid)), 0.0)
        / counts[None, :, None]
    )
    bias_part = jnp.einsum("hqk,cqk->hc", score_grad, onehot, precision=lax.Precision.HIGHEST)
    return (weights, score_grad.astype(jnp.bfloat16), bias_part)


def body(projected, cotangent, out_weight, time_bias, block_lists, stamps):
    tokens = projected.shape[1]
    local_heads = time_bias.shape[0]
    head_width = local_heads * HEAD_DIM
    score_scale = HEAD_DIM ** (-0.5)
    arranged = projected[0].reshape(tokens, 4, HEADS, HEAD_DIM)
    by_head = lax.all_to_all(arranged, "head", split_axis=2, concat_axis=0, tiled=True)
    seq_rows = by_head.shape[0]
    local_blocks = seq_rows // BLOCK
    seq_count = lax.axis_size("seq")
    first_own = lax.axis_index("seq") * local_blocks
    list_rows = block_lists[0]
    stamps_row = stamps[0]
    queries = by_head[:, 0]
    key_rows = by_head[:, 1]
    value_rows = by_head[:, 2]
    gate_rows = by_head[:, 3]
    tile_zero = jnp.zeros((BLOCK, local_heads, HEAD_DIM), jnp.float32)
    running = jnp.zeros((seq_rows, local_heads, HEAD_DIM), jnp.float32)
    key_piece = lax.all_gather(key_rows, "seq", axis=0, tiled=True)
    value_piece = lax.all_gather(value_rows, "seq", axis=0, tiled=True)
    piece_blocks = key_piece.shape[0] // BLOCK
    for slot in range(local_blocks):
        query_block = first_own + slot
        entries = list_rows[query_block]
        listed = jnp.sum((entries >= 0).astype(jnp.int32))
        query_tile = queries[slot * BLOCK : (slot + 1) * BLOCK]

        def attend_visit(number, partial_sum):
            target = entries[number]
            piece_slot = target
            active = (target >= 0) & (piece_slot >= 0) & (piece_slot < piece_blocks)

            def attend_compute(current):
                offset = jnp.clip(piece_slot, 0, piece_blocks - 1) * BLOCK
                key_tile = lax.dynamic_slice_in_dim(key_piece, offset, BLOCK, 0)
                value_tile = lax.dynamic_slice_in_dim(value_piece, offset, BLOCK, 0)
                scores, allowed, onehot, counts = tile_scores(
                    query_tile,
                    key_tile,
                    query_block * BLOCK,
                    target * BLOCK,
                    stamps_row,
                    time_bias,
                    listed,
                )
                weights = (
                    jnp.where(allowed[None], jax.nn.silu(scores), 0.0) / counts[None, :, None]
                ).astype(jnp.bfloat16)
                return current + jnp.einsum(
                    "hqk,khd->qhd", weights, value_tile, preferred_element_type=jnp.float32
                )

            return lax.cond(active, attend_compute, lambda current: current, partial_sum)

        block_sum = lax.fori_loop(0, entries.shape[0], attend_visit, tile_zero)
        running = running.at[slot * BLOCK : (slot + 1) * BLOCK].add(block_sum)
    flat = running.reshape(seq_rows, head_width)
    row_stats = lax.psum((jnp.sum(flat, 1), jnp.sum(flat * flat, 1)), "head")
    row_mean = row_stats[0] / D
    inverse = lax.rsqrt(row_stats[1] / D - row_mean * row_mean + eps)
    normed = (flat - row_mean[:, None]) * inverse[:, None]
    gate_flat = gate_rows.reshape(seq_rows, head_width)
    gated = (normed * gate_flat).astype(jnp.bfloat16)
    token_side = lax.all_to_all(
        gated.reshape(seq_rows, local_heads, HEAD_DIM),
        "head",
        split_axis=0,
        concat_axis=1,
        tiled=True,
    ).reshape(tokens, D)
    layer_out = jnp.dot(
        token_side,
        lax.all_gather(out_weight, "head", axis=0, tiled=True),
        preferred_element_type=jnp.float32,
    )
    layer_out = layer_out.astype(jnp.bfloat16).reshape(1, tokens, D)
    grad_rows = lax.all_gather(cotangent[0], "head", axis=0, tiled=True)
    product_rows = lax.dot_general(
        grad_rows, out_weight, (((1,), (1,)), ((), ())), preferred_element_type=jnp.float32
    )
    weight_part = lax.dot_general(
        gated, grad_rows, (((0,), (0,)), ((), ())), preferred_element_type=jnp.float32
    )
    gated_grad, weight_part = (product_rows, weight_part)
    grad_u = (gated_grad * normed).astype(jnp.bfloat16)
    normed_grad = gated_grad * gate_flat
    grad_stats = lax.psum((jnp.sum(normed_grad, 1), jnp.sum(normed_grad * normed, 1)), "head")
    attended_grad = (
        normed_grad - grad_stats[0][:, None] / D - normed * (grad_stats[1][:, None] / D)
    ) * inverse[:, None]
    attended_grad = attended_grad.astype(jnp.bfloat16).reshape(seq_rows, local_heads, HEAD_DIM)
    query_zero = jnp.zeros((seq_rows, local_heads, HEAD_DIM), jnp.float32)
    bias_zero = jnp.zeros((local_heads, BUCKETS), jnp.float32)
    pair_zero = jnp.zeros((seq_rows * seq_count, 2, local_heads, HEAD_DIM), jnp.float32)
    carry = (query_zero, pair_zero, bias_zero)
    query_key_piece = lax.all_gather(key_rows, "seq", axis=0, tiled=True)
    query_value_piece = lax.all_gather(value_rows, "seq", axis=0, tiled=True)
    query_piece_blocks = query_key_piece.shape[0] // BLOCK
    for slot in range(local_blocks):
        query_query_block = first_own + slot
        query_entries = list_rows[query_query_block]
        query_listed = jnp.sum((query_entries >= 0).astype(jnp.int32))
        query_query_tile = queries[slot * BLOCK : (slot + 1) * BLOCK]
        grad_tile = attended_grad[slot * BLOCK : (slot + 1) * BLOCK]

        def query_visit(number, state):
            target = query_entries[number]
            piece_slot = target
            active = (target >= 0) & (piece_slot >= 0) & (piece_slot < query_piece_blocks)

            def query_compute(inner):
                offset = jnp.clip(piece_slot, 0, query_piece_blocks - 1) * BLOCK
                key_tile = lax.dynamic_slice_in_dim(query_key_piece, offset, BLOCK, 0)
                value_tile = lax.dynamic_slice_in_dim(query_value_piece, offset, BLOCK, 0)
                weights, score_grad, bias_part = tile_grads(
                    query_query_tile,
                    grad_tile,
                    key_tile,
                    value_tile,
                    query_query_block * BLOCK,
                    target * BLOCK,
                    stamps_row,
                    time_bias,
                    query_listed,
                )
                block_grad = inner[0] + jnp.einsum(
                    "hqk,khd->qhd", score_grad, key_tile, preferred_element_type=jnp.float32
                )
                bias_acc = inner[-1] + bias_part
                key_part = jnp.einsum(
                    "hqk,qhd->khd", score_grad, query_query_tile, preferred_element_type=jnp.float32
                )
                value_part = jnp.einsum(
                    "hqk,qhd->khd", weights, grad_tile, preferred_element_type=jnp.float32
                )
                rows_at = target * BLOCK
                current = lax.dynamic_slice_in_dim(inner[1], rows_at, BLOCK, 0)
                pair_grad = lax.dynamic_update_slice_in_dim(
                    inner[1], current + jnp.stack([key_part, value_part], 1), rows_at, 0
                )
                return (block_grad, pair_grad, bias_acc)

            return lax.cond(active, query_compute, lambda inner: inner, state)

        block_state = (tile_zero,) + tuple(carry[1:])
        block_state = lax.fori_loop(0, query_entries.shape[0], query_visit, block_state)
        query_grad = carry[0].at[slot * BLOCK : (slot + 1) * BLOCK].add(block_state[0])
        carry = (query_grad,) + tuple(block_state[1:])
    query_grad, pair_grad, bias_grad = carry
    pair_own = lax.psum_scatter(pair_grad, "seq", scatter_dimension=0, tiled=True)
    grads_local = jnp.stack(
        [
            (query_grad * score_scale).astype(jnp.bfloat16),
            (pair_own[:, 0] * score_scale).astype(jnp.bfloat16),
            pair_own[:, 1].astype(jnp.bfloat16),
            grad_u.reshape(seq_rows, local_heads, HEAD_DIM),
        ],
        1,
    )
    returned = lax.all_to_all(grads_local, "head", split_axis=0, concat_axis=2, tiled=True)
    input_grads = returned.reshape(1, tokens, 4, D)
    weight_grad, bias_total = lax.psum((weight_part, bias_grad), ("dp", "seq"))
    return (layer_out, input_grads, weight_grad, bias_total)


def solution(mesh):
    in_specs = (
        P("dp", ("seq", "head"), None, None),
        P("dp", ("seq", "head"), None),
        P("head", None),
        P("head", None),
        P("dp", None, None),
        P("dp", None),
    )
    out_specs = (
        P("dp", ("seq", "head"), None),
        P("dp", ("seq", "head"), None, None),
        P("head", None),
        P("head", None),
    )
    return jax.shard_map(body, mesh=mesh, in_specs=in_specs, out_specs=out_specs, check_vma=False)
```

profile of v0, /device:TPU:1, one launch (start us, length us, event | category | flops | bytes accessed | tf_op | source)
XLA Modules:
  0.0 2402.1 jit_solution(9568202010780728492)
XLA Ops:
  9.2 25.1 %all_to_all.48 = bf16[32,4,8,128]{3,0,1,2:T(8,128)(2,1)S(1)} all-to-all(bf16[32,4,8,128]{3,0,1,2:T(8,128)(2,1)S(1)} %copy.72), channel_id=1, replica_groups=mesh['dp'=4,'seq'=16,'head'=8] {'head'}, dimensions={2} | all-to-all | bytes 524288 | tf_op jit(solution)/shard_map/all_to_all | solution.py:76
  37.5 43.2 %all-gather.2 = bf16[1,256,1024]{2,1,0:T(8,128)(2,1)S(1)} all-gather(bf16[1,32,1024]{2,1,0:T(8,128)(2,1)} %param.31), channel_id=4, replica_groups=mesh['dp'=4,'seq'=16,'head'=8] {'head'}, dimensions={1}, use_global_device_ids=true | all-gather | bytes 589824 | tf_op jit(solution)/shard_map/all_gather | solution.py:147
  80.8 34.6 %all-gather.11.cloned.1.call-done = bf16[4096,1,1,128]{3,0,1,2:T(8,128)(2,1)} async-done(((bf16[256,1,1,128]{3,0,1,2:T(8,128)(2,1)}), bf16[4096,1,1,128]{3,0,1,2:T(8,128)(2,1)}) %all-gather.11.cloned.1.call-update) | async-done | bytes 1048592 | tf_op jit(solution)/shard_map/all_gather | solution.py:89
  115.4 72.7 %all-gather.9.cloned.1.call-done = bf16[4096,1,1,128]{3,0,1,2:T(8,128)(2,1)} async-done(((bf16[256,1,1,128]{3,0,1,2:T(8,128)(2,1)}), bf16[4096,1,1,128]{3,0,1,2:T(8,128)(2,1)}) %all-gather.9.cloned.1.call-update) | async-done | bytes 1048592 | tf_op jit(solution)/shard_map/all_gather | solution.py:90
  188.2 68.4 %while.71 = (s32[]{:T(128)}, f32[128,1,128]{0,2,1:T(8,128)S(1)}, s32[24]{0:T(128)S(1)}, bf16[4096,1,128]{2,0,1:T(8,128)(2,1)}, s32[]{:T(128)}, /*index=5*/bf16[4...) while((s32[]{:T(128)}, f32[128,1,128]{0,2,1:T(8,128)S(1)}, ...), condition=%wide.region_11.12_spmd, body=%wide.region_7.11_spmd.sunk | while | flops 12731436 | bytes 1285764 | solution.py:125
  190.1 5.6 conditional.9
  197.5 5.6 conditional.9
  205.0 5.6 conditional.9
  256.6 62.6 %while.70 = (s32[]{:T(128)}, f32[128,1,128]{0,2,1:T(8,128)S(1)}, s32[24]{0:T(128)S(1)}, bf16[4096,1,128]{2,0,1:T(8,128)(2,1)}, s32[]{:T(128)}, /*index=5*/bf16[4...) while((s32[]{:T(128)}, f32[128,1,128]{0,2,1:T(8,128)S(1)}, ...), condition=%wide.region_5.6_spmd, body=%wide.region_1.5_spmd.sunk | while | flops 12731436 | bytes 1285764 | solution.py:125
  319.3 21.7 all-reduce.2
  341.4 23.2 all-reduce.1
  367.1 75.7 %while.72 = (s32[]{:T(128)}, f32[128,1,128]{0,2,1:T(8,128)S(1)}, f32[4096,2,1,128]{3,0,2,1:T(8,128)}, f32[1,16]{1,0:T(1,128)S(1)}, s32[24]{0:T(128)S(1)}, /*inde...) while((s32[]{:T(128)}, f32[128,1,128]{0,2,1:T(8,128)S(1)}, ...), condition=%wide.region_24.25_spmd, body=%wide.region_20.24_spmd.sunk | while | flops 28738620 | bytes 3187060 | solution.py:216
  369.0 9.8 conditional.10
  380.8 9.9 conditional.10
  392.5 9.8 conditional.10
  442.8 85.8 %while.73 = (s32[]{:T(128)}, f32[128,1,128]{0,2,1:T(8,128)S(1)}, f32[4096,2,1,128]{3,0,2,1:T(8,128)}, f32[1,16]{1,0:T(1,128)S(1)}, s32[24]{0:T(128)S(1)}, /*inde...) while((s32[]{:T(128)}, f32[128,1,128]{0,2,1:T(8,128)S(1)}, ...), condition=%wide.region_29.30_spmd, body=%wide.region_25.29_spmd.sunk | while | flops 28738620 | bytes 3187060 | solution.py:216
  444.7 9.9 conditional.11
  456.6 9.9 conditional.11
  468.3 9.9 conditional.11
  480.2 9.9 conditional.11
  528.6 5.7 copy.79
  540.2 769.2 %reduce-scatter.2.cloned.1.call-done = f32[256,2,1,128]{0,3,2,1:T(8,128)} async-done(((f32[4096,2,1,128]{0,3,2,1:T(8,128)}), f32[256,2,1,128]{0,3,2,1:T(8,128)}) %reduce-scatter.2.cloned.1.call-update) | async-done | bytes 262160 | tf_op jit(solution)/shard_map/reduce_scatter | solution.py:220
  1316.7 280.1 %psum.47 = f32[1,16]{1,0:T(1,128)} all-reduce(f32[1,16]{1,0:T(1,128)S(1)} %get-tuple-element.1001), channel_id=1, replica_groups=mesh['dp'=4,'seq'=16,'head'=8] {'dp','seq'}, use_global_device_ids=true, to_apply=%region_32.33 | all-reduce | flops 16 | bytes 128 | tf_op jit(solution)/shard_map/psum | solution.py:232
  1600.6 792.5 %all-reduce.5.cloned.1.call-done = f32[128,1024]{1,0:T(8,128)} async-done(((f32[128,1024]{1,0:T(8,128)}), f32[128,1024]{1,0:T(8,128)}) %all-reduce.5.cloned.1.call-update) | async-done | bytes 524304 | tf_op jit(solution)/shard_map/psum | solution.py:232
  (433 shorter events, 185.5 us)
Async XLA Ops:
  8.0 107.4 %all-gather.11.cloned.1.call-start = ((), (), s32[]{:S(2)}) async-start(), calls=%async_computation.8 | async-start | bytes 1114112 | tf_op jit(solution)/shard_map/all_gather | solution.py:89
  35.0 153.2 %all-gather.9.cloned.1.call-start = ((), (), s32[]{:S(2)}) async-start(), calls=%async_computation.7 | async-start | bytes 1114112 | tf_op jit(solution)/shard_map/all_gather | solution.py:90
  35.7 1273.7 %reduce-scatter.2.cloned.1.call-start = ((), (), s32[]{:S(2)}) async-start(), calls=%async_computation.5 | async-start | bytes 4456448 | tf_op jit(solution)/shard_map/reduce_scatter | solution.py:220
  256.6 84.4 %copy-start = (bf16[128,1024]{1,0:T(8,128)(2,1)S(1)}, bf16[128,1024]{1,0:T(8,128)(2,1)}, u32[]{:S(2)}) copy-start(bf16[128,1024]{1,0:T(8,128)(2,1)} %param.32) | copy-start | bytes 786436
  319.2 47.9 %copy-start.1 = (f32[1,16]{1,0:T(1,128)S(1)}, f32[1,16]{1,0:T(1,128)}, u32[]{:S(2)}) copy-start(f32[1,16]{1,0:T(1,128)} %get-tuple-element.1853) | copy-start | bytes 196
  534.3 1062.7 %all-gather.7.cloned.1.call-start = ((), (), s32[]{:S(2)}) async-start(), calls=%async_computation.4 | async-start | bytes 2359296 | tf_op jit(solution)/shard_map/all_gather | solution.py:143
  536.8 775.4 %all-to-all-start.1 = ((bf16[8,2,2048]{2,1,0:T(2,128)(2,1)}), bf16[8,2,2048]{2,1,0:T(2,128)(2,1)S(1)}, u32[]{:S(2)}, u32[]{:S(2)}) async-start(bf16[8,2,2048]{2,1,0:T(2,128)(2,1)} %reshape.691), calls=%async_computation.1 | async-start | bytes 131072 | tf_op jit(solution)/shard_map/all_to_all | solution.py:134
  1312.2 287.5 %all-to-all-start.2 = ((bf16[256,4,1,128]{3,1,2,0:T(4,128)(2,1)}), bf16[256,4,1,128]{3,1,2,0:T(4,128)(2,1)S(1)}, u32[]{:S(2)}, u32[]{:S(2)}) async-start(bf16[256,4,1,128]{3,1,2,0:T(4,128)(2,1)} %copy.80), calls=%async_computation.3 | async-start | bytes 524288 | tf_op jit(solution)/shard_map/all_to_all | solution.py:230
  1315.6 1077.4 %all-reduce.5.cloned.1.call-start = ((), (), s32[]{:S(2)}) async-start(), calls=%async_computation.6 | async-start | bytes 1048576 | tf_op jit(solution)/shard_map/psum | solution.py:232
Sparse Core Ops, SparseCore 0:
  35.1 80.2 all-gather.10
  119.3 68.8 all-gather.8
  534.4 774.9 reduce-scatter.1
  1319.9 1073.1 all-reduce.4
Sparse Core Ops, SparseCore 1:
  536.9 728.9 all-gather.6
where the time goes:
time: 2420 us; the launch traced here: 2400 us
  waiting for transfers between devices  1670 us (69%)
  blocking collectives  393 us (16%)
  loops' own time  156 us (6%)
  local copies, waits for them, and re-layouts  90 us (4%)
  matrix products  50.3 us (2%)
    psum x1, waiting for transfers between devices, body(): weight_grad, bias_total = lax.psum((weight_part, bias_grad), ('dp', 'seq'))  792 us
    reduce_scatter x1, waiting for transfers between devices, body(): lax.psum_scatter(pair_grad, 'seq', scatter_dimension=0, tiled=True)  769 us
    psum x1, blocking collectives, body(): weight_grad, bias_total = lax.psum((weight_part, bias_grad), ('dp', 'seq'))  280 us
    all_gather x1, waiting for transfers between devices, body(): value_piece = lax.all_gather(value_rows, 'seq', axis=0, tiled=True)  72.7 us
    another operation x2, loops' own time, body(): block_sum = lax.fori_loop(0, entries.shape[0], attend_visit, tile_zero)  63.6 us
    another operation x2, loops' own time, body(): lax.fori_loop(0, query_entries.shape[0], query_visit, block_state)  63.5 us
  transfers between devices with their start and end apart: 7, of which 4 were waited for; matrix products, arithmetic and copies ran while one was open for 0% of the time, Pallas kernels for 0%

commit v1 on v0

v1 whole, which is shorter than its diff:
```python
import functools

import jax
import jax.numpy as jnp
from jax import lax
from jax.experimental import pallas as pl
from jax.experimental.pallas import tpu as pltpu
from jax.sharding import Mesh, PartitionSpec as P

HEADS = 8
HEAD_DIM = 128
D = 1024
BLOCK = 128
BUCKETS = 16
BLOCKS = 32
LIST_MAX = 24
EPS = 1e-05
SCALE = HEAD_DIM ** (-0.5)

SEQ = ("x", "zh", "core")
ZLINE = ("zh", "head")
TEAM = ("dp", "x", "zh", "core")
VMEM_LIMIT = 48 * 1024 * 1024
f32 = jnp.float32
bf16 = jnp.bfloat16

FWD_GROUP = 4
BWD_GROUP = 2


def nt_dot(a, b):
    return lax.dot_general(a, b, (((1,), (1,)), ((), ())), preferred_element_type=f32)


def nn_dot(a, b):
    return lax.dot_general(a, b, (((1,), (0,)), ((), ())), preferred_element_type=f32)


def half_bias(spread, bias_ref):
    bias = jnp.full((BLOCK, BLOCK), bias_ref[0] * 0.5, f32)
    for e in range(BUCKETS - 1):
        bias = jnp.where(spread >= float(2**e), bias_ref[e + 1] * 0.5, bias)
    return bias


def column_of(row):
    return jnp.transpose(jnp.broadcast_to(row, (BLOCK, BLOCK)))


def slot_setup(slot, blk_ref, n_ref, stamps_ref):
    listed = n_ref[slot]
    block = blk_ref[slot, 0]
    query_stamps = column_of(stamps_ref[pl.ds(block, 1), :].astype(f32))
    within = lax.broadcasted_iota(jnp.int32, (BLOCK, BLOCK), 0)
    counts = (BLOCK * (listed - 1) + within + 1).astype(f32)
    return listed, query_stamps, 1.0 / counts


def causal():
    rows = lax.broadcasted_iota(jnp.int32, (BLOCK, BLOCK), 0)
    cols = lax.broadcasted_iota(jnp.int32, (BLOCK, BLOCK), 1)
    return cols <= rows


def load_pairs(own_ref, other_ref, kv, sems):
    rows = own_ref.shape[0]
    first = pltpu.make_async_copy(own_ref, kv.at[pl.ds(0, rows)], sems.at[0])
    second = pltpu.make_async_copy(other_ref, kv.at[pl.ds(rows, rows)], sems.at[1])
    first.start()
    second.start()
    first.wait()
    second.wait()


def attend_kernel(
    pos_ref, blk_ref, n_ref, bias_ref, stamps_ref, q_ref, own_ref, other_ref, out_ref, kv, sems
):
    load_pairs(own_ref, other_ref, kv, sems)
    for slot in range(2):
        listed, query_stamps, inverse = slot_setup(slot, blk_ref, n_ref, stamps_ref)
        query = q_ref[slot * BLOCK : (slot + 1) * BLOCK, :]

        def tile(entry, share):
            rows = pl.ds(pl.multiple_of(pos_ref[slot, entry] * BLOCK, BLOCK), BLOCK)
            key = kv[rows, 0:HEAD_DIM]
            value = kv[rows, HEAD_DIM : 2 * HEAD_DIM]
            spread = query_stamps - stamps_ref[pl.ds(blk_ref[slot, entry], 1), :].astype(f32)
            half = nt_dot(query, key) * (0.5 * SCALE) + half_bias(spread, bias_ref)
            weights = ((half + half * jnp.tanh(half)) * share).astype(bf16)
            return nn_dot(weights, value)

        total = tile(0, jnp.where(causal(), inverse, 0.0))

        def group(step, acc):
            for j in range(FWD_GROUP):
                entry = 1 + step * FWD_GROUP + j
                valid = (entry < listed).astype(f32)
                acc = acc + tile(jnp.minimum(entry, LIST_MAX - 1), inverse * valid)
            return acc

        steps = (listed - 1 + FWD_GROUP - 1) // FWD_GROUP
        out_ref[slot * BLOCK : (slot + 1) * BLOCK, :] = lax.fori_loop(0, steps, group, total)


def grads_kernel(
    pos_ref,
    blk_ref,
    n_ref,
    bias_ref,
    stamps_ref,
    q_ref,
    g_ref,
    own_ref,
    other_ref,
    dq_ref,
    own_acc_ref,
    other_acc_ref,
    bias_acc_ref,
    kv,
    acc,
    sems,
):
    rows_half = BLOCKS // 2
    acc[...] = jnp.zeros(acc.shape, f32)
    bias_acc_ref[...] = jnp.zeros(bias_acc_ref.shape, f32)
    load_pairs(own_ref, other_ref, kv, sems)
    for slot in range(2):
        listed, query_stamps, inverse = slot_setup(slot, blk_ref, n_ref, stamps_ref)
        query = q_ref[slot * BLOCK : (slot + 1) * BLOCK, :]
        grad = g_ref[slot * BLOCK : (slot + 1) * BLOCK, :]
        query_t = jnp.transpose(query.astype(f32)).astype(bf16)
        grad_t = jnp.transpose(grad.astype(f32)).astype(bf16)

        def fold(values):
            return jnp.sum(values.reshape(BLOCK // 8, 8, BLOCK), axis=0)

        def tile(entry, share):
            at = pos_ref[slot, entry]
            rows = pl.ds(pl.multiple_of(at * BLOCK, BLOCK), BLOCK)
            key = kv[rows, 0:HEAD_DIM]
            value = kv[rows, HEAD_DIM : 2 * HEAD_DIM]
            spread = query_stamps - stamps_ref[pl.ds(blk_ref[slot, entry], 1), :].astype(f32)
            half = nt_dot(query, key) * (0.5 * SCALE) + half_bias(spread, bias_ref)
            prob_grad = nt_dot(grad, value)
            th = jnp.tanh(half)
            up = 1.0 + th
            weights = (half * up * share).astype(bf16)
            slope = up * (1.0 + half * (1.0 - th))
            score_grad = prob_grad * slope * (0.5 * share)
            low = score_grad.astype(bf16)
            acc[at, 0] += nn_dot(query_t, low)
            acc[at, 1] += nn_dot(grad_t, weights)
            bias_parts = [fold(score_grad)]
            for e in range(BUCKETS - 1):
                bias_parts.append(fold(jnp.where(spread >= float(2**e), score_grad, 0.0)))
            return nn_dot(low, key), bias_parts

        def add_bias(parts):
            for c in range(BUCKETS):
                bias_acc_ref[c] += parts[c]

        total, parts = tile(0, jnp.where(causal(), inverse, 0.0))
        add_bias(parts)

        def group(step, acc_q):
            sums = None
            for j in range(BWD_GROUP):
                entry = 1 + step * BWD_GROUP + j
                valid = (entry < listed).astype(f32)
                piece, parts = tile(jnp.minimum(entry, LIST_MAX - 1), inverse * valid)
                acc_q = acc_q + piece
                sums = parts if sums is None else [a + b for a, b in zip(sums, parts)]
            add_bias(sums)
            return acc_q

        steps = (listed - 1 + BWD_GROUP - 1) // BWD_GROUP
        total = lax.fori_loop(0, steps, group, total)
        dq_ref[slot * BLOCK : (slot + 1) * BLOCK, :] = (total * SCALE).astype(bf16)
    own_acc_ref[...] = acc[0:rows_half]
    other_acc_ref[...] = acc[rows_half:].astype(bf16)


SMEM = functools.partial(pl.BlockSpec, memory_space=pltpu.SMEM)
VMEM = functools.partial(pl.BlockSpec, memory_space=pltpu.VMEM)
ANY = functools.partial(pl.BlockSpec, memory_space=pl.ANY)


def attend(pos, blk, listed, bias, stamps, query, own, other):
    return pl.pallas_call(
        attend_kernel,
        out_shape=jax.ShapeDtypeStruct((2 * BLOCK, HEAD_DIM), f32),
        in_specs=[SMEM(), SMEM(), SMEM(), SMEM(), VMEM(), VMEM(), ANY(), ANY()],
        out_specs=VMEM(),
        scratch_shapes=[
            pltpu.VMEM((BLOCKS * BLOCK, 2 * HEAD_DIM), bf16),
            pltpu.SemaphoreType.DMA((2,)),
        ],
        compiler_params=pltpu.CompilerParams(vmem_limit_bytes=VMEM_LIMIT),
        cost_estimate=pl.CostEstimate(
            flops=48 * 4 * BLOCK**3, bytes_accessed=3 << 20, transcendentals=48 * BLOCK**2
        ),
        name="attend",
    )(pos, blk, listed, bias, stamps, query, own, other)


def attend_grads(pos, blk, listed, bias, stamps, query, grad, own, other):
    half = BLOCKS // 2
    return pl.pallas_call(
        grads_kernel,
        out_shape=(
            jax.ShapeDtypeStruct((2 * BLOCK, HEAD_DIM), bf16),
            jax.ShapeDtypeStruct((half, 2, HEAD_DIM, BLOCK), f32),
            jax.ShapeDtypeStruct((half, 2, HEAD_DIM, BLOCK), bf16),
            jax.ShapeDtypeStruct((BUCKETS, 8, BLOCK), f32),
        ),
        in_specs=[SMEM(), SMEM(), SMEM(), SMEM(), VMEM(), VMEM(), VMEM(), ANY(), ANY()],
        out_specs=(VMEM(), VMEM(), VMEM(), VMEM()),
        scratch_shapes=[
            pltpu.VMEM((BLOCKS * BLOCK, 2 * HEAD_DIM), bf16),
            pltpu.VMEM((BLOCKS, 2, HEAD_DIM, BLOCK), f32),
            pltpu.SemaphoreType.DMA((2,)),
        ],
        compiler_params=pltpu.CompilerParams(vmem_limit_bytes=VMEM_LIMIT),
        cost_estimate=pl.CostEstimate(
            flops=48 * 10 * BLOCK**3, bytes_accessed=6 << 20, transcendentals=48 * BLOCK**2
        ),
        name="attend_grads",
    )(pos, blk, listed, bias, stamps, query, grad, own, other)


def exchange(values, axes):
    return lax.all_to_all(values, axes, split_axis=0, concat_axis=0, tiled=True)


def to_all(values, axes, count):
    return exchange(jnp.broadcast_to(values[None], (count,) + values.shape), axes)


def swap_core(values):
    return lax.ppermute(values, "core", [(0, 1), (1, 0)])


def body(projected, cotangent, out_weight, time_bias, block_lists, stamps):
    tokens = projected.shape[1]
    x, zh, core = lax.axis_index("x"), lax.axis_index("zh"), lax.axis_index("core")
    run = (x * 2 + zh) * 2 + core

    all_weight = lax.all_gather(out_weight, "head", axis=0, tiled=True)

    by_head = projected[0].reshape(tokens, 4, HEADS, HEAD_DIM).transpose(2, 0, 1, 3)
    by_head = by_head.reshape(HEADS, tokens, 4 * HEAD_DIM)
    got = exchange(jnp.concatenate([by_head, by_head], 0), ZLINE)
    pairs = got[:, :, HEAD_DIM : 3 * HEAD_DIM].reshape(4 * BLOCK, 2 * HEAD_DIM)
    own_run = lax.dynamic_slice_in_dim(got, zh * HEADS, HEADS, 0).reshape(2 * BLOCK, 4 * HEAD_DIM)
    query = own_run[:, :HEAD_DIM]
    gate = own_run[:, 3 * HEAD_DIM :].astype(f32)
    own_pairs = to_all(pairs, "x", 4).reshape(16 * BLOCK, 2 * HEAD_DIM)
    other_pairs = swap_core(own_pairs)

    lists = lax.dynamic_slice_in_dim(block_lists[0], run * 2, 2, 0)
    listed = jnp.sum((lists >= 0).astype(jnp.int32), 1)
    blk = jnp.maximum(lists, 0)
    side = ((blk // 2) % 2) ^ core
    pos = ((side * 4 + blk // 8) * 2 + (blk // 4) % 2) * 2 + blk % 2
    bias = time_bias[0]
    stamp_blocks = stamps[0].reshape(BLOCKS, BLOCK)

    attended = attend(pos, blk, listed, bias, stamp_blocks, query, own_pairs, other_pairs)

    cot = to_all(cotangent[0], "head", HEADS).reshape(2 * BLOCK, D)
    gated_grad = nt_dot(cot, out_weight)
    normed_grad = gated_grad * gate
    sums = jnp.stack(
        [
            jnp.sum(attended, 1),
            jnp.sum(attended * attended, 1),
            jnp.sum(normed_grad, 1),
            jnp.sum(normed_grad * attended, 1),
        ]
    )
    sums = jnp.sum(to_all(sums, "head", HEADS).reshape(HEADS, 4, 2 * BLOCK), 0) / D
    mean = sums[0]
    inverse = lax.rsqrt(sums[1] - mean * mean + EPS)
    first = sums[2]
    second = inverse * (sums[3] - mean * sums[2])
    normed = (attended - mean[:, None]) * inverse[:, None]
    gated = (normed * gate).astype(bf16)
    grad_u = (gated_grad * normed).astype(bf16)
    attended_grad = (
        (normed_grad - first[:, None] - normed * second[:, None]) * inverse[:, None]
    ).astype(bf16)

    weight_part = lax.dot_general(gated, cot, (((0,), (0,)), ((), ())), preferred_element_type=f32)
    weight_rows = exchange(weight_part.astype(bf16).reshape(64, 2, D), TEAM)
    weight_rows = jnp.sum(weight_rows.astype(f32), 0)
    weight_grad = to_all(weight_rows, TEAM, 64).reshape(HEAD_DIM, D)

    grad_q, own_grads, other_grads, bias_sums = attend_grads(
        pos, blk, listed, bias, stamp_blocks, query, attended_grad, own_pairs, other_pairs
    )
    reach = jnp.sum(bias_sums, (1, 2))
    bias_part = reach - jnp.concatenate([reach[1:], jnp.zeros((1,), f32)])
    bias_grad = jnp.sum(to_all(bias_part, TEAM, 64).reshape(64, 1, BUCKETS), 0)

    chip = (own_grads + swap_core(other_grads).astype(f32)).astype(bf16)
    line = exchange(chip.reshape(4, 4, 2, HEAD_DIM, BLOCK), "x")
    line = jnp.sum(line.reshape(4, 4, 2, HEAD_DIM, BLOCK).astype(f32), 0).astype(bf16)
    line = line.transpose(0, 3, 1, 2).reshape(16, tokens, 2 * HEAD_DIM)
    rows = jnp.concatenate([grad_q, grad_u, gated], 1).reshape(HEADS, tokens, 3 * HEAD_DIM)
    back = jnp.concatenate([line, jnp.concatenate([rows, rows], 0)], 2)
    back = exchange(back, ZLINE)
    pair_grads = back[:HEADS, :, : 2 * HEAD_DIM].astype(f32) + back[HEADS:, :, : 2 * HEAD_DIM]
    rows = lax.dynamic_slice_in_dim(back, zh * HEADS, HEADS, 0)[:, :, 2 * HEAD_DIM :]
    grad_k = (pair_grads[:, :, :HEAD_DIM] * SCALE).astype(bf16)
    grad_v = pair_grads[:, :, HEAD_DIM:].astype(bf16)
    grads = jnp.stack(
        [rows[:, :, :HEAD_DIM], grad_k, grad_v, rows[:, :, HEAD_DIM : 2 * HEAD_DIM]], 0
    )
    input_grads = grads.transpose(2, 0, 1, 3).reshape(1, tokens, 4, D)
    token_side = rows[:, :, 2 * HEAD_DIM :].transpose(1, 0, 2).reshape(tokens, D)
    layer_out = nn_dot(token_side, all_weight).astype(bf16).reshape(1, tokens, D)
    return (layer_out, input_grads, weight_grad, bias_grad)


def solution(mesh):
    fine = Mesh(
        mesh.devices.reshape(4, 4, 2, 2, 8), ("dp", "x", "zh", "core", "head")
    )
    run = SEQ + ("head",)
    in_specs = (
        P("dp", run, None, None),
        P("dp", run, None),
        P("head", None),
        P("head", None),
        P("dp", None, None),
        P("dp", None),
    )
    out_specs = (
        P("dp", run, None),
        P("dp", run, None, None),
        P("head", None),
        P("head", None),
    )
    return jax.shard_map(body, mesh=fine, in_specs=in_specs, out_specs=out_specs, check_vma=False)
```

time: 2420 us -> 339 us (0.14)
  waiting for transfers between devices: 1670 us -> 144 us
  blocking collectives: 393 us -> 72.7 us
  loops' own time: 156 us -> 0 us
  local copies, waits for them, and re-layouts: 90 us -> 9.54 us
  starting transfers between devices: 6.97 us -> 77.5 us
  matrix products: 50.3 us -> 5.56 us
    psum x1 -> x0, waiting for transfers between devices: 792 us -> none  [body(): weight_grad, bias_total = lax.psum((weight_part, bias_grad), ('dp', 'seq'))]
    reduce_scatter x1 -> x0, waiting for transfers between devices: 769 us -> none  [body(): lax.psum_scatter(pair_grad, 'seq', scatter_dimension=0, tiled=True)]
    psum x3 -> x0, blocking collectives: 325 us -> none  [the longest x1 280 us: body(): weight_grad, bias_total = lax.psum((weight_part, bias_grad), ('dp', 'seq'))]
    another operation x100 -> x0, loops' own time: 156 us -> none  [the longest x2 63.6 us: body(): block_sum = lax.fori_loop(0, entries.shape[0], attend_visit, tile_zero)]
    all_to_all x2 -> x6, waiting for transfers between devices: 0.01 us -> 122 us  [exchange(): return lax.all_to_all(values, axes, split_axis=0, concat_axis=0, tiled=True)]
    all_gather x3 -> x1, waiting for transfers between devices: 107 us -> 18.9 us  [body(): all_weight = lax.all_gather(out_weight, 'head', axis=0, tiled=True)]
    dynamic_slice x111 -> x2, local copies, waits for them, and re-layouts: 69 us -> 0.1 us  [the longest x1 0.07 us: body(): lists = lax.dynamic_slice_in_dim(block_lists[0], run * 2, 2, 0)]
    all_to_all x2 -> x6, starting transfers between devices: 6.77 us -> 69.9 us  [exchange(): return lax.all_to_all(values, axes, split_axis=0, concat_axis=0, tiled=True)]
  transfers between devices with their start and end apart: 7 -> 9, of which waited for: 4 -> 8; matrix products, arithmetic and copies ran while one was open for 0% -> 3% of each run, Pallas kernels for 0% -> 1%
where the time goes in v1:
time: 339 us; the launch traced here: 337 us
  waiting for transfers between devices  144 us (42%)
  starting transfers between devices  77.5 us (23%)
  blocking collectives  72.7 us (21%)
  between operations  14.4 us (4%)
  local copies, waits for them, and re-layouts  9.54 us (3%)
  Pallas kernels  6.96 us (2%)
  other arithmetic  6.31 us (2%)
  matrix products  5.56 us (2%)
    all_to_all x6, waiting for transfers between devices, exchange(): return lax.all_to_all(values, axes, split_axis=0, concat_axis=0, tiled=True)  122 us
    all_to_all x3, blocking collectives, exchange(): return lax.all_to_all(values, axes, split_axis=0, concat_axis=0, tiled=True)  72.7 us
    all_to_all x6, starting transfers between devices, exchange(): return lax.all_to_all(values, axes, split_axis=0, concat_axis=0, tiled=True)  69.9 us
    all_gather x1, waiting for transfers between devices, body(): all_weight = lax.all_gather(out_weight, 'head', axis=0, tiled=True)  18.9 us
    ppermute x2, starting transfers between devices, swap_core(): return lax.ppermute(values, 'core', [(0, 1), (1, 0)])  7.57 us
  transfers between devices with their start and end apart: 9, of which 8 were waited for; matrix products, arithmetic and copies ran while one was open for 3% of the time, Pallas kernels for 1%

profile of v1, /device:TPU:1, one launch (start us, length us, event | category | flops | bytes accessed | tf_op | source)
XLA Modules:
  0.0 336.7 jit_solution(7972545195416684319)
XLA Ops:
  8.5 38.4 %all_to_all.46 = bf16[16,32,512]{2,1,0:T(8,128)(2,1)S(1)} all-to-all(bf16[16,32,512]{2,1,0:T(8,128)(2,1)S(1)} %pad_maximum_fusion), channel_id=1, replica_groups=mesh['dp'=4,'x'=4,'zh'=2,'core'=2,'head'=8] {'zh','head'}, dimensions={0} | all-to-all | bytes 1048576 | tf_op jit(solution)/shard_map/all_to_all | solution.py:232
  47.0 13.6 %all_to_all.47 = bf16[4,512,256]{2,1,0:T(8,128)(2,1)S(1)} all-to-all(bf16[4,512,256]{2,1,0:T(8,128)(2,1)S(1)} %broadcast_in_dim.17), channel_id=1, replica_groups=mesh['dp'=4,'x'=4,'zh'=2,'core'=2,'head'=8] {'x'}, dimensions={0} | all-to-all | bytes 2097152 | tf_op jit(solution)/shard_map/all_to_all | solution.py:232
  61.4 16.4 %all-to-all-start.1 = ((bf16[8,32,1024]{2,1,0:T(8,128)(2,1)}), bf16[8,32,1024]{2,1,0:T(8,128)(2,1)S(1)}, u32[]{:S(2)}, u32[]{:S(2)}) async-start(bf16[8,32,1024]{2,1,0:T(8,128)(2,1)} %broadcast_in_dim.15), calls=%async_computation.1 | async-start | bytes 1048576 | tf_op jit(solution)/shard_map/all_to_all | solution.py:232
  77.9 4.3 %collective-permute-start = (bf16[2048,256]{1,0:T(8,128)(2,1)S(1)}, bf16[2048,256]{1,0:T(8,128)(2,1)S(1)}, u32[]{:S(2)}, u32[]{:S(2)}) collective-permute-start(bf16[2048,256]{1,0:T(8,128)(2,1)S(1)} %bitcast.49), channel_id=1, source_target_pairs={{0,8},{8,0},{1,9},{9,1},{2,10},{10,2},{3,11},{11,3},{4,12},{12,4},... | collective-permute-start | bytes 3145736 | tf_op jit(solution)/shard_map/ppermute | solution.py:240
  82.5 1.9 collective-permute-done.other_ref
  84.4 2.6 attend.1
  87.0 11.6 %all-to-all-done.1 = bf16[8,32,1024]{2,1,0:T(8,128)(2,1)S(1)} async-done(((bf16[8,32,1024]{2,1,0:T(8,128)(2,1)}), bf16[8,32,1024]{2,1,0:T(8,128)(2,1)S(1)}, u32[]{:S(2)}, u32[]{:S(2)}) %all-to-all-start.1) | async-done | bytes 524320 | tf_op jit(solution)/shard_map/all_to_all | solution.py:232
  98.6 1.6 fusion.7
  100.2 20.8 %all_to_all.48 = f32[8,4,256]{2,1,0:T(4,128)S(1)} all-to-all(f32[8,4,256]{2,1,0:T(4,128)S(1)} %broadcast_in_dim.18), channel_id=1, replica_groups=mesh['dp'=4,'x'=4,'zh'=2,'core'=2,'head'=8] {'head'}, dimensions={0} | all-to-all | bytes 65536 | tf_op jit(solution)/shard_map/all_to_all | solution.py:232
  122.5 4.4 %attend_grads.1 = (bf16[256,128]{1,0:T(8,128)(2,1)S(1)}, f32[16,2,128,128]{3,2,1,0:T(8,128)S(1)}, bf16[16,2,128,128]{3,2,1,0:T(8,128)(2,1)S(1)}, f32[16,8,128]{2,1,0:T(8,128)S(1)}) custom-call(s32[2,24]{1,0:T(2,128)S(1)} %fusion.12.pos_ref, s32[2,24]{1,0:T(2,128)S(1)} %get-tuple-element.45.blk_ref, s32[2]{0:T(128)S(1)} %get-tuple-element.44.n_ref, ...), custom_call_target="tpu_custom_call" | custom-call | flops 1006632960 | bytes 6291456 | tf_op jit(solution)/shard_map/attend_grads/pallas_call | solution.py:208
  128.2 3.3 collective-permute-start.1
  132.2 25.2 %all-to-all-start.8 = ((f32[64,1,16]{2,1,0:T(1,128)}), f32[64,1,16]{2,1,0:T(1,128)S(1)}, u32[]{:S(2)}, u32[]{:S(2)}) async-start(f32[64,1,16]{2,1,0:T(1,128)} %broadcast_in_dim.20), calls=%async_computation.8 | async-start | bytes 65536 | tf_op jit(solution)/shard_map/all_to_all | solution.py:232
  159.5 14.3 %all-to-all-done.8 = f32[64,1,16]{2,1,0:T(1,128)S(1)} async-done(((f32[64,1,16]{2,1,0:T(1,128)}), f32[64,1,16]{2,1,0:T(1,128)S(1)}, u32[]{:S(2)}, u32[]{:S(2)}) %all-to-all-start.8) | async-done | bytes 4128 | tf_op jit(solution)/shard_map/all_to_all | solution.py:232
  173.7 5.6 %all-to-all-start.6 = ((bf16[64,2,1024]{2,1,0:T(2,128)(2,1)}), bf16[64,2,1024]{2,1,0:T(2,128)(2,1)}, u32[]{:S(2)}, u32[]{:S(2)}) async-start(bf16[64,2,1024]{2,1,0:T(2,128)(2,1)} %reshape.121), calls=%async_computation.6 | async-start | bytes 524288 | tf_op jit(solution)/shard_map/all_to_all | solution.py:232
  179.4 2.6 add_convert_fusion
  181.9 16.3 %all-to-all-done.6 = bf16[64,2,1024]{2,1,0:T(2,128)(2,1)} async-done(((bf16[64,2,1024]{2,1,0:T(2,128)(2,1)}), bf16[64,2,1024]{2,1,0:T(2,128)(2,1)}, u32[]{:S(2)}, u32[]{:S(2)}) %all-to-all-start.6) | async-done | bytes 262176 | tf_op jit(solution)/shard_map/all_to_all | solution.py:232
  198.2 3.5 %all-to-all-start.4 = ((bf16[4,4,2,128,128]{4,3,2,1,0:T(8,128)(2,1)}), bf16[4,4,2,128,128]{4,3,2,1,0:T(8,128)(2,1)S(1)}, u32[]{:S(2)}, u32[]{:S(2)}) async-start(bf16[4,4,2,128,128]{4,3,2,1,0:T(8,128)(2,1)} %bitcast.58), calls=%async_computation.4 | async-start | bytes 2097152 | tf_op jit(solution)/shard_map/all_to_all | solution.py:232
  202.9 13.4 %all-to-all-done.4 = bf16[4,4,2,128,128]{4,3,2,1,0:T(8,128)(2,1)S(1)} async-done(((bf16[4,4,2,128,128]{4,3,2,1,0:T(8,128)(2,1)}), bf16[4,4,2,128,128]{4,3,2,1,0:T(8,128)(2,1)S(1)}, u32[]{:S(2)}, u32[]{:S(2)}) %all-to-all-start.4) | async-done | bytes 1048608 | tf_op jit(solution)/shard_map/all_to_all | solution.py:232
  217.2 5.5 %all-to-all-start.7 = ((f32[64,2,1024]{2,1,0:T(2,128)}), f32[64,2,1024]{2,1,0:T(2,128)S(1)}, u32[]{:S(2)}, u32[]{:S(2)}) async-start(f32[64,2,1024]{2,1,0:T(2,128)} %broadcast_in_dim.19), calls=%async_computation.7 | async-start | bytes 1048576 | tf_op jit(solution)/shard_map/all_to_all | solution.py:232
  225.0 24.7 %all-to-all-done.7 = f32[64,2,1024]{2,1,0:T(2,128)S(1)} async-done(((f32[64,2,1024]{2,1,0:T(2,128)}), f32[64,2,1024]{2,1,0:T(2,128)S(1)}, u32[]{:S(2)}, u32[]{:S(2)}) %all-to-all-start.7) | async-done | bytes 524320 | tf_op jit(solution)/shard_map/all_to_all | solution.py:232
  249.7 13.7 %all-to-all-start.5 = ((bf16[16,32,640]{2,1,0:T(8,128)(2,1)}), bf16[16,32,640]{2,1,0:T(8,128)(2,1)S(1)}, u32[]{:S(2)}, u32[]{:S(2)}) async-start(bf16[16,32,640]{2,1,0:T(8,128)(2,1)} %maximum_maximum_fusion), calls=%async_computation.5 | async-start | bytes 1310720 | tf_op jit(solution)/shard_map/all_to_all | solution.py:232
  265.2 42.0 %all-to-all-done.5 = bf16[16,32,640]{2,1,0:T(8,128)(2,1)S(1)} async-done(((bf16[16,32,640]{2,1,0:T(8,128)(2,1)}), bf16[16,32,640]{2,1,0:T(8,128)(2,1)S(1)}, u32[]{:S(2)}, u32[]{:S(2)}) %all-to-all-start.5) | async-done | bytes 655392 | tf_op jit(solution)/shard_map/all_to_all | solution.py:232
  308.2 18.9 %all-gather.2.cloned.1.call-done = bf16[1024,1024]{1,0:T(8,128)(2,1)} async-done(((bf16[128,1024]{1,0:T(8,128)(2,1)}), bf16[1024,1024]{1,0:T(8,128)(2,1)}) %all-gather.2.cloned.1.call-update) | async-done | bytes 2097168 | tf_op jit(solution)/shard_map/all_gather | solution.py:248
  327.1 2.7 fusion
  (65 shorter events, 15.3 us)
Async XLA Ops:
  7.2 75.0 %copy-start = (s32[1,32,24]{1,2,0:T(8,128)S(1)}, s32[1,32,24]{1,2,0:T(8,128)}, u32[]{:S(2)}) copy-start(s32[1,32,24]{1,2,0:T(8,128)} %param.10) | copy-start | bytes 9220
  46.9 13.7 %copy-start.9 = (bf16[1,32,1024]{2,1,0:T(8,128)(2,1)S(1)}, bf16[1,32,1024]{2,1,0:T(8,128)(2,1)}, u32[]{:S(2)}) copy-start(bf16[1,32,1024]{2,1,0:T(8,128)(2,1)} %param.7) | copy-start | bytes 196612
  47.0 37.4 %copy-start.3 = (s32[1,4096]{1,0:T(1,128)S(1)}, s32[1,4096]{1,0:T(1,128)}, u32[]{:S(2)}) copy-start(s32[1,4096]{1,0:T(1,128)} %param.11) | copy-start | bytes 49156
  47.0 37.4 %copy-start.4 = (f32[1,16]{1,0:T(1,128)S(1)}, f32[1,16]{1,0:T(1,128)}, u32[]{:S(2)}) copy-start(f32[1,16]{1,0:T(1,128)} %param.9) | copy-start | bytes 196
  61.4 37.1 %all-to-all-start.1 = ((bf16[8,32,1024]{2,1,0:T(8,128)(2,1)}), bf16[8,32,1024]{2,1,0:T(8,128)(2,1)S(1)}, u32[]{:S(2)}, u32[]{:S(2)}) async-start(bf16[8,32,1024]{2,1,0:T(8,128)(2,1)} %broadcast_in_dim.15), calls=%async_computation.1 | async-start | bytes 1048576 | tf_op jit(solution)/shard_map/all_to_all | solution.py:232
  77.9 6.5 %collective-permute-start = (bf16[2048,256]{1,0:T(8,128)(2,1)S(1)}, bf16[2048,256]{1,0:T(8,128)(2,1)S(1)}, u32[]{:S(2)}, u32[]{:S(2)}) collective-permute-start(bf16[2048,256]{1,0:T(8,128)(2,1)S(1)} %bitcast.49), channel_id=1, source_target_pairs={{0,8},{8,0},{1,9},{9,1},{2,10},{10,2},{3,11},{11,3},{4,12},{12,4},... | collective-permute-start | bytes 3145736 | tf_op jit(solution)/shard_map/ppermute | solution.py:240
  82.5 1.9 copy-start.7
  84.4 36.8 %copy-start.1 = (bf16[2048,256]{1,0:T(8,128)(2,1)}, bf16[2048,256]{1,0:T(8,128)(2,1)S(1)}, u32[]{:S(2)}) copy-start(bf16[2048,256]{1,0:T(8,128)(2,1)S(1)} %collective-permute-done.other_ref) | copy-start | bytes 3145732
  84.4 14.1 %copy-start.8 = (bf16[8,32,512]{2,1,0:T(8,128)(2,1)S(1)}, bf16[8,32,512]{2,1,0:T(8,128)(2,1)}, u32[]{:S(2)}) copy-start(bf16[8,32,512]{2,1,0:T(8,128)(2,1)} %copy-done.7) | copy-start | bytes 786436
  98.6 22.7 %copy-start.6 = (bf16[8,32,1024]{2,1,0:T(8,128)(2,1)}, bf16[8,32,1024]{2,1,0:T(8,128)(2,1)S(1)}, u32[]{:S(2)}) copy-start(bf16[8,32,1024]{2,1,0:T(8,128)(2,1)S(1)} %all-to-all-done.1) | copy-start | bytes 1572868
  121.3 1.2 copy-start.2
  126.9 1.0 copy-start.5
  128.2 51.2 %collective-permute-start.1 = (bf16[16,2,128,128]{3,2,1,0:T(8,128)(2,1)}, bf16[16,2,128,128]{3,2,1,0:T(8,128)(2,1)}, u32[]{:S(2)}, u32[]{:S(2)}) collective-permute-start(bf16[16,2,128,128]{3,2,1,0:T(8,128)(2,1)} %copy-done.5), channel_id=1, source_target_pairs={{0,8},{8,0},{1,9},{9,1},{2,10},{10,2},{3,11},{11,3},{4,12},{12,4},... | collective-permute-start | bytes 3145736 | tf_op jit(solution)/shard_map/ppermute | solution.py:240
  132.2 41.5 %all-to-all-start.8 = ((f32[64,1,16]{2,1,0:T(1,128)}), f32[64,1,16]{2,1,0:T(1,128)S(1)}, u32[]{:S(2)}, u32[]{:S(2)}) async-start(f32[64,1,16]{2,1,0:T(1,128)} %broadcast_in_dim.20), calls=%async_computation.8 | async-start | bytes 65536 | tf_op jit(solution)/shard_map/all_to_all | solution.py:232
  173.7 24.4 %all-to-all-start.6 = ((bf16[64,2,1024]{2,1,0:T(2,128)(2,1)}), bf16[64,2,1024]{2,1,0:T(2,128)(2,1)}, u32[]{:S(2)}, u32[]{:S(2)}) async-start(bf16[64,2,1024]{2,1,0:T(2,128)(2,1)} %reshape.121), calls=%async_computation.6 | async-start | bytes 524288 | tf_op jit(solution)/shard_map/all_to_all | solution.py:232
  198.2 18.1 %all-to-all-start.4 = ((bf16[4,4,2,128,128]{4,3,2,1,0:T(8,128)(2,1)}), bf16[4,4,2,128,128]{4,3,2,1,0:T(8,128)(2,1)S(1)}, u32[]{:S(2)}, u32[]{:S(2)}) async-start(bf16[4,4,2,128,128]{4,3,2,1,0:T(8,128)(2,1)} %bitcast.58), calls=%async_computation.4 | async-start | bytes 2097152 | tf_op jit(solution)/shard_map/all_to_all | solution.py:232
  217.2 32.4 %all-to-all-start.7 = ((f32[64,2,1024]{2,1,0:T(2,128)}), f32[64,2,1024]{2,1,0:T(2,128)S(1)}, u32[]{:S(2)}, u32[]{:S(2)}) async-start(f32[64,2,1024]{2,1,0:T(2,128)} %broadcast_in_dim.19), calls=%async_computation.7 | async-start | bytes 1048576 | tf_op jit(solution)/shard_map/all_to_all | solution.py:232
  222.7 104.4 %all-gather.2.cloned.1.call-start = ((), (), s32[]{:S(2)}) async-start(), calls=%async_computation.9 | async-start | bytes 2359296 | tf_op jit(solution)/shard_map/all_gather | solution.py:248
  249.7 57.5 %all-to-all-start.5 = ((bf16[16,32,640]{2,1,0:T(8,128)(2,1)}), bf16[16,32,640]{2,1,0:T(8,128)(2,1)S(1)}, u32[]{:S(2)}, u32[]{:S(2)}) async-start(bf16[16,32,640]{2,1,0:T(8,128)(2,1)} %maximum_maximum_fusion), calls=%async_computation.5 | async-start | bytes 1310720 | tf_op jit(solution)/shard_map/all_to_all | solution.py:232
Sparse Core Ops, SparseCore 0:
  225.7 101.4 all-gather.1

commit v2 on v1

v2 whole, which is shorter than its diff:
```python
import functools

import jax
import jax.numpy as jnp
from jax import lax
from jax.experimental import pallas as pl
from jax.experimental.pallas import tpu as pltpu
from jax.sharding import Mesh, PartitionSpec as P

HEADS = 8
HEAD_DIM = 128
D = 1024
BLOCK = 128
BUCKETS = 16
BLOCKS = 32
LIST_MAX = 24
EPS = 1e-05
SCALE = HEAD_DIM ** (-0.5)

SEQ = ("x", "zh", "core")
ZLINE = ("zh", "head")
VMEM_LIMIT = 48 * 1024 * 1024
f32 = jnp.float32
bf16 = jnp.bfloat16

FWD_GROUP = 4
BWD_GROUP = 4
NARROW = 2
PARTS = 2
TILES = 8
SHIFTS = (1, 3, 2)


def nt_dot(a, b):
    return lax.dot_general(a, b, (((1,), (1,)), ((), ())), preferred_element_type=f32)


def nn_dot(a, b):
    return lax.dot_general(a, b, (((1,), (0,)), ((), ())), preferred_element_type=f32)


def slot_setup(slot, blk_ref, n_ref, stamps_ref):
    listed = n_ref[slot]
    block = blk_ref[slot, 0]
    row = jnp.broadcast_to(stamps_ref[pl.ds(block, 1), :].astype(f32), (BLOCK, BLOCK))
    query_stamps = jnp.transpose(row)
    within = lax.broadcasted_iota(jnp.int32, (BLOCK, BLOCK), 0)
    counts = (BLOCK * (listed - 1) + within + 1).astype(f32)
    return listed, query_stamps, 1.0 / counts


def causal():
    rows = lax.broadcasted_iota(jnp.int32, (BLOCK, BLOCK), 0)
    cols = lax.broadcasted_iota(jnp.int32, (BLOCK, BLOCK), 1)
    return cols <= rows


def steps_of(low, narrow):
    if not narrow:
        return list(range(1, BUCKETS))
    return [jnp.minimum(low + k, BUCKETS) for k in range(1, NARROW + 1)]


def half_bias(spread, low, narrow, bias_ref, power_ref):
    first = low if narrow else 0
    bias = jnp.full((BLOCK, BLOCK), bias_ref[first] * 0.5, f32)
    for c in steps_of(low, narrow):
        bias = jnp.where(spread >= power_ref[c], bias_ref[c] * 0.5, bias)
    return bias


def all_narrow(width_ref, slot, entries):
    widest = width_ref[slot, entries[0]]
    for entry in entries[1:]:
        widest = jnp.maximum(widest, width_ref[slot, entry])
    return widest <= NARROW


def load_pairs(parts, kv, sems):
    copies = []
    for k, part in enumerate(parts):
        rows = part.shape[0]
        copies.append(pltpu.make_async_copy(part, kv.at[pl.ds(k * rows, rows)], sems.at[k]))
    for copy in copies:
        copy.start()
    for copy in copies:
        copy.wait()


def attend_kernel(
    pos_ref, home_ref, blk_ref, low_ref, width_ref, n_ref, bias_ref, power_ref, stamps_ref, q_ref, *refs
):
    parts, (out_ref, kv, sems) = refs[:PARTS], refs[PARTS:]
    load_pairs(parts, kv, sems)
    for slot in range(2):
        listed, query_stamps, inverse = slot_setup(slot, blk_ref, n_ref, stamps_ref)
        query = q_ref[slot * BLOCK : (slot + 1) * BLOCK, :]

        def tile(entry, share, narrow):
            rows = pl.ds(pl.multiple_of(pos_ref[slot, entry] * BLOCK, BLOCK), BLOCK)
            key = kv[rows, 0:HEAD_DIM]
            value = kv[rows, HEAD_DIM : 2 * HEAD_DIM]
            spread = query_stamps - stamps_ref[pl.ds(blk_ref[slot, entry], 1), :].astype(f32)
            bias = half_bias(spread, low_ref[slot, entry], narrow, bias_ref, power_ref)
            half = nt_dot(query, key) * (0.5 * SCALE) + bias
            weights = ((half + half * jnp.tanh(half)) * share).astype(bf16)
            return nn_dot(weights, value)

        def run(step, acc, narrow):
            for j in range(FWD_GROUP):
                entry = 1 + step * FWD_GROUP + j
                valid = (entry < listed).astype(f32)
                acc = acc + tile(jnp.minimum(entry, LIST_MAX - 1), inverse * valid, narrow)
            return acc

        def group(step, acc):
            entries = [jnp.minimum(1 + step * FWD_GROUP + j, LIST_MAX - 1) for j in range(FWD_GROUP)]
            return lax.cond(
                all_narrow(width_ref, slot, entries),
                lambda value: run(step, value, True),
                lambda value: run(step, value, False),
                acc,
            )

        total = tile(0, jnp.where(causal(), inverse, 0.0), False)
        steps = (listed - 1 + FWD_GROUP - 1) // FWD_GROUP
        out_ref[slot * BLOCK : (slot + 1) * BLOCK, :] = lax.fori_loop(0, steps, group, total)


def grads_kernel(
    pos_ref, home_ref, blk_ref, low_ref, width_ref, n_ref, bias_ref, power_ref, stamps_ref, q_ref, g_ref, *refs
):
    parts = refs[:PARTS]
    own_ref, other_ref, dq_ref, bins_ref, kv, acc, sems = refs[PARTS:]
    acc[...] = jnp.zeros(acc.shape, f32)
    bins_ref[...] = jnp.zeros(bins_ref.shape, f32)
    load_pairs(parts, kv, sems)
    for slot in range(2):
        listed, query_stamps, inverse = slot_setup(slot, blk_ref, n_ref, stamps_ref)
        query = q_ref[slot * BLOCK : (slot + 1) * BLOCK, :]
        grad = g_ref[slot * BLOCK : (slot + 1) * BLOCK, :]
        query_t = jnp.transpose(query.astype(f32)).astype(bf16)
        grad_t = jnp.transpose(grad.astype(f32)).astype(bf16)

        def fold(values):
            return jnp.sum(values.reshape(BLOCK // 8, 8, BLOCK), axis=0)

        def tile(entry, share, narrow):
            at = home_ref[slot, entry]
            low = low_ref[slot, entry]
            rows = pl.ds(pl.multiple_of(pos_ref[slot, entry] * BLOCK, BLOCK), BLOCK)
            key = kv[rows, 0:HEAD_DIM]
            value = kv[rows, HEAD_DIM : 2 * HEAD_DIM]
            spread = query_stamps - stamps_ref[pl.ds(blk_ref[slot, entry], 1), :].astype(f32)
            bias = half_bias(spread, low, narrow, bias_ref, power_ref)
            half = nt_dot(query, key) * (0.5 * SCALE) + bias
            prob_grad = nt_dot(grad, value)
            th = jnp.tanh(half)
            up = 1.0 + th
            weights = (half * up * share).astype(bf16)
            score_grad = prob_grad * (up * (1.0 + half * (1.0 - th))) * (0.5 * share)
            rounded = score_grad.astype(bf16)
            acc[at, 0] += nn_dot(query_t, rounded)
            acc[at, 1] += nn_dot(grad_t, weights)
            above = fold(score_grad)
            before = low if narrow else 0
            for c in steps_of(low, narrow):
                reach = fold(jnp.where(spread >= power_ref[c], score_grad, 0.0))
                bins_ref[before] += above - reach
                above, before = reach, c
            bins_ref[before] += above
            return nn_dot(rounded, key)

        def run(step, acc_q, narrow):
            for j in range(BWD_GROUP):
                entry = 1 + step * BWD_GROUP + j
                valid = (entry < listed).astype(f32)
                acc_q = acc_q + tile(jnp.minimum(entry, LIST_MAX - 1), inverse * valid, narrow)
            return acc_q

        def group(step, acc_q):
            entries = [jnp.minimum(1 + step * BWD_GROUP + j, LIST_MAX - 1) for j in range(BWD_GROUP)]
            return lax.cond(
                all_narrow(width_ref, slot, entries),
                lambda value: run(step, value, True),
                lambda value: run(step, value, False),
                acc_q,
            )

        total = tile(0, jnp.where(causal(), inverse, 0.0), False)
        steps = (listed - 1 + BWD_GROUP - 1) // BWD_GROUP
        total = lax.fori_loop(0, steps, group, total)
        dq_ref[slot * BLOCK : (slot + 1) * BLOCK, :] = (total * SCALE).astype(bf16)
    half = BLOCKS // 2
    own_ref[...] = acc[0:half].reshape(own_ref.shape)
    other_ref[0 : 4 * TILES] = acc[half:].reshape(own_ref.shape).astype(bf16)
    bins = jnp.sum(bins_ref[0:BUCKETS], axis=1)
    high = bins.astype(bf16)
    low = (bins - high.astype(f32)).astype(bf16)
    rest = jnp.zeros((BLOCK - 2 * BUCKETS, BLOCK), bf16)
    other_ref[4 * TILES] = jnp.concatenate([high, low, rest], 0)


SMEM = functools.partial(pl.BlockSpec, memory_space=pltpu.SMEM)
VMEM = functools.partial(pl.BlockSpec, memory_space=pltpu.VMEM)
ANY = functools.partial(pl.BlockSpec, memory_space=pl.ANY)


def attend(tables, query, parts):
    return pl.pallas_call(
        attend_kernel,
        out_shape=jax.ShapeDtypeStruct((2 * BLOCK, HEAD_DIM), f32),
        in_specs=[SMEM()] * 8 + [VMEM()] * 2 + [ANY()] * PARTS,
        out_specs=VMEM(),
        scratch_shapes=[
            pltpu.VMEM((BLOCKS * BLOCK, 2 * HEAD_DIM), bf16),
            pltpu.SemaphoreType.DMA((PARTS,)),
        ],
        compiler_params=pltpu.CompilerParams(vmem_limit_bytes=VMEM_LIMIT),
        cost_estimate=pl.CostEstimate(
            flops=5 * 10**9, bytes_accessed=3 << 20, transcendentals=48 * BLOCK**2
        ),
        name="attend",
    )(*tables, query, *parts)


def attend_grads(tables, query, grad, parts):
    return pl.pallas_call(
        grads_kernel,
        out_shape=(
            jax.ShapeDtypeStruct((4 * TILES, HEAD_DIM, BLOCK), f32),
            jax.ShapeDtypeStruct((4 * TILES + 1, HEAD_DIM, BLOCK), bf16),
            jax.ShapeDtypeStruct((2 * BLOCK, HEAD_DIM), bf16),
            jax.ShapeDtypeStruct((BUCKETS + 1, 8, BLOCK), f32),
        ),
        in_specs=[SMEM()] * 8 + [VMEM()] * 3 + [ANY()] * PARTS,
        out_specs=(VMEM(),) * 4,
        scratch_shapes=[
            pltpu.VMEM((BLOCKS * BLOCK, 2 * HEAD_DIM), bf16),
            pltpu.VMEM((BLOCKS, 2, HEAD_DIM, BLOCK), f32),
            pltpu.SemaphoreType.DMA((PARTS,)),
        ],
        compiler_params=pltpu.CompilerParams(vmem_limit_bytes=VMEM_LIMIT),
        cost_estimate=pl.CostEstimate(
            flops=12 * 10**9, bytes_accessed=6 << 20, transcendentals=48 * BLOCK**2
        ),
        name="attend_grads",
    )(*tables, query, grad, *parts)


def exchange(values, axes):
    return lax.all_to_all(values, axes, split_axis=0, concat_axis=0, tiled=True)


def to_all(values, axes, count):
    return exchange(jnp.broadcast_to(values[None], (count,) + values.shape), axes)


def swap_core(values):
    return lax.ppermute(values, "core", [(0, 1), (1, 0)])


def shift_x(values, by):
    return lax.ppermute(values, "x", [(i, (i + by) % 4) for i in range(4)])


def flip(values, axis, by):
    return lax.ppermute(values, axis, [(i, i ^ by) for i in range(lax.axis_size(axis))])


def after(values, *others):
    return lax.optimization_barrier((values,) + others)[0]


def joined(values, theirs, axis, by):
    late = (lax.axis_index(axis) & by) != 0
    return jnp.concatenate([jnp.where(late, theirs, values), jnp.where(late, values, theirs)], 1)


def halves(bias):
    high = lax.reduce_precision(bias, exponent_bits=8, mantissa_bits=7)
    return jnp.pad(jnp.stack([high, bias - high]), ((0, 14), (0, BLOCK - BUCKETS)))


def whole(rows):
    return rows[0, :BUCKETS] + rows[1, :BUCKETS]


def tables_of(lists, blk, pos, home, run, stamp_blocks, time_bias):
    listed = jnp.sum((lists >= 0).astype(jnp.int32), 1)
    powers = 2 ** jnp.arange(BUCKETS - 1, dtype=jnp.int32)
    own = lax.dynamic_slice_in_dim(stamp_blocks, run * 2, 2, 0)
    first = stamp_blocks[:, 0][blk]
    last = stamp_blocks[:, BLOCK - 1][blk]
    least = jnp.maximum(own[:, :1] - last, 0)
    most = own[:, BLOCK - 1 :] - first
    low = jnp.sum((least[:, :, None] >= powers).astype(jnp.int32), -1)
    high = jnp.sum((most[:, :, None] >= powers).astype(jnp.int32), -1)
    bias = jnp.concatenate([time_bias, jnp.zeros((1,), f32)])
    limits = jnp.concatenate([jnp.zeros((1,), jnp.int32), powers, jnp.full((1,), 1 << 30)])
    return (pos, home, blk, low, high - low, listed, bias, limits.astype(f32), stamp_blocks)


def body(projected, cotangent, out_weight, time_bias, block_lists, stamps):
    tokens = projected.shape[1]
    x, zh, core = lax.axis_index("x"), lax.axis_index("zh"), lax.axis_index("core")
    run = (x * 2 + zh) * 2 + core

    by_head = projected[0].reshape(tokens, 4, HEADS, HEAD_DIM).transpose(2, 0, 1, 3)
    pairs = by_head[:, :, 1:3].reshape(HEADS, tokens, 2 * HEAD_DIM)
    pairs = exchange(jnp.concatenate([pairs, pairs], 0), ZLINE).reshape(4 * BLOCK, 2 * HEAD_DIM)
    dp = lax.axis_index("dp")
    slab = lax.dynamic_slice(out_weight, (dp * tokens, (x * 2 + core) * BLOCK), (tokens, BLOCK))
    rest = jnp.concatenate([cotangent[0], slab], 1)
    rest = jnp.broadcast_to(rest, (HEADS,) + rest.shape)
    rest = exchange(jnp.concatenate([by_head[:, :, 0], by_head[:, :, 3], rest], 2), "head")
    slabs = rest[:, :, 2 * HEAD_DIM + D :].reshape(HEADS * tokens, BLOCK)
    all_weight = lax.all_gather(slabs, ("x", "core", "dp"), axis=0, tiled=True)
    all_weight = all_weight.reshape(8, 4, HEADS, tokens, BLOCK).transpose(0, 2, 1, 3, 4)
    all_weight = all_weight.reshape(8, D, BLOCK)
    rest = rest[:, :, : 2 * HEAD_DIM + D].reshape(2 * BLOCK, 2 * HEAD_DIM + D)
    query = rest[:, :HEAD_DIM]
    gate = rest[:, HEAD_DIM : 2 * HEAD_DIM].astype(f32)
    cot = rest[:, 2 * HEAD_DIM :]
    own_pairs = jnp.concatenate([pairs] + [shift_x(pairs, by) for by in SHIFTS], 0)
    parts = [own_pairs, swap_core(own_pairs)]

    lists = lax.dynamic_slice_in_dim(block_lists[0], run * 2, 2, 0)
    blk = jnp.maximum(lists, 0)
    side = ((blk // 2) % 2) ^ core
    ahead = (x - blk // 8) & 3
    place = jnp.where(ahead == 2, 3, jnp.where(ahead == 3, 2, ahead))
    pos = ((side * 4 + place) * 2 + (blk // 4) % 2) * 2 + blk % 2
    home = ((side * 4 + blk // 8) * 2 + (blk // 4) % 2) * 2 + blk % 2
    stamp_blocks = stamps[0].reshape(BLOCKS, BLOCK)
    tables = tables_of(lists, blk, pos, home, run, stamp_blocks, time_bias[0])

    attended = attend(tables, query, parts)

    gated_grad = nt_dot(cot, out_weight)
    normed_grad = gated_grad * gate
    sums = jnp.stack(
        [
            jnp.sum(attended, 1),
            jnp.sum(attended * attended, 1),
            jnp.sum(normed_grad, 1),
            jnp.sum(normed_grad * attended, 1),
        ]
    )
    sums = jnp.sum(to_all(sums, "head", HEADS).reshape(HEADS, 4, 2 * BLOCK), 0) / D
    mean = sums[0]
    inverse = lax.rsqrt(sums[1] - mean * mean + EPS)
    first = sums[2]
    second = inverse * (sums[3] - mean * sums[2])
    normed = (attended - mean[:, None]) * inverse[:, None]
    gated = (normed * gate).astype(bf16)
    grad_u = (gated_grad * normed).astype(bf16)
    attended_grad = (
        (normed_grad - first[:, None] - normed * second[:, None]) * inverse[:, None]
    ).astype(bf16)

    weight_part = lax.dot_general(gated, cot, (((0,), (0,)), ((), ())), preferred_element_type=f32)
    weight_part = weight_part.astype(bf16).reshape(HEAD_DIM, 8, BLOCK).transpose(1, 0, 2)
    weight_part = exchange(weight_part, "dp").reshape(4, 2, HEAD_DIM, BLOCK)

    own_grads, other_grads, grad_q, bins = attend_grads(tables, query, attended_grad, parts)
    weight_part = jnp.sum(weight_part.astype(f32), 0)
    sent = lax.dynamic_index_in_dim(weight_part, 1 - core, 0, True).astype(bf16)
    theirs = swap_core(jnp.concatenate([other_grads, sent], 0)).astype(f32)
    chip = (own_grads + theirs[: 4 * TILES]).reshape(4, TILES * HEAD_DIM, BLOCK)
    weight_part = lax.dynamic_index_in_dim(weight_part, core, 0, False) + theirs[4 * TILES + 1]
    bias_part = jnp.sum(theirs[4 * TILES, : 2 * BUCKETS], 1).reshape(2, BUCKETS).sum(0)
    bias_part += jnp.sum(bins, (1, 2))[:BUCKETS]
    side = jnp.concatenate([weight_part, halves(bias_part)], 0)
    side = jnp.broadcast_to(side, (4,) + side.shape)
    chip = jnp.concatenate([chip, side], 1).astype(bf16)
    line = jnp.sum(exchange(chip, "x").reshape(chip.shape).astype(f32), 0)

    split = TILES * HEAD_DIM
    pair = line[:split].reshape(2, split // 2, BLOCK)
    own_tiles = lax.dynamic_index_in_dim(pair, zh, 0, False)
    sent = lax.dynamic_index_in_dim(pair, 1 - zh, 0, False)
    weight_part, bias_part = line[split : split + HEAD_DIM], whole(line[split + HEAD_DIM :])
    sent = jnp.concatenate([sent, weight_part, halves(bias_part)], 0).astype(bf16)
    theirs = flip(sent, "zh", 1).astype(f32)
    own_tiles = own_tiles + theirs[: split // 2]
    theirs = theirs[split // 2 :]
    columns = weight_part.astype(bf16).astype(f32) + theirs[:HEAD_DIM]
    bias_part = bias_part + whole(theirs[HEAD_DIM:])

    for by in (1, 2):
        sent = jnp.pad(bias_part[None], ((0, 7), (0, columns.shape[1] - BUCKETS)))
        theirs = flip(jnp.concatenate([columns, sent], 0), "dp", by)
        bias_part = bias_part + theirs[HEAD_DIM, :BUCKETS]
        columns = joined(columns, theirs[:HEAD_DIM], "dp", by)
    bias_grad = bias_part[None]
    columns = columns.reshape(HEAD_DIM, 4, BLOCK)
    theirs = swap_core(columns)
    both = jnp.stack([jnp.where(core == 0, columns, theirs), jnp.where(core == 0, theirs, columns)])
    weight_grad = both.transpose(1, 2, 0, 3).reshape(HEAD_DIM, D)

    line = own_tiles.astype(bf16).reshape(2, 2, HEAD_DIM, BLOCK)
    line = line.transpose(0, 3, 1, 2).reshape(HEADS, tokens, 2 * HEAD_DIM)
    rows = jnp.concatenate([grad_q, grad_u, gated], 1).reshape(HEADS, tokens, 3 * HEAD_DIM)
    back = exchange(jnp.concatenate([line, rows], 2), "head")
    rows = back[:, :, 2 * HEAD_DIM :]
    pair_grads = back[:, :, : 2 * HEAD_DIM].astype(f32)
    grad_k = (pair_grads[:, :, :HEAD_DIM] * SCALE).astype(bf16)
    grad_v = pair_grads[:, :, HEAD_DIM:].astype(bf16)
    grad_u = rows[:, :, HEAD_DIM : 2 * HEAD_DIM]
    grads = jnp.stack([rows[:, :, :HEAD_DIM], grad_k, grad_v, grad_u], 0)
    input_grads = grads.transpose(2, 0, 1, 3).reshape(1, tokens, 4, D)
    token_side = rows[:, :, 2 * HEAD_DIM :].transpose(1, 0, 2).reshape(tokens, D)
    layer_out = jnp.concatenate([nn_dot(token_side, all_weight[k]) for k in range(8)], 1)
    layer_out = layer_out.astype(bf16).reshape(1, tokens, D)
    return (layer_out, input_grads, weight_grad, bias_grad)


def solution(mesh):
    fine = Mesh(
        mesh.devices.reshape(4, 4, 2, 2, 8), ("dp", "x", "zh", "core", "head")
    )
    run = SEQ + ("head",)
    in_specs = (
        P("dp", run, None, None),
        P("dp", run, None),
        P("head", None),
        P("head", None),
        P("dp", None, None),
        P("dp", None),
    )
    out_specs = (
        P("dp", run, None),
        P("dp", run, None, None),
        P("head", None),
        P("head", None),
    )
    return jax.shard_map(body, mesh=fine, in_specs=in_specs, out_specs=out_specs, check_vma=False)
```

time: 339 us -> 227 us (0.67)
  waiting for transfers between devices: 144 us -> 55.7 us
  blocking collectives: 72.7 us -> 0 us
  starting transfers between devices: 77.5 us -> 115 us
  local copies, waits for them, and re-layouts: 9.54 us -> 15.4 us
  other arithmetic: 6.31 us -> 11.3 us
    all_to_all x6, waiting for transfers between devices: 122 us -> 38.8 us  [exchange(): return lax.all_to_all(values, axes, split_axis=0, concat_axis=0, tiled=True)]
    all_to_all x3 -> x0, blocking collectives: 72.7 us -> none  [exchange(): return lax.all_to_all(values, axes, split_axis=0, concat_axis=0, tiled=True)]
    ppermute x0 -> x6, starting transfers between devices: none -> 38.2 us  [the longest x3 28.3 us: flip(): lax.ppermute(values, axis, [(i, i ^ by) for i in range(lax.axis_size(axis...]
    all_gather x1, waiting for transfers between devices: 18.9 us -> 0.01 us  [body(): all_weight = lax.all_gather(slabs, ('x', 'core', 'dp'), axis=0, tiled=True)]
    ppermute x0 -> x6, waiting for transfers between devices: none -> 13.8 us  [the longest x3 8.01 us: flip(): lax.ppermute(values, axis, [(i, i ^ by) for i in range(lax.axis_size(axis...]
    slice x3 -> x16, local copies, waits for them, and re-layouts: 0.1 us -> 3.99 us  [the longest x9 2.04 us: body(): all_weight[k]]
    concatenate x2 -> x12, other arithmetic: 0.95 us -> 4.81 us  [the longest x1 1.1 us: body(): chip = jnp.concatenate([chip, side], 1).astype(bf16)]
    all_to_all x6, starting transfers between devices: 69.9 us -> 66.4 us  [exchange(): return lax.all_to_all(values, axes, split_axis=0, concat_axis=0, tiled=True)]
  transfers between devices with their start and end apart: 9 -> 16, of which waited for: 8 -> 10; matrix products, arithmetic and copies ran while one was open for 3% -> 5% of each run, Pallas kernels for 1% -> 2%
where the time goes in v2:
time: 227 us; the launch traced here: 223 us
  starting transfers between devices  115 us (51%)
  waiting for transfers between devices  55.7 us (25%)
  local copies, waits for them, and re-layouts  15.4 us (7%)
  between operations  14.8 us (7%)
  other arithmetic  11.3 us (5%)
  Pallas kernels  7.79 us (3%)
  matrix products  3.15 us (1%)
    all_to_all x6, starting transfers between devices, exchange(): return lax.all_to_all(values, axes, split_axis=0, concat_axis=0, tiled=True)  66.4 us
    all_to_all x6, waiting for transfers between devices, exchange(): return lax.all_to_all(values, axes, split_axis=0, concat_axis=0, tiled=True)  38.8 us
    ppermute x3, starting transfers between devices, flip(): lax.ppermute(values, axis, [(i, i ^ by) for i in range(lax.axis_size(axis...  28.3 us
    ppermute x3, starting transfers between devices, swap_core(): return lax.ppermute(values, 'core', [(0, 1), (1, 0)])  10.5 us
    ppermute x3, starting transfers between devices, shift_x(): return lax.ppermute(values, 'x', [(i, (i + by) % 4) for i in range(4)])  9.93 us
    ppermute x3, waiting for transfers between devices, flip(): lax.ppermute(values, axis, [(i, i ^ by) for i in range(lax.axis_size(axis...  8.01 us
    ppermute x3, waiting for transfers between devices, shift_x(): return lax.ppermute(values, 'x', [(i, (i + by) % 4) for i in range(4)])  5.76 us
    pallas_call x1, Pallas kernels, attend_grads(): pl.pallas_call(grads_kernel, out_shape=(jax.ShapeDtypeStruct((4 * TILES,...  5.14 us
  transfers between devices with their start and end apart: 16, of which 10 were waited for; matrix products, arithmetic and copies ran while one was open for 5% of the time, Pallas kernels for 2%

profile of v2, /device:TPU:1, one launch (start us, length us, event | category | flops | bytes accessed | tf_op | source)
XLA Modules:
  0.0 223.3 jit_solution(17648170795553673887)
XLA Ops:
  9.1 15.7 %all-to-all-start.1 = ((bf16[16,32,256]{2,1,0:T(8,128)(2,1)}), bf16[16,32,256]{2,1,0:T(8,128)(2,1)S(1)}, u32[]{:S(2)}, u32[]{:S(2)}) async-start(bf16[16,32,256]{2,1,0:T(8,128)(2,1)} %pad_maximum_fusion.5), calls=%async_computation.1 | async-start | bytes 524288 | tf_op jit(solution)/shard_map/all_to_all | solution.py:252
  26.7 11.4 %all-to-all-done.1 = bf16[16,32,256]{2,1,0:T(8,128)(2,1)S(1)} async-done(((bf16[16,32,256]{2,1,0:T(8,128)(2,1)}), bf16[16,32,256]{2,1,0:T(8,128)(2,1)S(1)}, u32[]{:S(2)}, u32[]{:S(2)}) %all-to-all-start.1) | async-done | bytes 262176 | tf_op jit(solution)/shard_map/all_to_all | solution.py:252
  38.0 10.8 %all-to-all-start = ((bf16[8,32,1408]{2,1,0:T(8,128)(2,1)}), bf16[8,32,1408]{2,1,0:T(8,128)(2,1)S(1)}, u32[]{:S(2)}, u32[]{:S(2)}) async-start(bf16[8,32,1408]{2,1,0:T(8,128)(2,1)} %pad_maximum_fusion.3), calls=%async_computation | async-start | bytes 1441792 | tf_op jit(solution)/shard_map/all_to_all | solution.py:252
  49.2 3.1 %collective-permute-start = (bf16[512,256]{1,0:T(8,128)(2,1)S(1)}, bf16[512,256]{1,0:T(8,128)(2,1)S(1)}, u32[]{:S(2)}, u32[]{:S(2)}) collective-permute-start(bf16[512,256]{1,0:T(8,128)(2,1)S(1)} %bitcast.189), channel_id=1, source_target_pairs={{0,32},{32,64},{64,96},{96,0},{1,33},{33,65},{65,97},{97,1},{2,34}... | collective-permute-start | bytes 786440 | tf_op jit(solution)/shard_map/ppermute | solution.py:264
  52.4 3.4 %collective-permute-start.1 = (bf16[512,256]{1,0:T(8,128)(2,1)S(1)}, bf16[512,256]{1,0:T(8,128)(2,1)S(1)}, u32[]{:S(2)}, u32[]{:S(2)}) collective-permute-start(bf16[512,256]{1,0:T(8,128)(2,1)S(1)} %bitcast.190), channel_id=1, source_target_pairs={{0,96},{32,0},{64,32},{96,64},{1,97},{33,1},{65,33},{97,65},{2,98}... | collective-permute-start | bytes 786440 | tf_op jit(solution)/shard_map/ppermute | solution.py:264
  55.7 3.4 %collective-permute-start.2 = (bf16[512,256]{1,0:T(8,128)(2,1)S(1)}, bf16[512,256]{1,0:T(8,128)(2,1)S(1)}, u32[]{:S(2)}, u32[]{:S(2)}) collective-permute-start(bf16[512,256]{1,0:T(8,128)(2,1)S(1)} %bitcast.191), channel_id=1, source_target_pairs={{0,64},{32,96},{64,0},{96,32},{1,65},{33,97},{65,1},{97,33},{2,66}... | collective-permute-start | bytes 786440 | tf_op jit(solution)/shard_map/ppermute | solution.py:264
  60.8 4.6 %collective-permute-done.2 = bf16[512,256]{1,0:T(8,128)(2,1)S(1)} collective-permute-done((bf16[512,256]{1,0:T(8,128)(2,1)S(1)}, bf16[512,256]{1,0:T(8,128)(2,1)S(1)}, u32[]{:S(2)}, u32[]{:S(2)}) %collective-permute-start.2) | collective-permute-done | bytes 262176 | tf_op jit(solution)/shard_map/ppermute | solution.py:264
  65.4 4.4 %collective-permute-start.3 = (bf16[2048,256]{1,0:T(8,128)(2,1)S(1)}, bf16[2048,256]{1,0:T(8,128)(2,1)S(1)}, u32[]{:S(2)}, u32[]{:S(2)}) collective-permute-start(bf16[2048,256]{1,0:T(8,128)(2,1)S(1)} %pad_maximum_fusion.2.refs_0_), channel_id=1, source_target_pairs={{0,8},{8,0},{1,9},{9,1},{2,10},{10,2},{3,11},{11,3},{4,12},{12,4},... | collective-permute-start | bytes 3145736 | tf_op jit(solution)/shard_map/ppermute | solution.py:260
  72.0 3.4 %all-to-all-done = bf16[8,32,1408]{2,1,0:T(8,128)(2,1)S(1)} async-done(((bf16[8,32,1408]{2,1,0:T(8,128)(2,1)}), bf16[8,32,1408]{2,1,0:T(8,128)(2,1)S(1)}, u32[]{:S(2)}, u32[]{:S(2)}) %all-to-all-start) | async-done | bytes 720928 | tf_op jit(solution)/shard_map/all_to_all | solution.py:252
  75.5 2.7 %attend.1 = f32[256,128]{1,0:T(8,128)S(1)} custom-call(s32[2,24]{1,0:T(2,128)S(1)} %multiply_add_fusion.1.pos_ref, s32[2,24]{1,0:T(2,128)S(1)} %get-tuple-element.40.home_ref, s32[2,24]{1,0:T(2,128)S(1)} %get-tuple-element.74.blk_ref, s32[2,24]{1,0:T(2,128)S(1)} %get-tuple-element.37.low_ref, s32[2,24]{1,0:T(2,128)S(1)} %sub.113.width_ref, ...), custom_call_target="tpu_custom_call" | custom-call | flops 5000000000 | bytes 3145728 | tf_op jit(solution)/shard_map/attend/pallas_call | solution.py:210
  79.3 14.7 %all-to-all-start.2 = ((f32[8,4,256]{2,1,0:T(4,128)}), f32[8,4,256]{2,1,0:T(4,128)S(1)}, u32[]{:S(2)}, u32[]{:S(2)}) async-start(f32[8,4,256]{2,1,0:T(4,128)} %broadcast_in_dim.14), calls=%async_computation.2 | async-start | bytes 65536 | tf_op jit(solution)/shard_map/all_to_all | solution.py:252
  94.0 9.5 %all-to-all-done.2 = f32[8,4,256]{2,1,0:T(4,128)S(1)} async-done(((f32[8,4,256]{2,1,0:T(4,128)}), f32[8,4,256]{2,1,0:T(4,128)S(1)}, u32[]{:S(2)}, u32[]{:S(2)}) %all-to-all-start.2) | async-done | bytes 32800 | tf_op jit(solution)/shard_map/all_to_all | solution.py:252
  107.3 4.2 %all-to-all-start.3 = ((bf16[8,128,128]{2,1,0:T(8,128)(2,1)}), bf16[8,128,128]{2,1,0:T(8,128)(2,1)}, u32[]{:S(2)}, u32[]{:S(2)}) async-start(bf16[8,128,128]{2,1,0:T(8,128)(2,1)} %bitcast.165), calls=%async_computation.3 | async-start | bytes 524288 | tf_op jit(solution)/shard_map/all_to_all | solution.py:252
  114.0 5.1 %attend_grads.1 = (f32[32,128,128]{2,1,0:T(8,128)S(1)}, bf16[33,128,128]{2,1,0:T(8,128)(2,1)S(1)}, bf16[256,128]{1,0:T(8,128)(2,1)S(1)}, f32[17,8,128]{2,1,0:T(8,128)S(1)}) custom-call(s32[2,24]{1,0:T(2,128)S(1)} %multiply_add_fusion.1.pos_ref, s32[2,24]{1,0:T(2,128)S(1)} %get-tuple-element.40.home_ref, s32[2,24]{1,0:T(2,128)S(1)} %get-tuple-element.74.blk_ref, ...), custom_call_target="tpu_custom_call" | custom-call | flops 12000000000 | bytes 6291456 | tf_op jit(solution)/shard_map/attend_grads/pallas_call | solution.py:228
  121.2 3.0 %collective-permute-start.4 = (bf16[34,128,128]{2,1,0:T(8,128)(2,1)}, bf16[34,128,128]{2,1,0:T(8,128)(2,1)}, u32[]{:S(2)}, u32[]{:S(2)}) collective-permute-start(bf16[34,128,128]{2,1,0:T(8,128)(2,1)} %pad_maximum_fusion.1), channel_id=1, source_target_pairs={{0,8},{8,0},{1,9},{9,1},{2,10},{10,2},{3,11},{11,3},{4,12},{12,4},... | collective-permute-start | bytes 3342344 | tf_op jit(solution)/shard_map/ppermute | solution.py:260
  130.2 9.2 %all-to-all-start.4 = ((bf16[4,1168,128]{2,1,0:T(8,128)(2,1)}), bf16[4,1168,128]{2,1,0:T(8,128)(2,1)S(1)}, u32[]{:S(2)}, u32[]{:S(2)}) async-start(bf16[4,1168,128]{2,1,0:T(8,128)(2,1)} %pad_maximum_fusion), calls=%async_computation.4 | async-start | bytes 2392064 | tf_op jit(solution)/shard_map/all_to_all | solution.py:252
  141.0 14.5 %all-to-all-done.4 = bf16[4,1168,128]{2,1,0:T(8,128)(2,1)S(1)} async-done(((bf16[4,1168,128]{2,1,0:T(8,128)(2,1)}), bf16[4,1168,128]{2,1,0:T(8,128)(2,1)S(1)}, u32[]{:S(2)}, u32[]{:S(2)}) %all-to-all-start.4) | async-done | bytes 1196064 | tf_op jit(solution)/shard_map/all_to_all | solution.py:252
  155.8 14.3 %collective-permute-start.5 = (bf16[656,128]{1,0:T(8,128)(2,1)S(1)}, bf16[656,128]{1,0:T(8,128)(2,1)S(1)}, u32[]{:S(2)}, u32[]{:S(2)}) collective-permute-start(bf16[656,128]{1,0:T(8,128)(2,1)S(1)} %pad_maximum_fusion.8), channel_id=1, source_target_pairs={{0,16},{16,0},{1,17},{17,1},{2,18},{18,2},{3,19},{19,3},{4,20},{20... | collective-permute-start | bytes 503816 | tf_op jit(solution)/shard_map/ppermute | solution.py:268
  170.2 3.3 %collective-permute-done.5 = bf16[656,128]{1,0:T(8,128)(2,1)S(1)} collective-permute-done((bf16[656,128]{1,0:T(8,128)(2,1)S(1)}, bf16[656,128]{1,0:T(8,128)(2,1)S(1)}, u32[]{:S(2)}, u32[]{:S(2)}) %collective-permute-start.5) | collective-permute-done | bytes 167968 | tf_op jit(solution)/shard_map/ppermute | solution.py:268
  173.5 7.1 %collective-permute-start.6 = (f32[136,128]{1,0:T(8,128)S(1)}, f32[136,128]{1,0:T(8,128)S(1)}, u32[]{:S(2)}, u32[]{:S(2)}) collective-permute-start(f32[136,128]{1,0:T(8,128)S(1)} %select_maximum_fusion.1), channel_id=1, source_target_pairs={{0,128},{128,0},{256,384},{384,256},{1,129},{129,1},{257,385},{385... | collective-permute-start | bytes 208904 | tf_op jit(solution)/shard_map/ppermute | solution.py:268
  181.7 11.8 %all-to-all-start.5 = ((bf16[8,32,640]{2,1,0:T(8,128)(2,1)}), bf16[8,32,640]{2,1,0:T(8,128)(2,1)S(1)}, u32[]{:S(2)}, u32[]{:S(2)}) async-start(bf16[8,32,640]{2,1,0:T(8,128)(2,1)} %pad_maximum_fusion.4), calls=%async_computation.5 | async-start | bytes 655360 | tf_op jit(solution)/shard_map/all_to_all | solution.py:252
  193.5 6.9 %collective-permute-start.7 = (f32[136,256]{1,0:T(8,128)S(1)}, f32[136,256]{1,0:T(8,128)S(1)}, u32[]{:S(2)}, u32[]{:S(2)}) collective-permute-start(f32[136,256]{1,0:T(8,128)S(1)} %select_maximum_fusion), channel_id=1, source_target_pairs={{0,256},{128,384},{256,0},{384,128},{1,257},{129,385},{257,1},{385... | collective-permute-start | bytes 417800 | tf_op jit(solution)/shard_map/ppermute | solution.py:268
  200.4 4.7 %collective-permute-done.7 = f32[136,256]{1,0:T(8,128)S(1)} collective-permute-done((f32[136,256]{1,0:T(8,128)S(1)}, f32[136,256]{1,0:T(8,128)S(1)}, u32[]{:S(2)}, u32[]{:S(2)}) %collective-permute-start.7) | collective-permute-done | bytes 139296 | tf_op jit(solution)/shard_map/ppermute | solution.py:268
  205.3 3.0 %collective-permute-start.8 = (f32[128,4,128]{2,1,0:T(4,128)S(1)}, f32[128,4,128]{2,1,0:T(4,128)S(1)}, u32[]{:S(2)}, u32[]{:S(2)}) collective-permute-start(f32[128,4,128]{2,1,0:T(4,128)S(1)} %reshape.331), channel_id=1, source_target_pairs={{0,8},{8,0},{1,9},{9,1},{2,10},{10,2},{3,11},{11,3},{4,12},{12,4},... | collective-permute-start | bytes 786440 | tf_op jit(solution)/shard_map/ppermute | solution.py:260
  (149 shorter events, 34.2 us)
Async XLA Ops:
  7.2 41.7 %copy-start = (s32[1,32,24]{1,2,0:T(8,128)S(1)}, s32[1,32,24]{1,2,0:T(8,128)}, u32[]{:S(2)}) copy-start(s32[1,32,24]{1,2,0:T(8,128)} %param.10) | copy-start | bytes 9220
  7.2 18.4 %copy-start.11 = (bf16[1,32,1024]{2,1,0:T(8,128)(2,1)S(1)}, bf16[1,32,1024]{2,1,0:T(8,128)(2,1)}, u32[]{:S(2)}) copy-start(bf16[1,32,1024]{2,1,0:T(8,128)(2,1)} %param.7) | copy-start | bytes 196612
  9.1 28.9 %all-to-all-start.1 = ((bf16[16,32,256]{2,1,0:T(8,128)(2,1)}), bf16[16,32,256]{2,1,0:T(8,128)(2,1)S(1)}, u32[]{:S(2)}, u32[]{:S(2)}) async-start(bf16[16,32,256]{2,1,0:T(8,128)(2,1)} %pad_maximum_fusion.5), calls=%async_computation.1 | async-start | bytes 524288 | tf_op jit(solution)/shard_map/all_to_all | solution.py:252
  24.9 34.3 %copy-start.3 = (s32[1,4096]{1,0:T(1,128)S(1)}, s32[1,4096]{1,0:T(1,128)}, u32[]{:S(2)}) copy-start(s32[1,4096]{1,0:T(1,128)} %param.11) | copy-start | bytes 49156
  38.0 37.4 %all-to-all-start = ((bf16[8,32,1408]{2,1,0:T(8,128)(2,1)}), bf16[8,32,1408]{2,1,0:T(8,128)(2,1)S(1)}, u32[]{:S(2)}, u32[]{:S(2)}) async-start(bf16[8,32,1408]{2,1,0:T(8,128)(2,1)} %pad_maximum_fusion.3), calls=%async_computation | async-start | bytes 1441792 | tf_op jit(solution)/shard_map/all_to_all | solution.py:252
  49.2 10.4 %collective-permute-start = (bf16[512,256]{1,0:T(8,128)(2,1)S(1)}, bf16[512,256]{1,0:T(8,128)(2,1)S(1)}, u32[]{:S(2)}, u32[]{:S(2)}) collective-permute-start(bf16[512,256]{1,0:T(8,128)(2,1)S(1)} %bitcast.189), channel_id=1, source_target_pairs={{0,32},{32,64},{64,96},{96,0},{1,33},{33,65},{65,97},{97,1},{2,34}... | collective-permute-start | bytes 786440 | tf_op jit(solution)/shard_map/ppermute | solution.py:264
  52.4 8.4 %collective-permute-start.1 = (bf16[512,256]{1,0:T(8,128)(2,1)S(1)}, bf16[512,256]{1,0:T(8,128)(2,1)S(1)}, u32[]{:S(2)}, u32[]{:S(2)}) collective-permute-start(bf16[512,256]{1,0:T(8,128)(2,1)S(1)} %bitcast.190), channel_id=1, source_target_pairs={{0,96},{32,0},{64,32},{96,64},{1,97},{33,1},{65,33},{97,65},{2,98}... | collective-permute-start | bytes 786440 | tf_op jit(solution)/shard_map/ppermute | solution.py:264
  55.7 9.6 %collective-permute-start.2 = (bf16[512,256]{1,0:T(8,128)(2,1)S(1)}, bf16[512,256]{1,0:T(8,128)(2,1)S(1)}, u32[]{:S(2)}, u32[]{:S(2)}) collective-permute-start(bf16[512,256]{1,0:T(8,128)(2,1)S(1)} %bitcast.191), channel_id=1, source_target_pairs={{0,64},{32,96},{64,0},{96,32},{1,65},{33,97},{65,1},{97,33},{2,66}... | collective-permute-start | bytes 786440 | tf_op jit(solution)/shard_map/ppermute | solution.py:264
  59.6 12.3 %copy-start.14 = (f32[1,16]{1,0:T(1,128)S(1)}, f32[1,16]{1,0:T(1,128)}, u32[]{:S(2)}) copy-start(f32[1,16]{1,0:T(1,128)} %param.9) | copy-start | bytes 196
  65.4 12.7 %copy-start.1 = (bf16[2048,256]{1,0:T(8,128)(2,1)}, bf16[2048,256]{1,0:T(8,128)(2,1)S(1)}, u32[]{:S(2)}) copy-start(bf16[2048,256]{1,0:T(8,128)(2,1)S(1)} %pad_maximum_fusion.2.refs_0_) | copy-start | bytes 3145732
  65.4 10.0 %collective-permute-start.3 = (bf16[2048,256]{1,0:T(8,128)(2,1)S(1)}, bf16[2048,256]{1,0:T(8,128)(2,1)S(1)}, u32[]{:S(2)}, u32[]{:S(2)}) collective-permute-start(bf16[2048,256]{1,0:T(8,128)(2,1)S(1)} %pad_maximum_fusion.2.refs_0_), channel_id=1, source_target_pairs={{0,8},{8,0},{1,9},{9,1},{2,10},{10,2},{3,11},{11,3},{4,12},{12,4},... | collective-permute-start | bytes 3145736 | tf_op jit(solution)/shard_map/ppermute | solution.py:260
  79.3 24.2 %all-to-all-start.2 = ((f32[8,4,256]{2,1,0:T(4,128)}), f32[8,4,256]{2,1,0:T(4,128)S(1)}, u32[]{:S(2)}, u32[]{:S(2)}) async-start(f32[8,4,256]{2,1,0:T(4,128)} %broadcast_in_dim.14), calls=%async_computation.2 | async-start | bytes 65536 | tf_op jit(solution)/shard_map/all_to_all | solution.py:252
  105.2 6.3 %copy-start.8 = (bf16[256,128]{1,0:T(8,128)(2,1)}, bf16[256,128]{1,0:T(8,128)(2,1)S(1)}, u32[]{:S(2)}) copy-start(bf16[256,128]{1,0:T(8,128)(2,1)S(1)} %get-tuple-element.51) | copy-start | bytes 196612
  107.3 11.8 %all-to-all-start.3 = ((bf16[8,128,128]{2,1,0:T(8,128)(2,1)}), bf16[8,128,128]{2,1,0:T(8,128)(2,1)}, u32[]{:S(2)}, u32[]{:S(2)}) async-start(bf16[8,128,128]{2,1,0:T(8,128)(2,1)} %bitcast.165), calls=%async_computation.3 | async-start | bytes 524288 | tf_op jit(solution)/shard_map/all_to_all | solution.py:252
  121.2 5.7 %collective-permute-start.4 = (bf16[34,128,128]{2,1,0:T(8,128)(2,1)}, bf16[34,128,128]{2,1,0:T(8,128)(2,1)}, u32[]{:S(2)}, u32[]{:S(2)}) collective-permute-start(bf16[34,128,128]{2,1,0:T(8,128)(2,1)} %pad_maximum_fusion.1), channel_id=1, source_target_pairs={{0,8},{8,0},{1,9},{9,1},{2,10},{10,2},{3,11},{11,3},{4,12},{12,4},... | collective-permute-start | bytes 3342344 | tf_op jit(solution)/shard_map/ppermute | solution.py:260
  130.2 25.3 %all-to-all-start.4 = ((bf16[4,1168,128]{2,1,0:T(8,128)(2,1)}), bf16[4,1168,128]{2,1,0:T(8,128)(2,1)S(1)}, u32[]{:S(2)}, u32[]{:S(2)}) async-start(bf16[4,1168,128]{2,1,0:T(8,128)(2,1)} %pad_maximum_fusion), calls=%async_computation.4 | async-start | bytes 2392064 | tf_op jit(solution)/shard_map/all_to_all | solution.py:252
  139.4 30.8 %copy-start.9 = (bf16[256,128]{1,0:T(8,128)(2,1)S(1)}, bf16[256,128]{1,0:T(8,128)(2,1)}, u32[]{:S(2)}) copy-start(bf16[256,128]{1,0:T(8,128)(2,1)} %copy-done.8) | copy-start | bytes 196612
  139.4 30.8 %copy-start.10 = (bf16[256,128]{1,0:T(8,128)(2,1)S(1)}, bf16[256,128]{1,0:T(8,128)(2,1)}, u32[]{:S(2)}) copy-start(bf16[256,128]{1,0:T(8,128)(2,1)} %get-tuple-element.60) | copy-start | bytes 196612
  139.4 72.9 %all-gather.2.cloned.1.call-start = ((), (), s32[]{:S(2)}) async-start(), calls=%async_computation.6 | async-start | bytes 2162688 | tf_op jit(solution)/shard_map/all_gather | solution.py:318
  155.8 17.7 %collective-permute-start.5 = (bf16[656,128]{1,0:T(8,128)(2,1)S(1)}, bf16[656,128]{1,0:T(8,128)(2,1)S(1)}, u32[]{:S(2)}, u32[]{:S(2)}) collective-permute-start(bf16[656,128]{1,0:T(8,128)(2,1)S(1)} %pad_maximum_fusion.8), channel_id=1, source_target_pairs={{0,16},{16,0},{1,17},{17,1},{2,18},{18,2},{3,19},{19,3},{4,20},{20... | collective-permute-start | bytes 503816 | tf_op jit(solution)/shard_map/ppermute | solution.py:268
  173.5 19.9 %collective-permute-start.6 = (f32[136,128]{1,0:T(8,128)S(1)}, f32[136,128]{1,0:T(8,128)S(1)}, u32[]{:S(2)}, u32[]{:S(2)}) collective-permute-start(f32[136,128]{1,0:T(8,128)S(1)} %select_maximum_fusion.1), channel_id=1, source_target_pairs={{0,128},{128,0},{256,384},{384,256},{1,129},{129,1},{257,385},{385... | collective-permute-start | bytes 208904 | tf_op jit(solution)/shard_map/ppermute | solution.py:268
  181.7 29.6 %all-to-all-start.5 = ((bf16[8,32,640]{2,1,0:T(8,128)(2,1)}), bf16[8,32,640]{2,1,0:T(8,128)(2,1)S(1)}, u32[]{:S(2)}, u32[]{:S(2)}) async-start(bf16[8,32,640]{2,1,0:T(8,128)(2,1)} %pad_maximum_fusion.4), calls=%async_computation.5 | async-start | bytes 655360 | tf_op jit(solution)/shard_map/all_to_all | solution.py:252
  193.5 11.6 %collective-permute-start.7 = (f32[136,256]{1,0:T(8,128)S(1)}, f32[136,256]{1,0:T(8,128)S(1)}, u32[]{:S(2)}, u32[]{:S(2)}) collective-permute-start(f32[136,256]{1,0:T(8,128)S(1)} %select_maximum_fusion), channel_id=1, source_target_pairs={{0,256},{128,384},{256,0},{384,128},{1,257},{129,385},{257,1},{385... | collective-permute-start | bytes 417800 | tf_op jit(solution)/shard_map/ppermute | solution.py:268
  205.3 4.2 %collective-permute-start.8 = (f32[128,4,128]{2,1,0:T(4,128)S(1)}, f32[128,4,128]{2,1,0:T(4,128)S(1)}, u32[]{:S(2)}, u32[]{:S(2)}) collective-permute-start(f32[128,4,128]{2,1,0:T(4,128)S(1)} %reshape.331), channel_id=1, source_target_pairs={{0,8},{8,0},{1,9},{9,1},{2,10},{10,2},{3,11},{11,3},{4,12},{12,4},... | collective-permute-start | bytes 786440 | tf_op jit(solution)/shard_map/ppermute | solution.py:260
  (7 other events, 14.0 us)
Sparse Core Ops, SparseCore 0:
  143.9 63.1 all-gather.1

commit v3 on v2

--- a/solution.py
+++ b/solution.py
@@ -19,12 +19,12 @@
 
 SEQ = ("x", "zh", "core")
 ZLINE = ("zh", "head")
-VMEM_LIMIT = 48 * 1024 * 1024
+MIB = 1024 * 1024
 f32 = jnp.float32
 bf16 = jnp.bfloat16
 
-FWD_GROUP = 4
-BWD_GROUP = 4
+FWD_GROUP = 8
+BWD_GROUP = 8
 NARROW = 2
 PARTS = 2
 TILES = 8
@@ -83,46 +83,54 @@
         copies.append(pltpu.make_async_copy(part, kv.at[pl.ds(k * rows, rows)], sems.at[k]))
     for copy in copies:
         copy.start()
-    for copy in copies:
-        copy.wait()
+    return copies
+
+
+def loaded(kv, pos_ref, slot, entries):
+    keys, values = [], []
+    for entry in entries:
+        rows = pl.ds(pl.multiple_of(pos_ref[slot, entry] * BLOCK, BLOCK), BLOCK)
+        keys.append(kv[rows, 0:HEAD_DIM])
+        values.append(kv[rows, HEAD_DIM : 2 * HEAD_DIM])
+    return jnp.concatenate(keys, 0), jnp.concatenate(values, 0)
+
+
+def members(step, count, listed, inverse):
+    entries = [1 + step * count + j for j in range(count)]
+    shares = [inverse * (entry < listed).astype(f32) for entry in entries]
+    return [jnp.minimum(entry, LIST_MAX - 1) for entry in entries], shares
 
 
 def attend_kernel(
     pos_ref, home_ref, blk_ref, low_ref, width_ref, n_ref, bias_ref, power_ref, stamps_ref, q_ref, *refs
 ):
     parts, (out_ref, kv, sems) = refs[:PARTS], refs[PARTS:]
-    load_pairs(parts, kv, sems)
+    for copy in load_pairs(parts, kv, sems):
+        copy.wait()
     for slot in range(2):
         listed, query_stamps, inverse = slot_setup(slot, blk_ref, n_ref, stamps_ref)
         query = q_ref[slot * BLOCK : (slot + 1) * BLOCK, :]
 
-        def tile(entry, share, narrow):
-            rows = pl.ds(pl.multiple_of(pos_ref[slot, entry] * BLOCK, BLOCK), BLOCK)
-            key = kv[rows, 0:HEAD_DIM]
-            value = kv[rows, HEAD_DIM : 2 * HEAD_DIM]
-            spread = query_stamps - stamps_ref[pl.ds(blk_ref[slot, entry], 1), :].astype(f32)
-            bias = half_bias(spread, low_ref[slot, entry], narrow, bias_ref, power_ref)
-            half = nt_dot(query, key) * (0.5 * SCALE) + bias
-            weights = ((half + half * jnp.tanh(half)) * share).astype(bf16)
-            return nn_dot(weights, value)
-
-        def run(step, acc, narrow):
-            for j in range(FWD_GROUP):
-                entry = 1 + step * FWD_GROUP + j
-                valid = (entry < listed).astype(f32)
-                acc = acc + tile(jnp.minimum(entry, LIST_MAX - 1), inverse * valid, narrow)
-            return acc
+        def run(entries, shares, narrow):
+            keys, values = loaded(kv, pos_ref, slot, entries)
+            scores = nt_dot(query, keys) * (0.5 * SCALE)
+            weights = []
+            for j, (entry, share) in enumerate(zip(entries, shares)):
+                spread = query_stamps - stamps_ref[pl.ds(blk_ref[slot, entry], 1), :].astype(f32)
+                bias = half_bias(spread, low_ref[slot, entry], narrow, bias_ref, power_ref)
+                half = scores[:, j * BLOCK : (j + 1) * BLOCK] + bias
+                weights.append(((half + half * jnp.tanh(half)) * share).astype(bf16))
+            return nn_dot(jnp.concatenate(weights, 1), values)
 
         def group(step, acc):
-            entries = [jnp.minimum(1 + step * FWD_GROUP + j, LIST_MAX - 1) for j in range(FWD_GROUP)]
-            return lax.cond(
+            entries, shares = members(step, FWD_GROUP, listed, inverse)
+            return acc + lax.cond(
                 all_narrow(width_ref, slot, entries),
-                lambda value: run(step, value, True),
-                lambda value: run(step, value, False),
-                acc,
+                lambda: run(entries, shares, True),
+                lambda: run(entries, shares, False),
             )
 
-        total = tile(0, jnp.where(causal(), inverse, 0.0), False)
+        total = run([0], [jnp.where(causal(), inverse, 0.0)], False)
         steps = (listed - 1 + FWD_GROUP - 1) // FWD_GROUP
         out_ref[slot * BLOCK : (slot + 1) * BLOCK, :] = lax.fori_loop(0, steps, group, total)
 
@@ -132,9 +140,11 @@
 ):
     parts = refs[:PARTS]
     own_ref, other_ref, dq_ref, bins_ref, kv, acc, sems = refs[PARTS:]
+    copies = load_pairs(parts, kv, sems)
     acc[...] = jnp.zeros(acc.shape, f32)
     bins_ref[...] = jnp.zeros(bins_ref.shape, f32)
-    load_pairs(parts, kv, sems)
+    for copy in copies:
+        copy.wait()
     for slot in range(2):
         listed, query_stamps, inverse = slot_setup(slot, blk_ref, n_ref, stamps_ref)
         query = q_ref[slot * BLOCK : (slot + 1) * BLOCK, :]
@@ -145,49 +155,46 @@
         def fold(values):
             return jnp.sum(values.reshape(BLOCK // 8, 8, BLOCK), axis=0)
 
-        def tile(entry, share, narrow):
-            at = home_ref[slot, entry]
-            low = low_ref[slot, entry]
-            rows = pl.ds(pl.multiple_of(pos_ref[slot, entry] * BLOCK, BLOCK), BLOCK)
-            key = kv[rows, 0:HEAD_DIM]
-            value = kv[rows, HEAD_DIM : 2 * HEAD_DIM]
-            spread = query_stamps - stamps_ref[pl.ds(blk_ref[slot, entry], 1), :].astype(f32)
-            bias = half_bias(spread, low, narrow, bias_ref, power_ref)
-            half = nt_dot(query, key) * (0.5 * SCALE) + bias
-            prob_grad = nt_dot(grad, value)
-            th = jnp.tanh(half)
-            up = 1.0 + th
-            weights = (half * up * share).astype(bf16)
-            score_grad = prob_grad * (up * (1.0 + half * (1.0 - th))) * (0.5 * share)
-            rounded = score_grad.astype(bf16)
-            acc[at, 0] += nn_dot(query_t, rounded)
-            acc[at, 1] += nn_dot(grad_t, weights)
-            above = fold(score_grad)
-            before = low if narrow else 0
-            for c in steps_of(low, narrow):
-                reach = fold(jnp.where(spread >= power_ref[c], score_grad, 0.0))
-                bins_ref[before] += above - reach
-                above, before = reach, c
-            bins_ref[before] += above
-            return nn_dot(rounded, key)
-
-        def run(step, acc_q, narrow):
-            for j in range(BWD_GROUP):
-                entry = 1 + step * BWD_GROUP + j
-                valid = (entry < listed).astype(f32)
-                acc_q = acc_q + tile(jnp.minimum(entry, LIST_MAX - 1), inverse * valid, narrow)
-            return acc_q
+        def run(entries, shares, narrow):
+            keys, values = loaded(kv, pos_ref, slot, entries)
+            scores = nt_dot(query, keys) * (0.5 * SCALE)
+            prob_grads = nt_dot(grad, values)
+            weights, grads = [], []
+            for j, (entry, share) in enumerate(zip(entries, shares)):
+                low = low_ref[slot, entry]
+                spread = query_stamps - stamps_ref[pl.ds(blk_ref[slot, entry], 1), :].astype(f32)
+                bias = half_bias(spread, low, narrow, bias_ref, power_ref)
+                half = scores[:, j * BLOCK : (j + 1) * BLOCK] + bias
+                th = jnp.tanh(half)
+                up = 1.0 + th
+                weights.append((half * up * share).astype(bf16))
+                slope = up * (1.0 + half * (1.0 - th)) * (0.5 * share)
+                score_grad = prob_grads[:, j * BLOCK : (j + 1) * BLOCK] * slope
+                grads.append(score_grad.astype(bf16))
+                above = fold(score_grad)
+                before = low if narrow else 0
+                for c in steps_of(low, narrow):
+                    reach = fold(jnp.where(spread >= power_ref[c], score_grad, 0.0))
+                    bins_ref[before] += above - reach
+                    above, before = reach, c
+                bins_ref[before] += above
+            grads, weights = jnp.concatenate(grads, 1), jnp.concatenate(weights, 1)
+            key_grads, value_grads = nn_dot(query_t, grads), nn_dot(grad_t, weights)
+            for j, entry in enumerate(entries):
+                at = home_ref[slot, entry]
+                acc[at, 0] += key_grads[:, j * BLOCK : (j + 1) * BLOCK]
+                acc[at, 1] += value_grads[:, j * BLOCK : (j + 1) * BLOCK]
+            return nn_dot(grads, keys)
 
         def group(step, acc_q):
-            entries = [jnp.minimum(1 + step * BWD_GROUP + j, LIST_MAX - 1) for j in range(BWD_GROUP)]
-            return lax.cond(
+            entries, shares = members(step, BWD_GROUP, listed, inverse)
+            return acc_q + lax.cond(
                 all_narrow(width_ref, slot, entries),
-                lambda value: run(step, value, True),
-                lambda value: run(step, value, False),
-                acc_q,
+                lambda: run(entries, shares, True),
+                lambda: run(entries, shares, False),
             )
 
-        total = tile(0, jnp.where(causal(), inverse, 0.0), False)
+        total = run([0], [jnp.where(causal(), inverse, 0.0)], False)
         steps = (listed - 1 + BWD_GROUP - 1) // BWD_GROUP
         total = lax.fori_loop(0, steps, group, total)
         dq_ref[slot * BLOCK : (slot + 1) * BLOCK, :] = (total * SCALE).astype(bf16)
@@ -201,6 +208,54 @@
     other_ref[4 * TILES] = jnp.concatenate([high, low, rest], 0)
 
 
+def column(row):
+    return jnp.transpose(jnp.broadcast_to(row, (BLOCK, row.shape[1])))
+
+
+def norm_kernel(
+    sums_ref, attended_ref, gated_grad_ref, gate_ref, cot_ref, gated_ref, grad_u_ref, grad_ref, w_ref
+):
+    sums = jnp.sum(sums_ref[...], axis=0) * (1.0 / D)
+    mean, power, first, product = [column(sums[k : k + 1, :]) for k in range(4)]
+    inverse = lax.rsqrt(power - mean * mean + EPS)
+    second = inverse * (product - mean * first)
+    gate = gate_ref[...].astype(f32)
+    gated_grad = gated_grad_ref[...]
+    normed = (attended_ref[...] - mean) * inverse
+    gated = normed * gate
+    gated_ref[...] = gated.astype(bf16)
+    grad_u_ref[...] = (gated_grad * normed).astype(bf16)
+    grad_ref[...] = ((gated_grad * gate - first - normed * second) * inverse).astype(bf16)
+    gated_t = jnp.transpose(gated).astype(bf16)
+    for k in range(8):
+        w_ref[k] = nn_dot(gated_t, cot_ref[:, k * BLOCK : (k + 1) * BLOCK]).astype(bf16)
+
+
+def chip_kernel(own_ref, other_ref, weight_ref, bins_ref, out_ref):
+    split = TILES * HEAD_DIM
+    weight = jnp.sum(weight_ref[...].astype(f32), axis=0).astype(bf16)
+    tail = other_ref[4 * TILES].astype(f32)
+    bins = jnp.sum(bins_ref[0:BUCKETS], axis=1)
+    bins = bins + tail[0:BUCKETS] + tail[BUCKETS : 2 * BUCKETS]
+    high = bins.astype(bf16)
+    low = (bins - high.astype(f32)).astype(bf16)
+    for k in range(4):
+        for j in range(TILES):
+            tile = own_ref[k * TILES + j] + other_ref[k * TILES + j].astype(f32)
+            out_ref[k, j * HEAD_DIM : (j + 1) * HEAD_DIM] = tile.astype(bf16)
+        out_ref[k, split : split + HEAD_DIM] = weight
+        out_ref[k, split + HEAD_DIM : split + HEAD_DIM + BUCKETS] = high
+        out_ref[k, split + HEAD_DIM + BUCKETS : split + HEAD_DIM + 2 * BUCKETS] = low
+
+
+def project_kernel(back_ref, weight_ref, out_ref):
+    gated = jnp.concatenate([back_ref[h, :, 4 * HEAD_DIM :] for h in range(HEADS)], 1)
+    for k in range(8):
+        rows = [weight_ref[k, d, h] for h in range(HEADS) for d in range(4)]
+        product = nn_dot(gated, jnp.concatenate(rows, 0))
+        out_ref[:, k * BLOCK : (k + 1) * BLOCK] = product.astype(bf16)
+
+
 SMEM = functools.partial(pl.BlockSpec, memory_space=pltpu.SMEM)
 VMEM = functools.partial(pl.BlockSpec, memory_space=pltpu.VMEM)
 ANY = functools.partial(pl.BlockSpec, memory_space=pl.ANY)
@@ -216,7 +271,7 @@
             pltpu.VMEM((BLOCKS * BLOCK, 2 * HEAD_DIM), bf16),
             pltpu.SemaphoreType.DMA((PARTS,)),
         ],
-        compiler_params=pltpu.CompilerParams(vmem_limit_bytes=VMEM_LIMIT),
+        compiler_params=pltpu.CompilerParams(vmem_limit_bytes=12 * MIB),
         cost_estimate=pl.CostEstimate(
             flops=5 * 10**9, bytes_accessed=3 << 20, transcendentals=48 * BLOCK**2
         ),
@@ -240,7 +295,7 @@
             pltpu.VMEM((BLOCKS, 2, HEAD_DIM, BLOCK), f32),
             pltpu.SemaphoreType.DMA((PARTS,)),
         ],
-        compiler_params=pltpu.CompilerParams(vmem_limit_bytes=VMEM_LIMIT),
+        compiler_params=pltpu.CompilerParams(vmem_limit_bytes=24 * MIB),
         cost_estimate=pl.CostEstimate(
             flops=12 * 10**9, bytes_accessed=6 << 20, transcendentals=48 * BLOCK**2
         ),
@@ -248,6 +303,18 @@
     )(*tables, query, grad, *parts)
 
 
+def whole_call(kernel, out_shape, name, *args):
+    return pl.pallas_call(
+        kernel,
+        out_shape=out_shape,
+        in_specs=[VMEM()] * len(args),
+        out_specs=jax.tree.map(lambda _: VMEM(), out_shape),
+        compiler_params=pltpu.CompilerParams(vmem_limit_bytes=12 * MIB),
+        cost_estimate=pl.CostEstimate(flops=10**9, bytes_accessed=4 * MIB, transcendentals=0),
+        name=name,
+    )(*args)
+
+
 def exchange(values, axes):
     return lax.all_to_all(values, axes, split_axis=0, concat_axis=0, tiled=True)
 
@@ -279,11 +346,11 @@
 
 def halves(bias):
     high = lax.reduce_precision(bias, exponent_bits=8, mantissa_bits=7)
-    return jnp.pad(jnp.stack([high, bias - high]), ((0, 14), (0, BLOCK - BUCKETS)))
+    return jnp.concatenate([high, bias - high], 0)
 
 
 def whole(rows):
-    return rows[0, :BUCKETS] + rows[1, :BUCKETS]
+    return rows[:BUCKETS] + rows[BUCKETS:]
 
 
 def tables_of(lists, blk, pos, home, run, stamp_blocks, time_bias):
@@ -316,11 +383,10 @@
     rest = exchange(jnp.concatenate([by_head[:, :, 0], by_head[:, :, 3], rest], 2), "head")
     slabs = rest[:, :, 2 * HEAD_DIM + D :].reshape(HEADS * tokens, BLOCK)
     all_weight = lax.all_gather(slabs, ("x", "core", "dp"), axis=0, tiled=True)
-    all_weight = all_weight.reshape(8, 4, HEADS, tokens, BLOCK).transpose(0, 2, 1, 3, 4)
-    all_weight = all_weight.reshape(8, D, BLOCK)
+    all_weight = all_weight.reshape(8, 4, HEADS, tokens, BLOCK)
     rest = rest[:, :, : 2 * HEAD_DIM + D].reshape(2 * BLOCK, 2 * HEAD_DIM + D)
     query = rest[:, :HEAD_DIM]
-    gate = rest[:, HEAD_DIM : 2 * HEAD_DIM].astype(f32)
+    gate = rest[:, HEAD_DIM : 2 * HEAD_DIM]
     cot = rest[:, 2 * HEAD_DIM :]
     own_pairs = jnp.concatenate([pairs] + [shift_x(pairs, by) for by in SHIFTS], 0)
     parts = [own_pairs, swap_core(own_pairs)]
@@ -338,7 +404,7 @@
     attended = attend(tables, query, parts)
 
     gated_grad = nt_dot(cot, out_weight)
-    normed_grad = gated_grad * gate
+    normed_grad = gated_grad * gate.astype(f32)
     sums = jnp.stack(
         [
             jnp.sum(attended, 1),
@@ -347,36 +413,21 @@
             jnp.sum(normed_grad * attended, 1),
         ]
     )
-    sums = jnp.sum(to_all(sums, "head", HEADS).reshape(HEADS, 4, 2 * BLOCK), 0) / D
-    mean = sums[0]
-    inverse = lax.rsqrt(sums[1] - mean * mean + EPS)
-    first = sums[2]
-    second = inverse * (sums[3] - mean * sums[2])
-    normed = (attended - mean[:, None]) * inverse[:, None]
-    gated = (normed * gate).astype(bf16)
-    grad_u = (gated_grad * normed).astype(bf16)
-    attended_grad = (
-        (normed_grad - first[:, None] - normed * second[:, None]) * inverse[:, None]
-    ).astype(bf16)
-
-    weight_part = lax.dot_general(gated, cot, (((0,), (0,)), ((), ())), preferred_element_type=f32)
-    weight_part = weight_part.astype(bf16).reshape(HEAD_DIM, 8, BLOCK).transpose(1, 0, 2)
-    weight_part = exchange(weight_part, "dp").reshape(4, 2, HEAD_DIM, BLOCK)
+    sums = to_all(sums, "head", HEADS).reshape(HEADS, 4, 2 * BLOCK)
+    rows = jax.ShapeDtypeStruct((2 * BLOCK, HEAD_DIM), bf16)
+    tiles = jax.ShapeDtypeStruct((8, HEAD_DIM, BLOCK), bf16)
+    gated, grad_u, attended_grad, weight_part = whole_call(
+        norm_kernel, (rows, rows, rows, tiles), "norm", sums, attended, gated_grad, gate, cot
+    )
+    weight_part = exchange(weight_part, ("core", "dp"))
 
     own_grads, other_grads, grad_q, bins = attend_grads(tables, query, attended_grad, parts)
-    weight_part = jnp.sum(weight_part.astype(f32), 0)
-    sent = lax.dynamic_index_in_dim(weight_part, 1 - core, 0, True).astype(bf16)
-    theirs = swap_core(jnp.concatenate([other_grads, sent], 0)).astype(f32)
-    chip = (own_grads + theirs[: 4 * TILES]).reshape(4, TILES * HEAD_DIM, BLOCK)
-    weight_part = lax.dynamic_index_in_dim(weight_part, core, 0, False) + theirs[4 * TILES + 1]
-    bias_part = jnp.sum(theirs[4 * TILES, : 2 * BUCKETS], 1).reshape(2, BUCKETS).sum(0)
-    bias_part += jnp.sum(bins, (1, 2))[:BUCKETS]
-    side = jnp.concatenate([weight_part, halves(bias_part)], 0)
-    side = jnp.broadcast_to(side, (4,) + side.shape)
-    chip = jnp.concatenate([chip, side], 1).astype(bf16)
+    theirs = swap_core(other_grads)
+    split = TILES * HEAD_DIM
+    chip = jax.ShapeDtypeStruct((4, split + HEAD_DIM + 2 * BUCKETS, BLOCK), bf16)
+    chip = whole_call(chip_kernel, chip, "chip", own_grads, theirs, weight_part, bins)
     line = jnp.sum(exchange(chip, "x").reshape(chip.shape).astype(f32), 0)
 
-    split = TILES * HEAD_DIM
     pair = line[:split].reshape(2, split // 2, BLOCK)
     own_tiles = lax.dynamic_index_in_dim(pair, zh, 0, False)
     sent = lax.dynamic_index_in_dim(pair, 1 - zh, 0, False)
@@ -386,7 +437,7 @@
     own_tiles = own_tiles + theirs[: split // 2]
     theirs = theirs[split // 2 :]
     columns = weight_part.astype(bf16).astype(f32) + theirs[:HEAD_DIM]
-    bias_part = bias_part + whole(theirs[HEAD_DIM:])
+    bias_part = jnp.sum(bias_part + whole(theirs[HEAD_DIM:]), 1)
 
     for by in (1, 2):
         sent = jnp.pad(bias_part[None], ((0, 7), (0, columns.shape[1] - BUCKETS)))
@@ -394,10 +445,7 @@
         bias_part = bias_part + theirs[HEAD_DIM, :BUCKETS]
         columns = joined(columns, theirs[:HEAD_DIM], "dp", by)
     bias_grad = bias_part[None]
-    columns = columns.reshape(HEAD_DIM, 4, BLOCK)
-    theirs = swap_core(columns)
-    both = jnp.stack([jnp.where(core == 0, columns, theirs), jnp.where(core == 0, theirs, columns)])
-    weight_grad = both.transpose(1, 2, 0, 3).reshape(HEAD_DIM, D)
+    weight_grad = joined(columns, swap_core(columns), "core", 1)
 
     line = own_tiles.astype(bf16).reshape(2, 2, HEAD_DIM, BLOCK)
     line = line.transpose(0, 3, 1, 2).reshape(HEADS, tokens, 2 * HEAD_DIM)
@@ -410,9 +458,9 @@
     grad_u = rows[:, :, HEAD_DIM : 2 * HEAD_DIM]
     grads = jnp.stack([rows[:, :, :HEAD_DIM], grad_k, grad_v, grad_u], 0)
     input_grads = grads.transpose(2, 0, 1, 3).reshape(1, tokens, 4, D)
-    token_side = rows[:, :, 2 * HEAD_DIM :].transpose(1, 0, 2).reshape(tokens, D)
-    layer_out = jnp.concatenate([nn_dot(token_side, all_weight[k]) for k in range(8)], 1)
-    layer_out = layer_out.astype(bf16).reshape(1, tokens, D)
+    layer_out = jax.ShapeDtypeStruct((tokens, D), bf16)
+    layer_out = whole_call(project_kernel, layer_out, "project", back, all_weight)
+    layer_out = layer_out.reshape(1, tokens, D)
     return (layer_out, input_grads, weight_grad, bias_grad)
 
 

time: 227 us -> 217 us (0.956)
  starting transfers between devices: 115 us -> 90.4 us
  waiting for transfers between devices: 55.7 us -> 68.1 us
  blocking collectives: 0 us -> 11.3 us
  other arithmetic: 11.3 us -> 4.95 us
  Pallas kernels: 7.79 us -> 12.8 us
  local copies, waits for them, and re-layouts: 15.4 us -> 10.7 us
  matrix products: 3.15 us -> 0.45 us
    ppermute x3, starting transfers between devices: 28.3 us -> 12.5 us  [flip(): lax.ppermute(values, axis, [(i, i ^ by) for i in range(lax.axis_size(axis...]
    ppermute x3, waiting for transfers between devices: 8.01 us -> 21.6 us  [flip(): lax.ppermute(values, axis, [(i, i ^ by) for i in range(lax.axis_size(axis...]
    all_to_all x0 -> x1, blocking collectives: none -> 11.3 us  [exchange(): return lax.all_to_all(values, axes, split_axis=0, concat_axis=0, tiled=True)]
    all_to_all x6 -> x5, starting transfers between devices: 66.4 us -> 57.9 us  [exchange(): return lax.all_to_all(values, axes, split_axis=0, concat_axis=0, tiled=True)]
    convert_element_type x2 -> x0, other arithmetic: 3.14 us -> none  [the longest x1 1.66 us: body(): attended_grad = ((normed_grad - first[:, None] - normed * second[:, None]...]
    pallas_call x0 -> x3, Pallas kernels: none -> 2.81 us  [whole_call(): pl.pallas_call(kernel, out_shape=out_shape, in_specs=[VMEM()] * len(args)...]
    dot_general x9 -> x0, matrix products: 2.7 us -> none  [the longest x8 1.39 us: nn_dot(): lax.dot_general(a, b, (((1,), (0,)), ((), ())), preferred_element_type=f32)]
    all_to_all x6 -> x5, waiting for transfers between devices: 38.8 us -> 41.5 us  [exchange(): return lax.all_to_all(values, axes, split_axis=0, concat_axis=0, tiled=True)]
  transfers between devices with their start and end apart: 16 -> 15, of which waited for: 10 -> 9; matrix products, arithmetic and copies ran while one was open for 5% -> 5% of each run, Pallas kernels for 2% -> 0%
where the time goes in v3:
time: 217 us; the launch traced here: 213 us
  starting transfers between devices  90.4 us (42%)
  waiting for transfers between devices  68.1 us (31%)
  between operations  14.5 us (7%)
  Pallas kernels  12.8 us (6%)
  blocking collectives  11.3 us (5%)
  local copies, waits for them, and re-layouts  10.7 us (5%)
  other arithmetic  4.95 us (2%)
    all_to_all x5, starting transfers between devices, exchange(): return lax.all_to_all(values, axes, split_axis=0, concat_axis=0, tiled=True)  57.9 us
    all_to_all x5, waiting for transfers between devices, exchange(): return lax.all_to_all(values, axes, split_axis=0, concat_axis=0, tiled=True)  41.5 us
    ppermute x3, waiting for transfers between devices, flip(): lax.ppermute(values, axis, [(i, i ^ by) for i in range(lax.axis_size(axis...  21.6 us
    ppermute x3, starting transfers between devices, flip(): lax.ppermute(values, axis, [(i, i ^ by) for i in range(lax.axis_size(axis...  12.5 us
    all_to_all x1, blocking collectives, exchange(): return lax.all_to_all(values, axes, split_axis=0, concat_axis=0, tiled=True)  11.3 us
    ppermute x3, starting transfers between devices, swap_core(): return lax.ppermute(values, 'core', [(0, 1), (1, 0)])  10.1 us
    ppermute x3, starting transfers between devices, shift_x(): return lax.ppermute(values, 'x', [(i, (i + by) % 4) for i in range(4)])  9.93 us
    pallas_call x1, Pallas kernels, attend_grads(): pl.pallas_call(grads_kernel, out_shape=(jax.ShapeDtypeStruct((4 * TILES,...  6.75 us
  transfers between devices with their start and end apart: 15, of which 9 were waited for; matrix products, arithmetic and copies ran while one was open for 5% of the time, Pallas kernels for 0%

profile of v3, /device:TPU:1, one launch (start us, length us, event | category | flops | bytes accessed | tf_op | source)
XLA Modules:
  0.0 213.3 jit_solution(710218007255830420)
XLA Ops:
  9.2 15.7 %all-to-all-start.1 = ((bf16[16,32,256]{2,1,0:T(8,128)(2,1)}), bf16[16,32,256]{2,1,0:T(8,128)(2,1)S(1)}, u32[]{:S(2)}, u32[]{:S(2)}) async-start(bf16[16,32,256]{2,1,0:T(8,128)(2,1)} %pad_maximum_fusion.4), calls=%async_computation.1 | async-start | bytes 524288 | tf_op jit(solution)/shard_map/all_to_all | solution.py:319
  26.0 12.0 %all-to-all-done.1 = bf16[16,32,256]{2,1,0:T(8,128)(2,1)S(1)} async-done(((bf16[16,32,256]{2,1,0:T(8,128)(2,1)}), bf16[16,32,256]{2,1,0:T(8,128)(2,1)S(1)}, u32[]{:S(2)}, u32[]{:S(2)}) %all-to-all-start.1) | async-done | bytes 262176 | tf_op jit(solution)/shard_map/all_to_all | solution.py:319
  38.0 10.8 %all-to-all-start = ((bf16[8,32,1408]{2,1,0:T(8,128)(2,1)}), bf16[8,32,1408]{2,1,0:T(8,128)(2,1)}, u32[]{:S(2)}, u32[]{:S(2)}) async-start(bf16[8,32,1408]{2,1,0:T(8,128)(2,1)} %pad_maximum_fusion.1), calls=%async_computation | async-start | bytes 1441792 | tf_op jit(solution)/shard_map/all_to_all | solution.py:319
  49.6 3.1 %collective-permute-start = (bf16[512,256]{1,0:T(8,128)(2,1)S(1)}, bf16[512,256]{1,0:T(8,128)(2,1)S(1)}, u32[]{:S(2)}, u32[]{:S(2)}) collective-permute-start(bf16[512,256]{1,0:T(8,128)(2,1)S(1)} %bitcast.78), channel_id=1, source_target_pairs={{0,32},{32,64},{64,96},{96,0},{1,33},{33,65},{65,97},{97,1},{2,34}... | collective-permute-start | bytes 786440 | tf_op jit(solution)/shard_map/ppermute | solution.py:331
  52.8 3.4 %collective-permute-start.1 = (bf16[512,256]{1,0:T(8,128)(2,1)S(1)}, bf16[512,256]{1,0:T(8,128)(2,1)S(1)}, u32[]{:S(2)}, u32[]{:S(2)}) collective-permute-start(bf16[512,256]{1,0:T(8,128)(2,1)S(1)} %bitcast.79), channel_id=1, source_target_pairs={{0,96},{32,0},{64,32},{96,64},{1,97},{33,1},{65,33},{97,65},{2,98}... | collective-permute-start | bytes 786440 | tf_op jit(solution)/shard_map/ppermute | solution.py:331
  56.1 3.4 %collective-permute-start.2 = (bf16[512,256]{1,0:T(8,128)(2,1)S(1)}, bf16[512,256]{1,0:T(8,128)(2,1)S(1)}, u32[]{:S(2)}, u32[]{:S(2)}) collective-permute-start(bf16[512,256]{1,0:T(8,128)(2,1)S(1)} %bitcast.80), channel_id=1, source_target_pairs={{0,64},{32,96},{64,0},{96,32},{1,65},{33,97},{65,1},{97,33},{2,66}... | collective-permute-start | bytes 786440 | tf_op jit(solution)/shard_map/ppermute | solution.py:331
  61.4 4.4 %collective-permute-done.2 = bf16[512,256]{1,0:T(8,128)(2,1)S(1)} collective-permute-done((bf16[512,256]{1,0:T(8,128)(2,1)S(1)}, bf16[512,256]{1,0:T(8,128)(2,1)S(1)}, u32[]{:S(2)}, u32[]{:S(2)}) %collective-permute-start.2) | collective-permute-done | bytes 262176 | tf_op jit(solution)/shard_map/ppermute | solution.py:331
  65.9 4.3 %collective-permute-start.3 = (bf16[2048,256]{1,0:T(8,128)(2,1)S(1)}, bf16[2048,256]{1,0:T(8,128)(2,1)S(1)}, u32[]{:S(2)}, u32[]{:S(2)}) collective-permute-start(bf16[2048,256]{1,0:T(8,128)(2,1)S(1)} %pad_maximum_fusion.refs_0_), channel_id=1, source_target_pairs={{0,8},{8,0},{1,9},{9,1},{2,10},{10,2},{3,11},{11,3},{4,12},{12,4},... | collective-permute-start | bytes 3145736 | tf_op jit(solution)/shard_map/ppermute | solution.py:327
  70.6 4.9 %all-to-all-done = bf16[8,32,1408]{2,1,0:T(8,128)(2,1)} async-done(((bf16[8,32,1408]{2,1,0:T(8,128)(2,1)}), bf16[8,32,1408]{2,1,0:T(8,128)(2,1)}, u32[]{:S(2)}, u32[]{:S(2)}) %all-to-all-start) | async-done | bytes 720928 | tf_op jit(solution)/shard_map/all_to_all | solution.py:319
  76.7 3.3 %attend.1.attended_ref = f32[256,128]{1,0:T(8,128)S(1)} custom-call(s32[2,24]{1,0:T(2,128)S(1)} %multiply_add_fusion.1.pos_ref, s32[2,24]{1,0:T(2,128)S(1)} %get-tuple-element.42.home_ref, s32[2,24]{1,0:T(2,128)S(1)} %get-tuple-element.60.blk_ref, s32[2,24]{1,0:T(2,128)S(1)} %get-tuple-element.41.low_ref, s32[2,24]{1,0:T(2,128)S(1)} %sub.66.width_ref, ...), custom_call_target="tpu_custom_call" | custom-call | flops 5000000000 | bytes 3145728 | tf_op jit(solution)/shard_map/attend/pallas_call | solution.py:265
  81.1 14.7 %all-to-all-start.2 = ((f32[8,4,256]{2,1,0:T(4,128)}), f32[8,4,256]{2,1,0:T(4,128)S(1)}, u32[]{:S(2)}, u32[]{:S(2)}) async-start(f32[8,4,256]{2,1,0:T(4,128)} %broadcast_in_dim.14), calls=%async_computation.2 | async-start | bytes 65536 | tf_op jit(solution)/shard_map/all_to_all | solution.py:319
  96.9 8.4 %all-to-all-done.2.sums_ref = f32[8,4,256]{2,1,0:T(4,128)S(1)} async-done(((f32[8,4,256]{2,1,0:T(4,128)}), f32[8,4,256]{2,1,0:T(4,128)S(1)}, u32[]{:S(2)}, u32[]{:S(2)}) %all-to-all-start.2) | async-done | bytes 32800 | tf_op jit(solution)/shard_map/all_to_all | solution.py:319
  105.8 6.7 %attend_grads.1 = (f32[32,128,128]{2,1,0:T(8,128)S(1)}, bf16[33,128,128]{2,1,0:T(8,128)(2,1)S(1)}, bf16[256,128]{1,0:T(8,128)(2,1)S(1)}, f32[17,8,128]{2,1,0:T(8,128)S(1)}) custom-call(s32[2,24]{1,0:T(2,128)S(1)} %multiply_add_fusion.1.pos_ref, s32[2,24]{1,0:T(2,128)S(1)} %get-tuple-element.42.home_ref, s32[2,24]{1,0:T(2,128)S(1)} %get-tuple-element.60.blk_ref, ...), custom_call_target="tpu_custom_call" | custom-call | flops 12000000000 | bytes 6291456 | tf_op jit(solution)/shard_map/attend_grads/pallas_call | solution.py:283
  112.6 1.9 collective-permute-start.4
  114.5 11.3 %all_to_all.30.weight_ref = bf16[8,128,128]{2,1,0:T(8,128)(2,1)S(1)} all-to-all(bf16[8,128,128]{2,1,0:T(8,128)(2,1)S(1)} %get-tuple-element.15), channel_id=1, replica_groups=mesh['dp'=4,'x'=4,'zh'=2,'core'=2,'head'=8] {'core','dp'}, dimensions={0} | all-to-all | bytes 524288 | tf_op jit(solution)/shard_map/all_to_all | solution.py:319
  127.1 10.3 %all-to-all-start.4 = ((bf16[4,1184,128]{2,1,0:T(8,128)(2,1)}), bf16[4,1184,128]{2,1,0:T(8,128)(2,1)S(1)}, u32[]{:S(2)}, u32[]{:S(2)}) async-start(bf16[4,1184,128]{2,1,0:T(8,128)(2,1)} %chip.1), calls=%async_computation.4 | async-start | bytes 2424832 | tf_op jit(solution)/shard_map/all_to_all | solution.py:319
  138.9 14.8 %all-to-all-done.4 = bf16[4,1184,128]{2,1,0:T(8,128)(2,1)S(1)} async-done(((bf16[4,1184,128]{2,1,0:T(8,128)(2,1)}), bf16[4,1184,128]{2,1,0:T(8,128)(2,1)S(1)}, u32[]{:S(2)}, u32[]{:S(2)}) %all-to-all-start.4) | async-done | bytes 1212448 | tf_op jit(solution)/shard_map/all_to_all | solution.py:319
  154.0 7.4 %collective-permute-start.5 = (bf16[672,128]{1,0:T(8,128)(2,1)S(1)}, bf16[672,128]{1,0:T(8,128)(2,1)S(1)}, u32[]{:S(2)}, u32[]{:S(2)}) collective-permute-start(bf16[672,128]{1,0:T(8,128)(2,1)S(1)} %pad_maximum_fusion.7), channel_id=1, source_target_pairs={{0,16},{16,0},{1,17},{17,1},{2,18},{18,2},{3,19},{19,3},{4,20},{20... | collective-permute-start | bytes 516104 | tf_op jit(solution)/shard_map/ppermute | solution.py:335
  161.4 15.8 %collective-permute-done.5 = bf16[672,128]{1,0:T(8,128)(2,1)S(1)} collective-permute-done((bf16[672,128]{1,0:T(8,128)(2,1)S(1)}, bf16[672,128]{1,0:T(8,128)(2,1)S(1)}, u32[]{:S(2)}, u32[]{:S(2)}) %collective-permute-start.5) | collective-permute-done | bytes 172064 | tf_op jit(solution)/shard_map/ppermute | solution.py:335
  177.4 2.5 %collective-permute-start.6 = (f32[136,128]{1,0:T(8,128)S(1)}, f32[136,128]{1,0:T(8,128)S(1)}, u32[]{:S(2)}, u32[]{:S(2)}) collective-permute-start(f32[136,128]{1,0:T(8,128)S(1)} %select_maximum_fusion.1), channel_id=1, source_target_pairs={{0,128},{128,0},{256,384},{384,256},{1,129},{129,1},{257,385},{385... | collective-permute-start | bytes 208904 | tf_op jit(solution)/shard_map/ppermute | solution.py:335
  180.9 6.2 %all-to-all-start.5 = ((bf16[8,32,640]{2,1,0:T(8,128)(2,1)}), bf16[8,32,640]{2,1,0:T(8,128)(2,1)S(1)}, u32[]{:S(2)}, u32[]{:S(2)}) async-start(bf16[8,32,640]{2,1,0:T(8,128)(2,1)} %pad_maximum_fusion.3), calls=%async_computation.5 | async-start | bytes 655360 | tf_op jit(solution)/shard_map/all_to_all | solution.py:319
  187.2 2.6 %collective-permute-start.7 = (f32[136,256]{1,0:T(8,128)S(1)}, f32[136,256]{1,0:T(8,128)S(1)}, u32[]{:S(2)}, u32[]{:S(2)}) collective-permute-start(f32[136,256]{1,0:T(8,128)S(1)} %select_maximum_fusion), channel_id=1, source_target_pairs={{0,256},{128,384},{256,0},{384,128},{1,257},{129,385},{257,1},{385... | collective-permute-start | bytes 417800 | tf_op jit(solution)/shard_map/ppermute | solution.py:335
  189.8 5.8 %collective-permute-done.7 = f32[136,256]{1,0:T(8,128)S(1)} collective-permute-done((f32[136,256]{1,0:T(8,128)S(1)}, f32[136,256]{1,0:T(8,128)S(1)}, u32[]{:S(2)}, u32[]{:S(2)}) %collective-permute-start.7) | collective-permute-done | bytes 139296 | tf_op jit(solution)/shard_map/ppermute | solution.py:335
  195.7 3.8 %collective-permute-start.8 = (f32[128,512]{1,0:T(8,128)S(1)}, f32[128,512]{1,0:T(8,128)S(1)}, u32[]{:S(2)}, u32[]{:S(2)}) collective-permute-start(f32[128,512]{1,0:T(8,128)S(1)} %pad_maximum_fusion.5), channel_id=1, source_target_pairs={{0,8},{8,0},{1,9},{9,1},{2,10},{10,2},{3,11},{11,3},{4,12},{12,4},... | collective-permute-start | bytes 786440 | tf_op jit(solution)/shard_map/ppermute | solution.py:327
  (92 shorter events, 20.9 us)
Async XLA Ops:
  7.2 41.7 %copy-start = (s32[1,32,24]{1,2,0:T(8,128)S(1)}, s32[1,32,24]{1,2,0:T(8,128)}, u32[]{:S(2)}) copy-start(s32[1,32,24]{1,2,0:T(8,128)} %param.10) | copy-start | bytes 9220
  7.2 17.8 %copy-start.5 = (bf16[128,1024]{1,0:T(8,128)(2,1)S(1)}, bf16[128,1024]{1,0:T(8,128)(2,1)}, u32[]{:S(2)}) copy-start(bf16[128,1024]{1,0:T(8,128)(2,1)} %param.8) | copy-start | bytes 786436
  7.2 17.8 %copy-start.4 = (bf16[1,32,1024]{2,1,0:T(8,128)(2,1)S(1)}, bf16[1,32,1024]{2,1,0:T(8,128)(2,1)}, u32[]{:S(2)}) copy-start(bf16[1,32,1024]{2,1,0:T(8,128)(2,1)} %param.7) | copy-start | bytes 196612
  9.2 28.9 %all-to-all-start.1 = ((bf16[16,32,256]{2,1,0:T(8,128)(2,1)}), bf16[16,32,256]{2,1,0:T(8,128)(2,1)S(1)}, u32[]{:S(2)}, u32[]{:S(2)}) async-start(bf16[16,32,256]{2,1,0:T(8,128)(2,1)} %pad_maximum_fusion.4), calls=%async_computation.1 | async-start | bytes 524288 | tf_op jit(solution)/shard_map/all_to_all | solution.py:319
  24.9 24.3 %copy-start.1 = (s32[1,4096]{1,0:T(1,128)S(1)}, s32[1,4096]{1,0:T(1,128)}, u32[]{:S(2)}) copy-start(s32[1,4096]{1,0:T(1,128)} %param.11) | copy-start | bytes 49156
  38.0 37.5 %all-to-all-start = ((bf16[8,32,1408]{2,1,0:T(8,128)(2,1)}), bf16[8,32,1408]{2,1,0:T(8,128)(2,1)}, u32[]{:S(2)}, u32[]{:S(2)}) async-start(bf16[8,32,1408]{2,1,0:T(8,128)(2,1)} %pad_maximum_fusion.1), calls=%async_computation | async-start | bytes 1441792 | tf_op jit(solution)/shard_map/all_to_all | solution.py:319
  49.6 11.8 %collective-permute-start = (bf16[512,256]{1,0:T(8,128)(2,1)S(1)}, bf16[512,256]{1,0:T(8,128)(2,1)S(1)}, u32[]{:S(2)}, u32[]{:S(2)}) collective-permute-start(bf16[512,256]{1,0:T(8,128)(2,1)S(1)} %bitcast.78), channel_id=1, source_target_pairs={{0,32},{32,64},{64,96},{96,0},{1,33},{33,65},{65,97},{97,1},{2,34}... | collective-permute-start | bytes 786440 | tf_op jit(solution)/shard_map/ppermute | solution.py:331
  52.8 8.7 %collective-permute-start.1 = (bf16[512,256]{1,0:T(8,128)(2,1)S(1)}, bf16[512,256]{1,0:T(8,128)(2,1)S(1)}, u32[]{:S(2)}, u32[]{:S(2)}) collective-permute-start(bf16[512,256]{1,0:T(8,128)(2,1)S(1)} %bitcast.79), channel_id=1, source_target_pairs={{0,96},{32,0},{64,32},{96,64},{1,97},{33,1},{65,33},{97,65},{2,98}... | collective-permute-start | bytes 786440 | tf_op jit(solution)/shard_map/ppermute | solution.py:331
  56.1 9.7 %collective-permute-start.2 = (bf16[512,256]{1,0:T(8,128)(2,1)S(1)}, bf16[512,256]{1,0:T(8,128)(2,1)S(1)}, u32[]{:S(2)}, u32[]{:S(2)}) collective-permute-start(bf16[512,256]{1,0:T(8,128)(2,1)S(1)} %bitcast.80), channel_id=1, source_target_pairs={{0,64},{32,96},{64,0},{96,32},{1,65},{33,97},{65,1},{97,33},{2,66}... | collective-permute-start | bytes 786440 | tf_op jit(solution)/shard_map/ppermute | solution.py:331
  59.6 10.9 %copy-start.6 = (f32[1,16]{1,0:T(1,128)S(1)}, f32[1,16]{1,0:T(1,128)}, u32[]{:S(2)}) copy-start(f32[1,16]{1,0:T(1,128)} %param.9) | copy-start | bytes 196
  65.9 10.7 %collective-permute-start.3 = (bf16[2048,256]{1,0:T(8,128)(2,1)S(1)}, bf16[2048,256]{1,0:T(8,128)(2,1)S(1)}, u32[]{:S(2)}, u32[]{:S(2)}) collective-permute-start(bf16[2048,256]{1,0:T(8,128)(2,1)S(1)} %pad_maximum_fusion.refs_0_), channel_id=1, source_target_pairs={{0,8},{8,0},{1,9},{9,1},{2,10},{10,2},{3,11},{11,3},{4,12},{12,4},... | collective-permute-start | bytes 3145736 | tf_op jit(solution)/shard_map/ppermute | solution.py:327
  76.6 3.3 %copy-start.3 = (bf16[8,32,1280]{2,1,0:T(8,128)(2,1)}, bf16[8,32,1280]{2,1,0:T(8,128)(2,1)S(1)}, u32[]{:S(2)}) copy-start(bf16[8,32,1280]{2,1,0:T(8,128)(2,1)S(1)} %slice.146) | copy-start | bytes 1966084
  81.1 24.2 %all-to-all-start.2 = ((f32[8,4,256]{2,1,0:T(4,128)}), f32[8,4,256]{2,1,0:T(4,128)S(1)}, u32[]{:S(2)}, u32[]{:S(2)}) async-start(f32[8,4,256]{2,1,0:T(4,128)} %broadcast_in_dim.14), calls=%async_computation.2 | async-start | bytes 65536 | tf_op jit(solution)/shard_map/all_to_all | solution.py:319
  112.6 13.3 %collective-permute-start.4 = (bf16[33,128,128]{2,1,0:T(8,128)(2,1)S(1)}, bf16[33,128,128]{2,1,0:T(8,128)(2,1)S(1)}, u32[]{:S(2)}, u32[]{:S(2)}) collective-permute-start(bf16[33,128,128]{2,1,0:T(8,128)(2,1)S(1)} %get-tuple-element.14), channel_id=1, source_target_pairs={{0,8},{8,0},{1,9},{9,1},{2,10},{10,2},{3,11},{11,3},{4,12},{12,4},... | collective-permute-start | bytes 3244040 | tf_op jit(solution)/shard_map/ppermute | solution.py:327
  127.1 26.6 %all-to-all-start.4 = ((bf16[4,1184,128]{2,1,0:T(8,128)(2,1)}), bf16[4,1184,128]{2,1,0:T(8,128)(2,1)S(1)}, u32[]{:S(2)}, u32[]{:S(2)}) async-start(bf16[4,1184,128]{2,1,0:T(8,128)(2,1)} %chip.1), calls=%async_computation.4 | async-start | bytes 2424832 | tf_op jit(solution)/shard_map/all_to_all | solution.py:319
  137.4 66.4 %all-gather.2.cloned.1.call-start = ((), (), s32[]{:S(2)}) async-start(), calls=%async_computation.6 | async-start | bytes 2162688 | tf_op jit(solution)/shard_map/all_gather | solution.py:385
  154.0 23.2 %collective-permute-start.5 = (bf16[672,128]{1,0:T(8,128)(2,1)S(1)}, bf16[672,128]{1,0:T(8,128)(2,1)S(1)}, u32[]{:S(2)}, u32[]{:S(2)}) collective-permute-start(bf16[672,128]{1,0:T(8,128)(2,1)S(1)} %pad_maximum_fusion.7), channel_id=1, source_target_pairs={{0,16},{16,0},{1,17},{17,1},{2,18},{18,2},{3,19},{19,3},{4,20},{20... | collective-permute-start | bytes 516104 | tf_op jit(solution)/shard_map/ppermute | solution.py:335
  177.4 9.8 %collective-permute-start.6 = (f32[136,128]{1,0:T(8,128)S(1)}, f32[136,128]{1,0:T(8,128)S(1)}, u32[]{:S(2)}, u32[]{:S(2)}) collective-permute-start(f32[136,128]{1,0:T(8,128)S(1)} %select_maximum_fusion.1), channel_id=1, source_target_pairs={{0,128},{128,0},{256,384},{384,256},{1,129},{129,1},{257,385},{385... | collective-permute-start | bytes 208904 | tf_op jit(solution)/shard_map/ppermute | solution.py:335
  180.9 21.9 %all-to-all-start.5 = ((bf16[8,32,640]{2,1,0:T(8,128)(2,1)}), bf16[8,32,640]{2,1,0:T(8,128)(2,1)S(1)}, u32[]{:S(2)}, u32[]{:S(2)}) async-start(bf16[8,32,640]{2,1,0:T(8,128)(2,1)} %pad_maximum_fusion.3), calls=%async_computation.5 | async-start | bytes 655360 | tf_op jit(solution)/shard_map/all_to_all | solution.py:319
  187.2 8.4 %collective-permute-start.7 = (f32[136,256]{1,0:T(8,128)S(1)}, f32[136,256]{1,0:T(8,128)S(1)}, u32[]{:S(2)}, u32[]{:S(2)}) collective-permute-start(f32[136,256]{1,0:T(8,128)S(1)} %select_maximum_fusion), channel_id=1, source_target_pairs={{0,256},{128,384},{256,0},{384,128},{1,257},{129,385},{257,1},{385... | collective-permute-start | bytes 417800 | tf_op jit(solution)/shard_map/ppermute | solution.py:335
  195.7 5.0 %collective-permute-start.8 = (f32[128,512]{1,0:T(8,128)S(1)}, f32[128,512]{1,0:T(8,128)S(1)}, u32[]{:S(2)}, u32[]{:S(2)}) collective-permute-start(f32[128,512]{1,0:T(8,128)S(1)} %pad_maximum_fusion.5), channel_id=1, source_target_pairs={{0,8},{8,0},{1,9},{9,1},{2,10},{10,2},{3,11},{11,3},{4,12},{12,4},... | collective-permute-start | bytes 786440 | tf_op jit(solution)/shard_map/ppermute | solution.py:327
  203.9 1.6 copy-start.2
Sparse Core Ops, SparseCore 0:
  141.9 56.0 all-gather.1

commit v4 on v3

--- a/solution.py
+++ b/solution.py
@@ -384,10 +384,9 @@
     slabs = rest[:, :, 2 * HEAD_DIM + D :].reshape(HEADS * tokens, BLOCK)
     all_weight = lax.all_gather(slabs, ("x", "core", "dp"), axis=0, tiled=True)
     all_weight = all_weight.reshape(8, 4, HEADS, tokens, BLOCK)
-    rest = rest[:, :, : 2 * HEAD_DIM + D].reshape(2 * BLOCK, 2 * HEAD_DIM + D)
-    query = rest[:, :HEAD_DIM]
-    gate = rest[:, HEAD_DIM : 2 * HEAD_DIM]
-    cot = rest[:, 2 * HEAD_DIM :]
+    query = rest[:, :, :HEAD_DIM].reshape(2 * BLOCK, HEAD_DIM)
+    gate = rest[:, :, HEAD_DIM : 2 * HEAD_DIM].reshape(2 * BLOCK, HEAD_DIM)
+    cot = rest[:, :, 2 * HEAD_DIM : 2 * HEAD_DIM + D].reshape(2 * BLOCK, D)
     own_pairs = jnp.concatenate([pairs] + [shift_x(pairs, by) for by in SHIFTS], 0)
     parts = [own_pairs, swap_core(own_pairs)]
 

time: 217 us -> 212 us (0.977)
  blocking collectives: 11.3 us -> 35.4 us
  starting transfers between devices: 90.4 us -> 71.2 us
  waiting for transfers between devices: 68.1 us -> 62.4 us
  local copies, waits for them, and re-layouts: 10.7 us -> 7.15 us
    all_to_all x1 -> x2, blocking collectives: 11.3 us -> 35.4 us  [exchange(): return lax.all_to_all(values, axes, split_axis=0, concat_axis=0, tiled=True)]
    all_to_all x5 -> x4, starting transfers between devices: 57.9 us -> 40.5 us  [exchange(): return lax.all_to_all(values, axes, split_axis=0, concat_axis=0, tiled=True)]
    all_to_all x5 -> x4, waiting for transfers between devices: 41.5 us -> 34.1 us  [exchange(): return lax.all_to_all(values, axes, split_axis=0, concat_axis=0, tiled=True)]
  transfers between devices with their start and end apart: 15 -> 14, of which waited for: 9 -> 8; matrix products, arithmetic and copies ran while one was open for 5% -> 4% of each run, Pallas kernels for 0% -> 0%
where the time goes in v4:
time: 212 us; the launch traced here: 209 us
  starting transfers between devices  71.2 us (34%)
  waiting for transfers between devices  62.4 us (29%)
  blocking collectives  35.4 us (17%)
  between operations  14.5 us (7%)
  Pallas kernels  12.8 us (6%)
  local copies, waits for them, and re-layouts  7.15 us (3%)
  other arithmetic  4.92 us (2%)
    all_to_all x4, starting transfers between devices, exchange(): return lax.all_to_all(values, axes, split_axis=0, concat_axis=0, tiled=True)  40.5 us
    all_to_all x2, blocking collectives, exchange(): return lax.all_to_all(values, axes, split_axis=0, concat_axis=0, tiled=True)  35.4 us
    all_to_all x4, waiting for transfers between devices, exchange(): return lax.all_to_all(values, axes, split_axis=0, concat_axis=0, tiled=True)  34.1 us
    ppermute x3, waiting for transfers between devices, flip(): lax.ppermute(values, axis, [(i, i ^ by) for i in range(lax.axis_size(axis...  22.7 us
    ppermute x3, starting transfers between devices, flip(): lax.ppermute(values, axis, [(i, i ^ by) for i in range(lax.axis_size(axis...  11 us
    ppermute x3, starting transfers between devices, shift_x(): return lax.ppermute(values, 'x', [(i, (i + by) % 4) for i in range(4)])  9.93 us
    ppermute x3, starting transfers between devices, swap_core(): return lax.ppermute(values, 'core', [(0, 1), (1, 0)])  9.71 us
    pallas_call x1, Pallas kernels, attend_grads(): pl.pallas_call(grads_kernel, out_shape=(jax.ShapeDtypeStruct((4 * TILES,...  6.72 us
  transfers between devices with their start and end apart: 14, of which 8 were waited for; matrix products, arithmetic and copies ran while one was open for 4% of the time, Pallas kernels for 0%

profile of v4, /device:TPU:1, one launch (start us, length us, event | category | flops | bytes accessed | tf_op | source)
XLA Modules:
  0.0 208.8 jit_solution(4770995908618598950)
XLA Ops:
  9.2 15.7 %all-to-all-start.1 = ((bf16[16,32,256]{2,1,0:T(8,128)(2,1)}), bf16[16,32,256]{2,1,0:T(8,128)(2,1)S(1)}, u32[]{:S(2)}, u32[]{:S(2)}) async-start(bf16[16,32,256]{2,1,0:T(8,128)(2,1)} %pad_maximum_fusion.4), calls=%async_computation.1 | async-start | bytes 524288 | tf_op jit(solution)/shard_map/all_to_all | solution.py:319
  26.0 12.1 %all-to-all-done.1 = bf16[16,32,256]{2,1,0:T(8,128)(2,1)S(1)} async-done(((bf16[16,32,256]{2,1,0:T(8,128)(2,1)}), bf16[16,32,256]{2,1,0:T(8,128)(2,1)S(1)}, u32[]{:S(2)}, u32[]{:S(2)}) %all-to-all-start.1) | async-done | bytes 262176 | tf_op jit(solution)/shard_map/all_to_all | solution.py:319
  38.0 10.8 %all-to-all-start = ((bf16[8,32,1408]{2,1,0:T(8,128)(2,1)}), bf16[8,32,1408]{2,1,0:T(8,128)(2,1)S(1)}, u32[]{:S(2)}, u32[]{:S(2)}) async-start(bf16[8,32,1408]{2,1,0:T(8,128)(2,1)} %pad_maximum_fusion.1), calls=%async_computation | async-start | bytes 1441792 | tf_op jit(solution)/shard_map/all_to_all | solution.py:319
  49.6 3.1 %collective-permute-start = (bf16[512,256]{1,0:T(8,128)(2,1)S(1)}, bf16[512,256]{1,0:T(8,128)(2,1)S(1)}, u32[]{:S(2)}, u32[]{:S(2)}) collective-permute-start(bf16[512,256]{1,0:T(8,128)(2,1)S(1)} %bitcast.85), channel_id=1, source_target_pairs={{0,32},{32,64},{64,96},{96,0},{1,33},{33,65},{65,97},{97,1},{2,34}... | collective-permute-start | bytes 786440 | tf_op jit(solution)/shard_map/ppermute | solution.py:331
  52.8 3.4 %collective-permute-start.1 = (bf16[512,256]{1,0:T(8,128)(2,1)S(1)}, bf16[512,256]{1,0:T(8,128)(2,1)S(1)}, u32[]{:S(2)}, u32[]{:S(2)}) collective-permute-start(bf16[512,256]{1,0:T(8,128)(2,1)S(1)} %bitcast.86), channel_id=1, source_target_pairs={{0,96},{32,0},{64,32},{96,64},{1,97},{33,1},{65,33},{97,65},{2,98}... | collective-permute-start | bytes 786440 | tf_op jit(solution)/shard_map/ppermute | solution.py:331
  56.1 3.4 %collective-permute-start.2 = (bf16[512,256]{1,0:T(8,128)(2,1)S(1)}, bf16[512,256]{1,0:T(8,128)(2,1)S(1)}, u32[]{:S(2)}, u32[]{:S(2)}) collective-permute-start(bf16[512,256]{1,0:T(8,128)(2,1)S(1)} %bitcast.87), channel_id=1, source_target_pairs={{0,64},{32,96},{64,0},{96,32},{1,65},{33,97},{65,1},{97,33},{2,66}... | collective-permute-start | bytes 786440 | tf_op jit(solution)/shard_map/ppermute | solution.py:331
  61.4 4.3 %collective-permute-done.2 = bf16[512,256]{1,0:T(8,128)(2,1)S(1)} collective-permute-done((bf16[512,256]{1,0:T(8,128)(2,1)S(1)}, bf16[512,256]{1,0:T(8,128)(2,1)S(1)}, u32[]{:S(2)}, u32[]{:S(2)}) %collective-permute-start.2) | collective-permute-done | bytes 262176 | tf_op jit(solution)/shard_map/ppermute | solution.py:331
  65.8 4.4 %collective-permute-start.3 = (bf16[2048,256]{1,0:T(8,128)(2,1)S(1)}, bf16[2048,256]{1,0:T(8,128)(2,1)S(1)}, u32[]{:S(2)}, u32[]{:S(2)}) collective-permute-start(bf16[2048,256]{1,0:T(8,128)(2,1)S(1)} %pad_maximum_fusion.refs_0_), channel_id=1, source_target_pairs={{0,8},{8,0},{1,9},{9,1},{2,10},{10,2},{3,11},{11,3},{4,12},{12,4},... | collective-permute-start | bytes 3145736 | tf_op jit(solution)/shard_map/ppermute | solution.py:327
  70.6 4.8 %all-to-all-done = bf16[8,32,1408]{2,1,0:T(8,128)(2,1)S(1)} async-done(((bf16[8,32,1408]{2,1,0:T(8,128)(2,1)}), bf16[8,32,1408]{2,1,0:T(8,128)(2,1)S(1)}, u32[]{:S(2)}, u32[]{:S(2)}) %all-to-all-start) | async-done | bytes 720928 | tf_op jit(solution)/shard_map/all_to_all | solution.py:319
  76.1 3.3 %attend.1.attended_ref = f32[256,128]{1,0:T(8,128)S(1)} custom-call(s32[2,24]{1,0:T(2,128)S(1)} %multiply_add_fusion.1.pos_ref, s32[2,24]{1,0:T(2,128)S(1)} %get-tuple-element.42.home_ref, s32[2,24]{1,0:T(2,128)S(1)} %get-tuple-element.61.blk_ref, s32[2,24]{1,0:T(2,128)S(1)} %get-tuple-element.41.low_ref, s32[2,24]{1,0:T(2,128)S(1)} %sub.66.width_ref, ...), custom_call_target="tpu_custom_call" | custom-call | flops 5000000000 | bytes 3145728 | tf_op jit(solution)/shard_map/attend/pallas_call | solution.py:265
  79.9 24.0 %all_to_all.30.sums_ref = f32[8,4,256]{2,1,0:T(4,128)S(1)} all-to-all(f32[8,4,256]{2,1,0:T(4,128)S(1)} %broadcast_in_dim.14), channel_id=1, replica_groups=mesh['dp'=4,'x'=4,'zh'=2,'core'=2,'head'=8] {'head'}, dimensions={0} | all-to-all | bytes 65536 | tf_op jit(solution)/shard_map/all_to_all | solution.py:319
  104.4 6.7 %attend_grads.1 = (f32[32,128,128]{2,1,0:T(8,128)S(1)}, bf16[33,128,128]{2,1,0:T(8,128)(2,1)S(1)}, bf16[256,128]{1,0:T(8,128)(2,1)S(1)}, f32[17,8,128]{2,1,0:T(8,128)S(1)}) custom-call(s32[2,24]{1,0:T(2,128)S(1)} %multiply_add_fusion.1.pos_ref, s32[2,24]{1,0:T(2,128)S(1)} %get-tuple-element.42.home_ref, s32[2,24]{1,0:T(2,128)S(1)} %get-tuple-element.61.blk_ref, ...), custom_call_target="tpu_custom_call" | custom-call | flops 12000000000 | bytes 6291456 | tf_op jit(solution)/shard_map/attend_grads/pallas_call | solution.py:283
  111.1 1.9 collective-permute-start.4
  113.1 11.3 %all_to_all.31.weight_ref = bf16[8,128,128]{2,1,0:T(8,128)(2,1)S(1)} all-to-all(bf16[8,128,128]{2,1,0:T(8,128)(2,1)S(1)} %get-tuple-element.15), channel_id=1, replica_groups=mesh['dp'=4,'x'=4,'zh'=2,'core'=2,'head'=8] {'core','dp'}, dimensions={0} | all-to-all | bytes 524288 | tf_op jit(solution)/shard_map/all_to_all | solution.py:319
  125.7 7.2 %all-to-all-start.4 = ((bf16[4,1184,128]{2,1,0:T(8,128)(2,1)}), bf16[4,1184,128]{2,1,0:T(8,128)(2,1)S(1)}, u32[]{:S(2)}, u32[]{:S(2)}) async-start(bf16[4,1184,128]{2,1,0:T(8,128)(2,1)} %chip.1), calls=%async_computation.4 | async-start | bytes 2424832 | tf_op jit(solution)/shard_map/all_to_all | solution.py:319
  133.6 15.6 %all-to-all-done.4 = bf16[4,1184,128]{2,1,0:T(8,128)(2,1)S(1)} async-done(((bf16[4,1184,128]{2,1,0:T(8,128)(2,1)}), bf16[4,1184,128]{2,1,0:T(8,128)(2,1)S(1)}, u32[]{:S(2)}, u32[]{:S(2)}) %all-to-all-start.4) | async-done | bytes 1212448 | tf_op jit(solution)/shard_map/all_to_all | solution.py:319
  149.5 5.9 %collective-permute-start.5 = (bf16[672,128]{1,0:T(8,128)(2,1)S(1)}, bf16[672,128]{1,0:T(8,128)(2,1)S(1)}, u32[]{:S(2)}, u32[]{:S(2)}) collective-permute-start(bf16[672,128]{1,0:T(8,128)(2,1)S(1)} %pad_maximum_fusion.7), channel_id=1, source_target_pairs={{0,16},{16,0},{1,17},{17,1},{2,18},{18,2},{3,19},{19,3},{4,20},{20... | collective-permute-start | bytes 516104 | tf_op jit(solution)/shard_map/ppermute | solution.py:335
  155.4 16.7 %collective-permute-done.5 = bf16[672,128]{1,0:T(8,128)(2,1)S(1)} collective-permute-done((bf16[672,128]{1,0:T(8,128)(2,1)S(1)}, bf16[672,128]{1,0:T(8,128)(2,1)S(1)}, u32[]{:S(2)}, u32[]{:S(2)}) %collective-permute-start.5) | collective-permute-done | bytes 172064 | tf_op jit(solution)/shard_map/ppermute | solution.py:335
  172.3 2.5 %collective-permute-start.6 = (f32[136,128]{1,0:T(8,128)S(1)}, f32[136,128]{1,0:T(8,128)S(1)}, u32[]{:S(2)}, u32[]{:S(2)}) collective-permute-start(f32[136,128]{1,0:T(8,128)S(1)} %select_maximum_fusion.1), channel_id=1, source_target_pairs={{0,128},{128,0},{256,384},{384,256},{1,129},{129,1},{257,385},{385... | collective-permute-start | bytes 208904 | tf_op jit(solution)/shard_map/ppermute | solution.py:335
  175.8 6.7 %all-to-all-start.5 = ((bf16[8,32,640]{2,1,0:T(8,128)(2,1)}), bf16[8,32,640]{2,1,0:T(8,128)(2,1)S(1)}, u32[]{:S(2)}, u32[]{:S(2)}) async-start(bf16[8,32,640]{2,1,0:T(8,128)(2,1)} %pad_maximum_fusion.3), calls=%async_computation.5 | async-start | bytes 655360 | tf_op jit(solution)/shard_map/all_to_all | solution.py:319
  182.6 2.6 %collective-permute-start.7 = (f32[136,256]{1,0:T(8,128)S(1)}, f32[136,256]{1,0:T(8,128)S(1)}, u32[]{:S(2)}, u32[]{:S(2)}) collective-permute-start(f32[136,256]{1,0:T(8,128)S(1)} %select_maximum_fusion), channel_id=1, source_target_pairs={{0,256},{128,384},{256,0},{384,128},{1,257},{129,385},{257,1},{385... | collective-permute-start | bytes 417800 | tf_op jit(solution)/shard_map/ppermute | solution.py:335
  185.2 6.0 %collective-permute-done.7 = f32[136,256]{1,0:T(8,128)S(1)} collective-permute-done((f32[136,256]{1,0:T(8,128)S(1)}, f32[136,256]{1,0:T(8,128)S(1)}, u32[]{:S(2)}, u32[]{:S(2)}) %collective-permute-start.7) | collective-permute-done | bytes 139296 | tf_op jit(solution)/shard_map/ppermute | solution.py:335
  191.2 3.4 %collective-permute-start.8 = (f32[128,512]{1,0:T(8,128)S(1)}, f32[128,512]{1,0:T(8,128)S(1)}, u32[]{:S(2)}, u32[]{:S(2)}) collective-permute-start(f32[128,512]{1,0:T(8,128)S(1)} %pad_maximum_fusion.5), channel_id=1, source_target_pairs={{0,8},{8,0},{1,9},{9,1},{2,10},{10,2},{3,11},{11,3},{4,12},{12,4},... | collective-permute-start | bytes 786440 | tf_op jit(solution)/shard_map/ppermute | solution.py:327
  196.6 1.6 all-to-all-done.5.back_ref
  (87 shorter events, 16.7 us)
Async XLA Ops:
  7.2 41.7 %copy-start = (s32[1,32,24]{1,2,0:T(8,128)S(1)}, s32[1,32,24]{1,2,0:T(8,128)}, u32[]{:S(2)}) copy-start(s32[1,32,24]{1,2,0:T(8,128)} %param.10) | copy-start | bytes 9220
  7.2 17.8 %copy-start.3 = (bf16[128,1024]{1,0:T(8,128)(2,1)S(1)}, bf16[128,1024]{1,0:T(8,128)(2,1)}, u32[]{:S(2)}) copy-start(bf16[128,1024]{1,0:T(8,128)(2,1)} %param.8) | copy-start | bytes 786436
  7.2 17.8 %copy-start.4 = (bf16[1,32,1024]{2,1,0:T(8,128)(2,1)S(1)}, bf16[1,32,1024]{2,1,0:T(8,128)(2,1)}, u32[]{:S(2)}) copy-start(bf16[1,32,1024]{2,1,0:T(8,128)(2,1)} %param.7) | copy-start | bytes 196612
  9.2 28.9 %all-to-all-start.1 = ((bf16[16,32,256]{2,1,0:T(8,128)(2,1)}), bf16[16,32,256]{2,1,0:T(8,128)(2,1)S(1)}, u32[]{:S(2)}, u32[]{:S(2)}) async-start(bf16[16,32,256]{2,1,0:T(8,128)(2,1)} %pad_maximum_fusion.4), calls=%async_computation.1 | async-start | bytes 524288 | tf_op jit(solution)/shard_map/all_to_all | solution.py:319
  24.9 24.3 %copy-start.1 = (s32[1,4096]{1,0:T(1,128)S(1)}, s32[1,4096]{1,0:T(1,128)}, u32[]{:S(2)}) copy-start(s32[1,4096]{1,0:T(1,128)} %param.11) | copy-start | bytes 49156
  38.0 37.4 %all-to-all-start = ((bf16[8,32,1408]{2,1,0:T(8,128)(2,1)}), bf16[8,32,1408]{2,1,0:T(8,128)(2,1)S(1)}, u32[]{:S(2)}, u32[]{:S(2)}) async-start(bf16[8,32,1408]{2,1,0:T(8,128)(2,1)} %pad_maximum_fusion.1), calls=%async_computation | async-start | bytes 1441792 | tf_op jit(solution)/shard_map/all_to_all | solution.py:319
  49.6 11.8 %collective-permute-start = (bf16[512,256]{1,0:T(8,128)(2,1)S(1)}, bf16[512,256]{1,0:T(8,128)(2,1)S(1)}, u32[]{:S(2)}, u32[]{:S(2)}) collective-permute-start(bf16[512,256]{1,0:T(8,128)(2,1)S(1)} %bitcast.85), channel_id=1, source_target_pairs={{0,32},{32,64},{64,96},{96,0},{1,33},{33,65},{65,97},{97,1},{2,34}... | collective-permute-start | bytes 786440 | tf_op jit(solution)/shard_map/ppermute | solution.py:331
  52.8 8.7 %collective-permute-start.1 = (bf16[512,256]{1,0:T(8,128)(2,1)S(1)}, bf16[512,256]{1,0:T(8,128)(2,1)S(1)}, u32[]{:S(2)}, u32[]{:S(2)}) collective-permute-start(bf16[512,256]{1,0:T(8,128)(2,1)S(1)} %bitcast.86), channel_id=1, source_target_pairs={{0,96},{32,0},{64,32},{96,64},{1,97},{33,1},{65,33},{97,65},{2,98}... | collective-permute-start | bytes 786440 | tf_op jit(solution)/shard_map/ppermute | solution.py:331
  56.1 9.6 %collective-permute-start.2 = (bf16[512,256]{1,0:T(8,128)(2,1)S(1)}, bf16[512,256]{1,0:T(8,128)(2,1)S(1)}, u32[]{:S(2)}, u32[]{:S(2)}) collective-permute-start(bf16[512,256]{1,0:T(8,128)(2,1)S(1)} %bitcast.87), channel_id=1, source_target_pairs={{0,64},{32,96},{64,0},{96,32},{1,65},{33,97},{65,1},{97,33},{2,66}... | collective-permute-start | bytes 786440 | tf_op jit(solution)/shard_map/ppermute | solution.py:331
  59.6 10.9 %copy-start.5 = (f32[1,16]{1,0:T(1,128)S(1)}, f32[1,16]{1,0:T(1,128)}, u32[]{:S(2)}) copy-start(f32[1,16]{1,0:T(1,128)} %param.9) | copy-start | bytes 196
  65.8 10.3 %collective-permute-start.3 = (bf16[2048,256]{1,0:T(8,128)(2,1)S(1)}, bf16[2048,256]{1,0:T(8,128)(2,1)S(1)}, u32[]{:S(2)}, u32[]{:S(2)}) collective-permute-start(bf16[2048,256]{1,0:T(8,128)(2,1)S(1)} %pad_maximum_fusion.refs_0_), channel_id=1, source_target_pairs={{0,8},{8,0},{1,9},{9,1},{2,10},{10,2},{3,11},{11,3},{4,12},{12,4},... | collective-permute-start | bytes 3145736 | tf_op jit(solution)/shard_map/ppermute | solution.py:327
  111.1 13.3 %collective-permute-start.4 = (bf16[33,128,128]{2,1,0:T(8,128)(2,1)S(1)}, bf16[33,128,128]{2,1,0:T(8,128)(2,1)S(1)}, u32[]{:S(2)}, u32[]{:S(2)}) collective-permute-start(bf16[33,128,128]{2,1,0:T(8,128)(2,1)S(1)} %get-tuple-element.14), channel_id=1, source_target_pairs={{0,8},{8,0},{1,9},{9,1},{2,10},{10,2},{3,11},{11,3},{4,12},{12,4},... | collective-permute-start | bytes 3244040 | tf_op jit(solution)/shard_map/ppermute | solution.py:327
  125.7 23.5 %all-to-all-start.4 = ((bf16[4,1184,128]{2,1,0:T(8,128)(2,1)}), bf16[4,1184,128]{2,1,0:T(8,128)(2,1)S(1)}, u32[]{:S(2)}, u32[]{:S(2)}) async-start(bf16[4,1184,128]{2,1,0:T(8,128)(2,1)} %chip.1), calls=%async_computation.4 | async-start | bytes 2424832 | tf_op jit(solution)/shard_map/all_to_all | solution.py:319
  132.9 66.4 %all-gather.2.cloned.1.call-start = ((), (), s32[]{:S(2)}) async-start(), calls=%async_computation.6 | async-start | bytes 2162688 | tf_op jit(solution)/shard_map/all_gather | solution.py:385
  149.5 22.6 %collective-permute-start.5 = (bf16[672,128]{1,0:T(8,128)(2,1)S(1)}, bf16[672,128]{1,0:T(8,128)(2,1)S(1)}, u32[]{:S(2)}, u32[]{:S(2)}) collective-permute-start(bf16[672,128]{1,0:T(8,128)(2,1)S(1)} %pad_maximum_fusion.7), channel_id=1, source_target_pairs={{0,16},{16,0},{1,17},{17,1},{2,18},{18,2},{3,19},{19,3},{4,20},{20... | collective-permute-start | bytes 516104 | tf_op jit(solution)/shard_map/ppermute | solution.py:335
  172.3 10.3 %collective-permute-start.6 = (f32[136,128]{1,0:T(8,128)S(1)}, f32[136,128]{1,0:T(8,128)S(1)}, u32[]{:S(2)}, u32[]{:S(2)}) collective-permute-start(f32[136,128]{1,0:T(8,128)S(1)} %select_maximum_fusion.1), channel_id=1, source_target_pairs={{0,128},{128,0},{256,384},{384,256},{1,129},{129,1},{257,385},{385... | collective-permute-start | bytes 208904 | tf_op jit(solution)/shard_map/ppermute | solution.py:335
  175.8 22.4 %all-to-all-start.5 = ((bf16[8,32,640]{2,1,0:T(8,128)(2,1)}), bf16[8,32,640]{2,1,0:T(8,128)(2,1)S(1)}, u32[]{:S(2)}, u32[]{:S(2)}) async-start(bf16[8,32,640]{2,1,0:T(8,128)(2,1)} %pad_maximum_fusion.3), calls=%async_computation.5 | async-start | bytes 655360 | tf_op jit(solution)/shard_map/all_to_all | solution.py:319
  182.6 8.6 %collective-permute-start.7 = (f32[136,256]{1,0:T(8,128)S(1)}, f32[136,256]{1,0:T(8,128)S(1)}, u32[]{:S(2)}, u32[]{:S(2)}) collective-permute-start(f32[136,256]{1,0:T(8,128)S(1)} %select_maximum_fusion), channel_id=1, source_target_pairs={{0,256},{128,384},{256,0},{384,128},{1,257},{129,385},{257,1},{385... | collective-permute-start | bytes 417800 | tf_op jit(solution)/shard_map/ppermute | solution.py:335
  191.2 4.5 %collective-permute-start.8 = (f32[128,512]{1,0:T(8,128)S(1)}, f32[128,512]{1,0:T(8,128)S(1)}, u32[]{:S(2)}, u32[]{:S(2)}) collective-permute-start(f32[128,512]{1,0:T(8,128)S(1)} %pad_maximum_fusion.5), channel_id=1, source_target_pairs={{0,8},{8,0},{1,9},{9,1},{2,10},{10,2},{3,11},{11,3},{4,12},{12,4},... | collective-permute-start | bytes 786440 | tf_op jit(solution)/shard_map/ppermute | solution.py:327
  199.3 1.6 copy-start.2
Sparse Core Ops, SparseCore 0:
  137.4 53.6 all-gather.1

commit v5 on v4

--- a/solution.py
+++ b/solution.py
@@ -138,13 +138,9 @@
 def grads_kernel(
     pos_ref, home_ref, blk_ref, low_ref, width_ref, n_ref, bias_ref, power_ref, stamps_ref, q_ref, g_ref, *refs
 ):
-    parts = refs[:PARTS]
-    own_ref, other_ref, dq_ref, bins_ref, kv, acc, sems = refs[PARTS:]
-    copies = load_pairs(parts, kv, sems)
+    kv, acc, other_ref, dq_ref, bins_ref = refs
     acc[...] = jnp.zeros(acc.shape, f32)
     bins_ref[...] = jnp.zeros(bins_ref.shape, f32)
-    for copy in copies:
-        copy.wait()
     for slot in range(2):
         listed, query_stamps, inverse = slot_setup(slot, blk_ref, n_ref, stamps_ref)
         query = q_ref[slot * BLOCK : (slot + 1) * BLOCK, :]
@@ -199,8 +195,7 @@
         total = lax.fori_loop(0, steps, group, total)
         dq_ref[slot * BLOCK : (slot + 1) * BLOCK, :] = (total * SCALE).astype(bf16)
     half = BLOCKS // 2
-    own_ref[...] = acc[0:half].reshape(own_ref.shape)
-    other_ref[0 : 4 * TILES] = acc[half:].reshape(own_ref.shape).astype(bf16)
+    other_ref[0 : 4 * TILES] = acc[half:].reshape(4 * TILES, HEAD_DIM, BLOCK).astype(bf16)
     bins = jnp.sum(bins_ref[0:BUCKETS], axis=1)
     high = bins.astype(bf16)
     low = (bins - high.astype(f32)).astype(bf16)
@@ -241,7 +236,7 @@
     low = (bins - high.astype(f32)).astype(bf16)
     for k in range(4):
         for j in range(TILES):
-            tile = own_ref[k * TILES + j] + other_ref[k * TILES + j].astype(f32)
+            tile = own_ref[(k * TILES + j) // 2, j % 2] + other_ref[k * TILES + j].astype(f32)
             out_ref[k, j * HEAD_DIM : (j + 1) * HEAD_DIM] = tile.astype(bf16)
         out_ref[k, split : split + HEAD_DIM] = weight
         out_ref[k, split + HEAD_DIM : split + HEAD_DIM + BUCKETS] = high
@@ -264,11 +259,13 @@
 def attend(tables, query, parts):
     return pl.pallas_call(
         attend_kernel,
-        out_shape=jax.ShapeDtypeStruct((2 * BLOCK, HEAD_DIM), f32),
+        out_shape=(
+            jax.ShapeDtypeStruct((2 * BLOCK, HEAD_DIM), f32),
+            jax.ShapeDtypeStruct((BLOCKS * BLOCK, 2 * HEAD_DIM), bf16),
+        ),
         in_specs=[SMEM()] * 8 + [VMEM()] * 2 + [ANY()] * PARTS,
-        out_specs=VMEM(),
+        out_specs=(VMEM(), VMEM()),
         scratch_shapes=[
-            pltpu.VMEM((BLOCKS * BLOCK, 2 * HEAD_DIM), bf16),
             pltpu.SemaphoreType.DMA((PARTS,)),
         ],
         compiler_params=pltpu.CompilerParams(vmem_limit_bytes=12 * MIB),
@@ -279,28 +276,23 @@
     )(*tables, query, *parts)
 
 
-def attend_grads(tables, query, grad, parts):
+def attend_grads(tables, query, grad, pairs):
     return pl.pallas_call(
         grads_kernel,
         out_shape=(
-            jax.ShapeDtypeStruct((4 * TILES, HEAD_DIM, BLOCK), f32),
+            jax.ShapeDtypeStruct((BLOCKS, 2, HEAD_DIM, BLOCK), f32),
             jax.ShapeDtypeStruct((4 * TILES + 1, HEAD_DIM, BLOCK), bf16),
             jax.ShapeDtypeStruct((2 * BLOCK, HEAD_DIM), bf16),
             jax.ShapeDtypeStruct((BUCKETS + 1, 8, BLOCK), f32),
         ),
-        in_specs=[SMEM()] * 8 + [VMEM()] * 3 + [ANY()] * PARTS,
+        in_specs=[SMEM()] * 8 + [VMEM()] * 4,
         out_specs=(VMEM(),) * 4,
-        scratch_shapes=[
-            pltpu.VMEM((BLOCKS * BLOCK, 2 * HEAD_DIM), bf16),
-            pltpu.VMEM((BLOCKS, 2, HEAD_DIM, BLOCK), f32),
-            pltpu.SemaphoreType.DMA((PARTS,)),
-        ],
         compiler_params=pltpu.CompilerParams(vmem_limit_bytes=24 * MIB),
         cost_estimate=pl.CostEstimate(
             flops=12 * 10**9, bytes_accessed=6 << 20, transcendentals=48 * BLOCK**2
         ),
         name="attend_grads",
-    )(*tables, query, grad, *parts)
+    )(*tables, query, grad, pairs)
 
 
 def whole_call(kernel, out_shape, name, *args):
@@ -400,7 +392,7 @@
     stamp_blocks = stamps[0].reshape(BLOCKS, BLOCK)
     tables = tables_of(lists, blk, pos, home, run, stamp_blocks, time_bias[0])
 
-    attended = attend(tables, query, parts)
+    attended, pairs = attend(tables, query, parts)
 
     gated_grad = nt_dot(cot, out_weight)
     normed_grad = gated_grad * gate.astype(f32)
@@ -420,7 +412,7 @@
     )
     weight_part = exchange(weight_part, ("core", "dp"))
 
-    own_grads, other_grads, grad_q, bins = attend_grads(tables, query, attended_grad, parts)
+    own_grads, other_grads, grad_q, bins = attend_grads(tables, query, attended_grad, pairs)
     theirs = swap_core(other_grads)
     split = TILES * HEAD_DIM
     chip = jax.ShapeDtypeStruct((4, split + HEAD_DIM + 2 * BUCKETS, BLOCK), bf16)

time: 212 us -> 213 us (level)
  starting transfers between devices: 71.2 us -> 74.2 us
  waiting for transfers between devices: 62.4 us -> 60 us
    ppermute x3, starting transfers between devices: 11 us -> 15.4 us  [flip(): lax.ppermute(values, axis, [(i, i ^ by) for i in range(lax.axis_size(axis...]
where the time goes in v5:
time: 213 us; the launch traced here: 209 us
  starting transfers between devices  74.2 us (35%)
  waiting for transfers between devices  60 us (28%)
  blocking collectives  35.4 us (17%)
  between operations  14.5 us (7%)
  Pallas kernels  12.5 us (6%)
  local copies, waits for them, and re-layouts  7.33 us (3%)
  other arithmetic  4.92 us (2%)
    all_to_all x4, starting transfers between devices, exchange(): return lax.all_to_all(values, axes, split_axis=0, concat_axis=0, tiled=True)  39.3 us
    all_to_all x2, blocking collectives, exchange(): return lax.all_to_all(values, axes, split_axis=0, concat_axis=0, tiled=True)  35.4 us
    all_to_all x4, waiting for transfers between devices, exchange(): return lax.all_to_all(values, axes, split_axis=0, concat_axis=0, tiled=True)  32.7 us
    ppermute x3, waiting for transfers between devices, flip(): lax.ppermute(values, axis, [(i, i ^ by) for i in range(lax.axis_size(axis...  21.6 us
    ppermute x3, starting transfers between devices, flip(): lax.ppermute(values, axis, [(i, i ^ by) for i in range(lax.axis_size(axis...  15.4 us
    ppermute x3, starting transfers between devices, shift_x(): return lax.ppermute(values, 'x', [(i, (i + by) % 4) for i in range(4)])  9.93 us
    ppermute x3, starting transfers between devices, swap_core(): return lax.ppermute(values, 'core', [(0, 1), (1, 0)])  9.58 us
    pallas_call x1, Pallas kernels, attend_grads(): pl.pallas_call(grads_kernel, out_shape=(jax.ShapeDtypeStruct((BLOCKS, 2,...  6.43 us
  transfers between devices with their start and end apart: 14, of which 8 were waited for; matrix products, arithmetic and copies ran while one was open for 4% of the time, Pallas kernels for 0%

profile of v5, /device:TPU:1, one launch (start us, length us, event | category | flops | bytes accessed | tf_op | source)
XLA Modules:
  0.0 209.2 jit_solution(5844899350303996589)
XLA Ops:
  9.3 15.7 %all-to-all-start.1 = ((bf16[16,32,256]{2,1,0:T(8,128)(2,1)}), bf16[16,32,256]{2,1,0:T(8,128)(2,1)S(1)}, u32[]{:S(2)}, u32[]{:S(2)}) async-start(bf16[16,32,256]{2,1,0:T(8,128)(2,1)} %pad_maximum_fusion.4), calls=%async_computation.1 | async-start | bytes 524288 | tf_op jit(solution)/shard_map/all_to_all | solution.py:311
  26.2 12.0 %all-to-all-done.1 = bf16[16,32,256]{2,1,0:T(8,128)(2,1)S(1)} async-done(((bf16[16,32,256]{2,1,0:T(8,128)(2,1)}), bf16[16,32,256]{2,1,0:T(8,128)(2,1)S(1)}, u32[]{:S(2)}, u32[]{:S(2)}) %all-to-all-start.1) | async-done | bytes 262176 | tf_op jit(solution)/shard_map/all_to_all | solution.py:311
  38.2 10.8 %all-to-all-start = ((bf16[8,32,1408]{2,1,0:T(8,128)(2,1)}), bf16[8,32,1408]{2,1,0:T(8,128)(2,1)S(1)}, u32[]{:S(2)}, u32[]{:S(2)}) async-start(bf16[8,32,1408]{2,1,0:T(8,128)(2,1)} %pad_maximum_fusion.1), calls=%async_computation | async-start | bytes 1441792 | tf_op jit(solution)/shard_map/all_to_all | solution.py:311
  49.8 3.1 %collective-permute-start = (bf16[512,256]{1,0:T(8,128)(2,1)S(1)}, bf16[512,256]{1,0:T(8,128)(2,1)S(1)}, u32[]{:S(2)}, u32[]{:S(2)}) collective-permute-start(bf16[512,256]{1,0:T(8,128)(2,1)S(1)} %bitcast.80), channel_id=1, source_target_pairs={{0,32},{32,64},{64,96},{96,0},{1,33},{33,65},{65,97},{97,1},{2,34}... | collective-permute-start | bytes 786440 | tf_op jit(solution)/shard_map/ppermute | solution.py:323
  52.9 3.4 %collective-permute-start.1 = (bf16[512,256]{1,0:T(8,128)(2,1)S(1)}, bf16[512,256]{1,0:T(8,128)(2,1)S(1)}, u32[]{:S(2)}, u32[]{:S(2)}) collective-permute-start(bf16[512,256]{1,0:T(8,128)(2,1)S(1)} %bitcast.81), channel_id=1, source_target_pairs={{0,96},{32,0},{64,32},{96,64},{1,97},{33,1},{65,33},{97,65},{2,98}... | collective-permute-start | bytes 786440 | tf_op jit(solution)/shard_map/ppermute | solution.py:323
  56.3 3.4 %collective-permute-start.2 = (bf16[512,256]{1,0:T(8,128)(2,1)S(1)}, bf16[512,256]{1,0:T(8,128)(2,1)S(1)}, u32[]{:S(2)}, u32[]{:S(2)}) collective-permute-start(bf16[512,256]{1,0:T(8,128)(2,1)S(1)} %bitcast.82), channel_id=1, source_target_pairs={{0,64},{32,96},{64,0},{96,32},{1,65},{33,97},{65,1},{97,33},{2,66}... | collective-permute-start | bytes 786440 | tf_op jit(solution)/shard_map/ppermute | solution.py:323
  61.6 4.3 %collective-permute-done.2 = bf16[512,256]{1,0:T(8,128)(2,1)S(1)} collective-permute-done((bf16[512,256]{1,0:T(8,128)(2,1)S(1)}, bf16[512,256]{1,0:T(8,128)(2,1)S(1)}, u32[]{:S(2)}, u32[]{:S(2)}) %collective-permute-start.2) | collective-permute-done | bytes 262176 | tf_op jit(solution)/shard_map/ppermute | solution.py:323
  66.0 4.4 %collective-permute-start.3 = (bf16[2048,256]{1,0:T(8,128)(2,1)S(1)}, bf16[2048,256]{1,0:T(8,128)(2,1)S(1)}, u32[]{:S(2)}, u32[]{:S(2)}) collective-permute-start(bf16[2048,256]{1,0:T(8,128)(2,1)S(1)} %pad_maximum_fusion.refs_0_), channel_id=1, source_target_pairs={{0,8},{8,0},{1,9},{9,1},{2,10},{10,2},{3,11},{11,3},{4,12},{12,4},... | collective-permute-start | bytes 3145736 | tf_op jit(solution)/shard_map/ppermute | solution.py:319
  70.8 4.8 %all-to-all-done = bf16[8,32,1408]{2,1,0:T(8,128)(2,1)S(1)} async-done(((bf16[8,32,1408]{2,1,0:T(8,128)(2,1)}), bf16[8,32,1408]{2,1,0:T(8,128)(2,1)S(1)}, u32[]{:S(2)}, u32[]{:S(2)}) %all-to-all-start) | async-done | bytes 720928 | tf_op jit(solution)/shard_map/all_to_all | solution.py:311
  76.3 3.3 %attend.1 = (f32[256,128]{1,0:T(8,128)S(1)}, bf16[4096,256]{1,0:T(8,128)(2,1)S(1)}) custom-call(s32[2,24]{1,0:T(2,128)S(1)} %multiply_add_fusion.1.pos_ref, s32[2,24]{1,0:T(2,128)S(1)} %get-tuple-element.54.home_ref, s32[2,24]{1,0:T(2,128)S(1)} %get-tuple-element.73.blk_ref, s32[2,24]{1,0:T(2,128)S(1)} %get-tuple-element.53.low_ref, ...), custom_call_target="tpu_custom_call" | custom-call | flops 5000000000 | bytes 3145728 | tf_op jit(solution)/shard_map/attend/pallas_call | solution.py:260
  80.1 24.0 %all_to_all.30.sums_ref = f32[8,4,256]{2,1,0:T(4,128)S(1)} all-to-all(f32[8,4,256]{2,1,0:T(4,128)S(1)} %broadcast_in_dim.14), channel_id=1, replica_groups=mesh['dp'=4,'x'=4,'zh'=2,'core'=2,'head'=8] {'head'}, dimensions={0} | all-to-all | bytes 65536 | tf_op jit(solution)/shard_map/all_to_all | solution.py:311
  104.6 6.4 %attend_grads.1 = (f32[32,2,128,128]{3,2,1,0:T(8,128)S(1)}, bf16[33,128,128]{2,1,0:T(8,128)(2,1)S(1)}, bf16[256,128]{1,0:T(8,128)(2,1)S(1)}, f32[17,8,128]{2,1,0:T(8,128)S(1)}) custom-call(s32[2,24]{1,0:T(2,128)S(1)} %multiply_add_fusion.1.pos_ref, s32[2,24]{1,0:T(2,128)S(1)} %get-tuple-element.54.home_ref, s32[2,24]{1,0:T(2,128)S(1)} %get-tuple-element.73.blk_ref, ...), custom_call_target="tpu_custom_call" | custom-call | flops 12000000000 | bytes 6291456 | tf_op jit(solution)/shard_map/attend_grads/pallas_call | solution.py:280
  111.0 1.9 collective-permute-start.4
  113.0 11.3 %all_to_all.31.weight_ref = bf16[8,128,128]{2,1,0:T(8,128)(2,1)S(1)} all-to-all(bf16[8,128,128]{2,1,0:T(8,128)(2,1)S(1)} %get-tuple-element.19), channel_id=1, replica_groups=mesh['dp'=4,'x'=4,'zh'=2,'core'=2,'head'=8] {'core','dp'}, dimensions={0} | all-to-all | bytes 524288 | tf_op jit(solution)/shard_map/all_to_all | solution.py:311
  125.5 7.8 %all-to-all-start.4 = ((bf16[4,1184,128]{2,1,0:T(8,128)(2,1)}), bf16[4,1184,128]{2,1,0:T(8,128)(2,1)S(1)}, u32[]{:S(2)}, u32[]{:S(2)}) async-start(bf16[4,1184,128]{2,1,0:T(8,128)(2,1)} %chip.1), calls=%async_computation.4 | async-start | bytes 2424832 | tf_op jit(solution)/shard_map/all_to_all | solution.py:311
  134.1 15.6 %all-to-all-done.4 = bf16[4,1184,128]{2,1,0:T(8,128)(2,1)S(1)} async-done(((bf16[4,1184,128]{2,1,0:T(8,128)(2,1)}), bf16[4,1184,128]{2,1,0:T(8,128)(2,1)S(1)}, u32[]{:S(2)}, u32[]{:S(2)}) %all-to-all-start.4) | async-done | bytes 1212448 | tf_op jit(solution)/shard_map/all_to_all | solution.py:311
  150.0 10.1 %collective-permute-start.5 = (bf16[672,128]{1,0:T(8,128)(2,1)S(1)}, bf16[672,128]{1,0:T(8,128)(2,1)S(1)}, u32[]{:S(2)}, u32[]{:S(2)}) collective-permute-start(bf16[672,128]{1,0:T(8,128)(2,1)S(1)} %pad_maximum_fusion.7), channel_id=1, source_target_pairs={{0,16},{16,0},{1,17},{17,1},{2,18},{18,2},{3,19},{19,3},{4,20},{20... | collective-permute-start | bytes 516104 | tf_op jit(solution)/shard_map/ppermute | solution.py:327
  160.1 14.2 %collective-permute-done.5 = bf16[672,128]{1,0:T(8,128)(2,1)S(1)} collective-permute-done((bf16[672,128]{1,0:T(8,128)(2,1)S(1)}, bf16[672,128]{1,0:T(8,128)(2,1)S(1)}, u32[]{:S(2)}, u32[]{:S(2)}) %collective-permute-start.5) | collective-permute-done | bytes 172064 | tf_op jit(solution)/shard_map/ppermute | solution.py:327
  174.5 2.7 %collective-permute-start.6 = (f32[136,128]{1,0:T(8,128)S(1)}, f32[136,128]{1,0:T(8,128)S(1)}, u32[]{:S(2)}, u32[]{:S(2)}) collective-permute-start(f32[136,128]{1,0:T(8,128)S(1)} %select_maximum_fusion.1), channel_id=1, source_target_pairs={{0,128},{128,0},{256,384},{384,256},{1,129},{129,1},{257,385},{385... | collective-permute-start | bytes 208904 | tf_op jit(solution)/shard_map/ppermute | solution.py:327
  178.1 4.9 %all-to-all-start.5 = ((bf16[8,32,640]{2,1,0:T(8,128)(2,1)}), bf16[8,32,640]{2,1,0:T(8,128)(2,1)S(1)}, u32[]{:S(2)}, u32[]{:S(2)}) async-start(bf16[8,32,640]{2,1,0:T(8,128)(2,1)} %pad_maximum_fusion.3), calls=%async_computation.5 | async-start | bytes 655360 | tf_op jit(solution)/shard_map/all_to_all | solution.py:311
  183.1 2.6 %collective-permute-start.7 = (f32[136,256]{1,0:T(8,128)S(1)}, f32[136,256]{1,0:T(8,128)S(1)}, u32[]{:S(2)}, u32[]{:S(2)}) collective-permute-start(f32[136,256]{1,0:T(8,128)S(1)} %select_maximum_fusion), channel_id=1, source_target_pairs={{0,256},{128,384},{256,0},{384,128},{1,257},{129,385},{257,1},{385... | collective-permute-start | bytes 417800 | tf_op jit(solution)/shard_map/ppermute | solution.py:327
  185.7 7.5 %collective-permute-done.7 = f32[136,256]{1,0:T(8,128)S(1)} collective-permute-done((f32[136,256]{1,0:T(8,128)S(1)}, f32[136,256]{1,0:T(8,128)S(1)}, u32[]{:S(2)}, u32[]{:S(2)}) %collective-permute-start.7) | collective-permute-done | bytes 139296 | tf_op jit(solution)/shard_map/ppermute | solution.py:327
  193.3 3.2 %collective-permute-start.8 = (f32[128,512]{1,0:T(8,128)S(1)}, f32[128,512]{1,0:T(8,128)S(1)}, u32[]{:S(2)}, u32[]{:S(2)}) collective-permute-start(f32[128,512]{1,0:T(8,128)S(1)} %pad_maximum_fusion.5), channel_id=1, source_target_pairs={{0,8},{8,0},{1,9},{9,1},{2,10},{10,2},{3,11},{11,3},{4,12},{12,4},... | collective-permute-start | bytes 786440 | tf_op jit(solution)/shard_map/ppermute | solution.py:319
  199.8 1.6 copy-done.2
  (90 shorter events, 15.5 us)
Async XLA Ops:
  7.2 41.9 %copy-start = (s32[1,32,24]{1,2,0:T(8,128)S(1)}, s32[1,32,24]{1,2,0:T(8,128)}, u32[]{:S(2)}) copy-start(s32[1,32,24]{1,2,0:T(8,128)} %param.10) | copy-start | bytes 9220
  7.2 17.9 %copy-start.3 = (bf16[128,1024]{1,0:T(8,128)(2,1)S(1)}, bf16[128,1024]{1,0:T(8,128)(2,1)}, u32[]{:S(2)}) copy-start(bf16[128,1024]{1,0:T(8,128)(2,1)} %param.8) | copy-start | bytes 786436
  7.2 17.9 %copy-start.4 = (bf16[1,32,1024]{2,1,0:T(8,128)(2,1)S(1)}, bf16[1,32,1024]{2,1,0:T(8,128)(2,1)}, u32[]{:S(2)}) copy-start(bf16[1,32,1024]{2,1,0:T(8,128)(2,1)} %param.7) | copy-start | bytes 196612
  9.3 28.9 %all-to-all-start.1 = ((bf16[16,32,256]{2,1,0:T(8,128)(2,1)}), bf16[16,32,256]{2,1,0:T(8,128)(2,1)S(1)}, u32[]{:S(2)}, u32[]{:S(2)}) async-start(bf16[16,32,256]{2,1,0:T(8,128)(2,1)} %pad_maximum_fusion.4), calls=%async_computation.1 | async-start | bytes 524288 | tf_op jit(solution)/shard_map/all_to_all | solution.py:311
  25.2 24.3 %copy-start.1 = (s32[1,4096]{1,0:T(1,128)S(1)}, s32[1,4096]{1,0:T(1,128)}, u32[]{:S(2)}) copy-start(s32[1,4096]{1,0:T(1,128)} %param.11) | copy-start | bytes 49156
  38.2 37.4 %all-to-all-start = ((bf16[8,32,1408]{2,1,0:T(8,128)(2,1)}), bf16[8,32,1408]{2,1,0:T(8,128)(2,1)S(1)}, u32[]{:S(2)}, u32[]{:S(2)}) async-start(bf16[8,32,1408]{2,1,0:T(8,128)(2,1)} %pad_maximum_fusion.1), calls=%async_computation | async-start | bytes 1441792 | tf_op jit(solution)/shard_map/all_to_all | solution.py:311
  49.8 11.8 %collective-permute-start = (bf16[512,256]{1,0:T(8,128)(2,1)S(1)}, bf16[512,256]{1,0:T(8,128)(2,1)S(1)}, u32[]{:S(2)}, u32[]{:S(2)}) collective-permute-start(bf16[512,256]{1,0:T(8,128)(2,1)S(1)} %bitcast.80), channel_id=1, source_target_pairs={{0,32},{32,64},{64,96},{96,0},{1,33},{33,65},{65,97},{97,1},{2,34}... | collective-permute-start | bytes 786440 | tf_op jit(solution)/shard_map/ppermute | solution.py:323
  52.9 8.7 %collective-permute-start.1 = (bf16[512,256]{1,0:T(8,128)(2,1)S(1)}, bf16[512,256]{1,0:T(8,128)(2,1)S(1)}, u32[]{:S(2)}, u32[]{:S(2)}) collective-permute-start(bf16[512,256]{1,0:T(8,128)(2,1)S(1)} %bitcast.81), channel_id=1, source_target_pairs={{0,96},{32,0},{64,32},{96,64},{1,97},{33,1},{65,33},{97,65},{2,98}... | collective-permute-start | bytes 786440 | tf_op jit(solution)/shard_map/ppermute | solution.py:323
  56.3 9.6 %collective-permute-start.2 = (bf16[512,256]{1,0:T(8,128)(2,1)S(1)}, bf16[512,256]{1,0:T(8,128)(2,1)S(1)}, u32[]{:S(2)}, u32[]{:S(2)}) collective-permute-start(bf16[512,256]{1,0:T(8,128)(2,1)S(1)} %bitcast.82), channel_id=1, source_target_pairs={{0,64},{32,96},{64,0},{96,32},{1,65},{33,97},{65,1},{97,33},{2,66}... | collective-permute-start | bytes 786440 | tf_op jit(solution)/shard_map/ppermute | solution.py:323
  59.8 10.9 %copy-start.5 = (f32[1,16]{1,0:T(1,128)S(1)}, f32[1,16]{1,0:T(1,128)}, u32[]{:S(2)}) copy-start(f32[1,16]{1,0:T(1,128)} %param.9) | copy-start | bytes 196
  66.0 10.3 %collective-permute-start.3 = (bf16[2048,256]{1,0:T(8,128)(2,1)S(1)}, bf16[2048,256]{1,0:T(8,128)(2,1)S(1)}, u32[]{:S(2)}, u32[]{:S(2)}) collective-permute-start(bf16[2048,256]{1,0:T(8,128)(2,1)S(1)} %pad_maximum_fusion.refs_0_), channel_id=1, source_target_pairs={{0,8},{8,0},{1,9},{9,1},{2,10},{10,2},{3,11},{11,3},{4,12},{12,4},... | collective-permute-start | bytes 3145736 | tf_op jit(solution)/shard_map/ppermute | solution.py:319
  111.0 13.3 %collective-permute-start.4 = (bf16[33,128,128]{2,1,0:T(8,128)(2,1)S(1)}, bf16[33,128,128]{2,1,0:T(8,128)(2,1)S(1)}, u32[]{:S(2)}, u32[]{:S(2)}) collective-permute-start(bf16[33,128,128]{2,1,0:T(8,128)(2,1)S(1)} %get-tuple-element.18), channel_id=1, source_target_pairs={{0,8},{8,0},{1,9},{9,1},{2,10},{10,2},{3,11},{11,3},{4,12},{12,4},... | collective-permute-start | bytes 3244040 | tf_op jit(solution)/shard_map/ppermute | solution.py:319
  125.5 24.1 %all-to-all-start.4 = ((bf16[4,1184,128]{2,1,0:T(8,128)(2,1)}), bf16[4,1184,128]{2,1,0:T(8,128)(2,1)S(1)}, u32[]{:S(2)}, u32[]{:S(2)}) async-start(bf16[4,1184,128]{2,1,0:T(8,128)(2,1)} %chip.1), calls=%async_computation.4 | async-start | bytes 2424832 | tf_op jit(solution)/shard_map/all_to_all | solution.py:311
  133.4 66.4 %all-gather.2.cloned.1.call-start = ((), (), s32[]{:S(2)}) async-start(), calls=%async_computation.6 | async-start | bytes 2162688 | tf_op jit(solution)/shard_map/all_gather | solution.py:377
  150.0 24.3 %collective-permute-start.5 = (bf16[672,128]{1,0:T(8,128)(2,1)S(1)}, bf16[672,128]{1,0:T(8,128)(2,1)S(1)}, u32[]{:S(2)}, u32[]{:S(2)}) collective-permute-start(bf16[672,128]{1,0:T(8,128)(2,1)S(1)} %pad_maximum_fusion.7), channel_id=1, source_target_pairs={{0,16},{16,0},{1,17},{17,1},{2,18},{18,2},{3,19},{19,3},{4,20},{20... | collective-permute-start | bytes 516104 | tf_op jit(solution)/shard_map/ppermute | solution.py:327
  174.5 8.6 %collective-permute-start.6 = (f32[136,128]{1,0:T(8,128)S(1)}, f32[136,128]{1,0:T(8,128)S(1)}, u32[]{:S(2)}, u32[]{:S(2)}) collective-permute-start(f32[136,128]{1,0:T(8,128)S(1)} %select_maximum_fusion.1), channel_id=1, source_target_pairs={{0,128},{128,0},{256,384},{384,256},{1,129},{129,1},{257,385},{385... | collective-permute-start | bytes 208904 | tf_op jit(solution)/shard_map/ppermute | solution.py:327
  178.1 20.6 %all-to-all-start.5 = ((bf16[8,32,640]{2,1,0:T(8,128)(2,1)}), bf16[8,32,640]{2,1,0:T(8,128)(2,1)S(1)}, u32[]{:S(2)}, u32[]{:S(2)}) async-start(bf16[8,32,640]{2,1,0:T(8,128)(2,1)} %pad_maximum_fusion.3), calls=%async_computation.5 | async-start | bytes 655360 | tf_op jit(solution)/shard_map/all_to_all | solution.py:311
  183.1 10.1 %collective-permute-start.7 = (f32[136,256]{1,0:T(8,128)S(1)}, f32[136,256]{1,0:T(8,128)S(1)}, u32[]{:S(2)}, u32[]{:S(2)}) collective-permute-start(f32[136,256]{1,0:T(8,128)S(1)} %select_maximum_fusion), channel_id=1, source_target_pairs={{0,256},{128,384},{256,0},{384,128},{1,257},{129,385},{257,1},{385... | collective-permute-start | bytes 417800 | tf_op jit(solution)/shard_map/ppermute | solution.py:327
  193.3 4.4 %collective-permute-start.8 = (f32[128,512]{1,0:T(8,128)S(1)}, f32[128,512]{1,0:T(8,128)S(1)}, u32[]{:S(2)}, u32[]{:S(2)}) collective-permute-start(f32[128,512]{1,0:T(8,128)S(1)} %pad_maximum_fusion.5), channel_id=1, source_target_pairs={{0,8},{8,0},{1,9},{9,1},{2,10},{10,2},{3,11},{11,3},{4,12},{12,4},... | collective-permute-start | bytes 786440 | tf_op jit(solution)/shard_map/ppermute | solution.py:319
  199.8 1.6 copy-start.2
Sparse Core Ops, SparseCore 0:
  137.9 58.4 all-gather.1

commit v6 on v5

--- a/solution.py
+++ b/solution.py
@@ -23,7 +23,7 @@
 f32 = jnp.float32
 bf16 = jnp.bfloat16
 
-FWD_GROUP = 8
+FWD_GROUP = 12
 BWD_GROUP = 8
 NARROW = 2
 PARTS = 2

time: 213 us -> 215 us (level)
  waiting for transfers between devices: 60 us -> 62.4 us
    ppermute x3, starting transfers between devices: 15.4 us -> 9.02 us  [flip(): lax.ppermute(values, axis, [(i, i ^ by) for i in range(lax.axis_size(axis...]
    all_to_all x4, starting transfers between devices: 39.3 us -> 43.7 us  [exchange(): return lax.all_to_all(values, axes, split_axis=0, concat_axis=0, tiled=True)]
where the time goes in v6:
time: 215 us; the launch traced here: 211 us
  starting transfers between devices  73 us (34%)
  waiting for transfers between devices  62.4 us (29%)
  blocking collectives  35.3 us (16%)
  between operations  14.5 us (7%)
  Pallas kernels  13.1 us (6%)
  local copies, waits for them, and re-layouts  7.33 us (3%)
  other arithmetic  4.92 us (2%)
    all_to_all x4, starting transfers between devices, exchange(): return lax.all_to_all(values, axes, split_axis=0, concat_axis=0, tiled=True)  43.7 us
    all_to_all x2, blocking collectives, exchange(): return lax.all_to_all(values, axes, split_axis=0, concat_axis=0, tiled=True)  35.3 us
    all_to_all x4, waiting for transfers between devices, exchange(): return lax.all_to_all(values, axes, split_axis=0, concat_axis=0, tiled=True)  34.5 us
    ppermute x3, waiting for transfers between devices, flip(): lax.ppermute(values, axis, [(i, i ^ by) for i in range(lax.axis_size(axis...  22.1 us
    ppermute x3, starting transfers between devices, swap_core(): return lax.ppermute(values, 'core', [(0, 1), (1, 0)])  10.3 us
    ppermute x3, starting transfers between devices, shift_x(): return lax.ppermute(values, 'x', [(i, (i + by) % 4) for i in range(4)])  9.93 us
    ppermute x3, starting transfers between devices, flip(): lax.ppermute(values, axis, [(i, i ^ by) for i in range(lax.axis_size(axis...  9.02 us
    pallas_call x1, Pallas kernels, attend_grads(): pl.pallas_call(grads_kernel, out_shape=(jax.ShapeDtypeStruct((BLOCKS, 2,...  6.43 us
  transfers between devices with their start and end apart: 14, of which 8 were waited for; matrix products, arithmetic and copies ran while one was open for 4% of the time, Pallas kernels for 0%

profile of v6, /device:TPU:1, one launch (start us, length us, event | category | flops | bytes accessed | tf_op | source)
XLA Modules:
  0.0 211.1 jit_solution(5724179911142342772)
XLA Ops:
  9.3 15.7 %all-to-all-start.1 = ((bf16[16,32,256]{2,1,0:T(8,128)(2,1)}), bf16[16,32,256]{2,1,0:T(8,128)(2,1)S(1)}, u32[]{:S(2)}, u32[]{:S(2)}) async-start(bf16[16,32,256]{2,1,0:T(8,128)(2,1)} %pad_maximum_fusion.4), calls=%async_computation.1 | async-start | bytes 524288 | tf_op jit(solution)/shard_map/all_to_all | solution.py:311
  26.2 12.0 %all-to-all-done.1 = bf16[16,32,256]{2,1,0:T(8,128)(2,1)S(1)} async-done(((bf16[16,32,256]{2,1,0:T(8,128)(2,1)}), bf16[16,32,256]{2,1,0:T(8,128)(2,1)S(1)}, u32[]{:S(2)}, u32[]{:S(2)}) %all-to-all-start.1) | async-done | bytes 262176 | tf_op jit(solution)/shard_map/all_to_all | solution.py:311
  38.2 10.8 %all-to-all-start = ((bf16[8,32,1408]{2,1,0:T(8,128)(2,1)}), bf16[8,32,1408]{2,1,0:T(8,128)(2,1)S(1)}, u32[]{:S(2)}, u32[]{:S(2)}) async-start(bf16[8,32,1408]{2,1,0:T(8,128)(2,1)} %pad_maximum_fusion.1), calls=%async_computation | async-start | bytes 1441792 | tf_op jit(solution)/shard_map/all_to_all | solution.py:311
  49.8 3.1 %collective-permute-start = (bf16[512,256]{1,0:T(8,128)(2,1)S(1)}, bf16[512,256]{1,0:T(8,128)(2,1)S(1)}, u32[]{:S(2)}, u32[]{:S(2)}) collective-permute-start(bf16[512,256]{1,0:T(8,128)(2,1)S(1)} %bitcast.80), channel_id=1, source_target_pairs={{0,32},{32,64},{64,96},{96,0},{1,33},{33,65},{65,97},{97,1},{2,34}... | collective-permute-start | bytes 786440 | tf_op jit(solution)/shard_map/ppermute | solution.py:323
  52.9 3.4 %collective-permute-start.1 = (bf16[512,256]{1,0:T(8,128)(2,1)S(1)}, bf16[512,256]{1,0:T(8,128)(2,1)S(1)}, u32[]{:S(2)}, u32[]{:S(2)}) collective-permute-start(bf16[512,256]{1,0:T(8,128)(2,1)S(1)} %bitcast.81), channel_id=1, source_target_pairs={{0,96},{32,0},{64,32},{96,64},{1,97},{33,1},{65,33},{97,65},{2,98}... | collective-permute-start | bytes 786440 | tf_op jit(solution)/shard_map/ppermute | solution.py:323
  56.3 3.4 %collective-permute-start.2 = (bf16[512,256]{1,0:T(8,128)(2,1)S(1)}, bf16[512,256]{1,0:T(8,128)(2,1)S(1)}, u32[]{:S(2)}, u32[]{:S(2)}) collective-permute-start(bf16[512,256]{1,0:T(8,128)(2,1)S(1)} %bitcast.82), channel_id=1, source_target_pairs={{0,64},{32,96},{64,0},{96,32},{1,65},{33,97},{65,1},{97,33},{2,66}... | collective-permute-start | bytes 786440 | tf_op jit(solution)/shard_map/ppermute | solution.py:323
  61.6 4.3 %collective-permute-done.2 = bf16[512,256]{1,0:T(8,128)(2,1)S(1)} collective-permute-done((bf16[512,256]{1,0:T(8,128)(2,1)S(1)}, bf16[512,256]{1,0:T(8,128)(2,1)S(1)}, u32[]{:S(2)}, u32[]{:S(2)}) %collective-permute-start.2) | collective-permute-done | bytes 262176 | tf_op jit(solution)/shard_map/ppermute | solution.py:323
  66.0 4.4 %collective-permute-start.3 = (bf16[2048,256]{1,0:T(8,128)(2,1)S(1)}, bf16[2048,256]{1,0:T(8,128)(2,1)S(1)}, u32[]{:S(2)}, u32[]{:S(2)}) collective-permute-start(bf16[2048,256]{1,0:T(8,128)(2,1)S(1)} %pad_maximum_fusion.refs_0_), channel_id=1, source_target_pairs={{0,8},{8,0},{1,9},{9,1},{2,10},{10,2},{3,11},{11,3},{4,12},{12,4},... | collective-permute-start | bytes 3145736 | tf_op jit(solution)/shard_map/ppermute | solution.py:319
  70.8 4.8 %all-to-all-done = bf16[8,32,1408]{2,1,0:T(8,128)(2,1)S(1)} async-done(((bf16[8,32,1408]{2,1,0:T(8,128)(2,1)}), bf16[8,32,1408]{2,1,0:T(8,128)(2,1)S(1)}, u32[]{:S(2)}, u32[]{:S(2)}) %all-to-all-start) | async-done | bytes 720928 | tf_op jit(solution)/shard_map/all_to_all | solution.py:311
  76.3 4.0 %attend.1 = (f32[256,128]{1,0:T(8,128)S(1)}, bf16[4096,256]{1,0:T(8,128)(2,1)S(1)}) custom-call(s32[2,24]{1,0:T(2,128)S(1)} %multiply_add_fusion.1.pos_ref, s32[2,24]{1,0:T(2,128)S(1)} %get-tuple-element.54.home_ref, s32[2,24]{1,0:T(2,128)S(1)} %get-tuple-element.73.blk_ref, s32[2,24]{1,0:T(2,128)S(1)} %get-tuple-element.53.low_ref, ...), custom_call_target="tpu_custom_call" | custom-call | flops 5000000000 | bytes 3145728 | tf_op jit(solution)/shard_map/attend/pallas_call | solution.py:260
  80.8 24.0 %all_to_all.30.sums_ref = f32[8,4,256]{2,1,0:T(4,128)S(1)} all-to-all(f32[8,4,256]{2,1,0:T(4,128)S(1)} %broadcast_in_dim.14), channel_id=1, replica_groups=mesh['dp'=4,'x'=4,'zh'=2,'core'=2,'head'=8] {'head'}, dimensions={0} | all-to-all | bytes 65536 | tf_op jit(solution)/shard_map/all_to_all | solution.py:311
  105.3 6.4 %attend_grads.1 = (f32[32,2,128,128]{3,2,1,0:T(8,128)S(1)}, bf16[33,128,128]{2,1,0:T(8,128)(2,1)S(1)}, bf16[256,128]{1,0:T(8,128)(2,1)S(1)}, f32[17,8,128]{2,1,0:T(8,128)S(1)}) custom-call(s32[2,24]{1,0:T(2,128)S(1)} %multiply_add_fusion.1.pos_ref, s32[2,24]{1,0:T(2,128)S(1)} %get-tuple-element.54.home_ref, s32[2,24]{1,0:T(2,128)S(1)} %get-tuple-element.73.blk_ref, ...), custom_call_target="tpu_custom_call" | custom-call | flops 12000000000 | bytes 6291456 | tf_op jit(solution)/shard_map/attend_grads/pallas_call | solution.py:280
  111.7 1.9 collective-permute-start.4
  113.6 11.3 %all_to_all.31.weight_ref = bf16[8,128,128]{2,1,0:T(8,128)(2,1)S(1)} all-to-all(bf16[8,128,128]{2,1,0:T(8,128)(2,1)S(1)} %get-tuple-element.19), channel_id=1, replica_groups=mesh['dp'=4,'x'=4,'zh'=2,'core'=2,'head'=8] {'core','dp'}, dimensions={0} | all-to-all | bytes 524288 | tf_op jit(solution)/shard_map/all_to_all | solution.py:311
  126.2 9.0 %all-to-all-start.4 = ((bf16[4,1184,128]{2,1,0:T(8,128)(2,1)}), bf16[4,1184,128]{2,1,0:T(8,128)(2,1)S(1)}, u32[]{:S(2)}, u32[]{:S(2)}) async-start(bf16[4,1184,128]{2,1,0:T(8,128)(2,1)} %chip.1), calls=%async_computation.4 | async-start | bytes 2424832 | tf_op jit(solution)/shard_map/all_to_all | solution.py:311
  135.9 15.6 %all-to-all-done.4 = bf16[4,1184,128]{2,1,0:T(8,128)(2,1)S(1)} async-done(((bf16[4,1184,128]{2,1,0:T(8,128)(2,1)}), bf16[4,1184,128]{2,1,0:T(8,128)(2,1)S(1)}, u32[]{:S(2)}, u32[]{:S(2)}) %all-to-all-start.4) | async-done | bytes 1212448 | tf_op jit(solution)/shard_map/all_to_all | solution.py:311
  151.8 3.9 %collective-permute-start.5 = (bf16[672,128]{1,0:T(8,128)(2,1)S(1)}, bf16[672,128]{1,0:T(8,128)(2,1)S(1)}, u32[]{:S(2)}, u32[]{:S(2)}) collective-permute-start(bf16[672,128]{1,0:T(8,128)(2,1)S(1)} %pad_maximum_fusion.7), channel_id=1, source_target_pairs={{0,16},{16,0},{1,17},{17,1},{2,18},{18,2},{3,19},{19,3},{4,20},{20... | collective-permute-start | bytes 516104 | tf_op jit(solution)/shard_map/ppermute | solution.py:327
  155.8 17.3 %collective-permute-done.5 = bf16[672,128]{1,0:T(8,128)(2,1)S(1)} collective-permute-done((bf16[672,128]{1,0:T(8,128)(2,1)S(1)}, bf16[672,128]{1,0:T(8,128)(2,1)S(1)}, u32[]{:S(2)}, u32[]{:S(2)}) %collective-permute-start.5) | collective-permute-done | bytes 172064 | tf_op jit(solution)/shard_map/ppermute | solution.py:327
  173.3 2.5 %collective-permute-start.6 = (f32[136,128]{1,0:T(8,128)S(1)}, f32[136,128]{1,0:T(8,128)S(1)}, u32[]{:S(2)}, u32[]{:S(2)}) collective-permute-start(f32[136,128]{1,0:T(8,128)S(1)} %select_maximum_fusion.1), channel_id=1, source_target_pairs={{0,128},{128,0},{256,384},{384,256},{1,129},{129,1},{257,385},{385... | collective-permute-start | bytes 208904 | tf_op jit(solution)/shard_map/ppermute | solution.py:327
  176.8 8.1 %all-to-all-start.5 = ((bf16[8,32,640]{2,1,0:T(8,128)(2,1)}), bf16[8,32,640]{2,1,0:T(8,128)(2,1)S(1)}, u32[]{:S(2)}, u32[]{:S(2)}) async-start(bf16[8,32,640]{2,1,0:T(8,128)(2,1)} %pad_maximum_fusion.3), calls=%async_computation.5 | async-start | bytes 655360 | tf_op jit(solution)/shard_map/all_to_all | solution.py:311
  185.0 2.6 %collective-permute-start.7 = (f32[136,256]{1,0:T(8,128)S(1)}, f32[136,256]{1,0:T(8,128)S(1)}, u32[]{:S(2)}, u32[]{:S(2)}) collective-permute-start(f32[136,256]{1,0:T(8,128)S(1)} %select_maximum_fusion), channel_id=1, source_target_pairs={{0,256},{128,384},{256,0},{384,128},{1,257},{129,385},{257,1},{385... | collective-permute-start | bytes 417800 | tf_op jit(solution)/shard_map/ppermute | solution.py:327
  187.6 4.9 %collective-permute-done.7 = f32[136,256]{1,0:T(8,128)S(1)} collective-permute-done((f32[136,256]{1,0:T(8,128)S(1)}, f32[136,256]{1,0:T(8,128)S(1)}, u32[]{:S(2)}, u32[]{:S(2)}) %collective-permute-start.7) | collective-permute-done | bytes 139296 | tf_op jit(solution)/shard_map/ppermute | solution.py:327
  192.5 4.0 %collective-permute-start.8 = (f32[128,512]{1,0:T(8,128)S(1)}, f32[128,512]{1,0:T(8,128)S(1)}, u32[]{:S(2)}, u32[]{:S(2)}) collective-permute-start(f32[128,512]{1,0:T(8,128)S(1)} %pad_maximum_fusion.5), channel_id=1, source_target_pairs={{0,8},{8,0},{1,9},{9,1},{2,10},{10,2},{3,11},{11,3},{4,12},{12,4},... | collective-permute-start | bytes 786440 | tf_op jit(solution)/shard_map/ppermute | solution.py:319
  198.5 2.1 %all-to-all-done.5.back_ref = bf16[8,32,640]{2,1,0:T(8,128)(2,1)S(1)} async-done(((bf16[8,32,640]{2,1,0:T(8,128)(2,1)}), bf16[8,32,640]{2,1,0:T(8,128)(2,1)S(1)}, u32[]{:S(2)}, u32[]{:S(2)}) %all-to-all-start.5) | async-done | bytes 327712 | tf_op jit(solution)/shard_map/all_to_all | solution.py:311
  (90 shorter events, 16.8 us)
Async XLA Ops:
  7.2 41.9 %copy-start = (s32[1,32,24]{1,2,0:T(8,128)S(1)}, s32[1,32,24]{1,2,0:T(8,128)}, u32[]{:S(2)}) copy-start(s32[1,32,24]{1,2,0:T(8,128)} %param.10) | copy-start | bytes 9220
  7.2 17.9 %copy-start.3 = (bf16[128,1024]{1,0:T(8,128)(2,1)S(1)}, bf16[128,1024]{1,0:T(8,128)(2,1)}, u32[]{:S(2)}) copy-start(bf16[128,1024]{1,0:T(8,128)(2,1)} %param.8) | copy-start | bytes 786436
  7.2 17.9 %copy-start.4 = (bf16[1,32,1024]{2,1,0:T(8,128)(2,1)S(1)}, bf16[1,32,1024]{2,1,0:T(8,128)(2,1)}, u32[]{:S(2)}) copy-start(bf16[1,32,1024]{2,1,0:T(8,128)(2,1)} %param.7) | copy-start | bytes 196612
  9.3 28.9 %all-to-all-start.1 = ((bf16[16,32,256]{2,1,0:T(8,128)(2,1)}), bf16[16,32,256]{2,1,0:T(8,128)(2,1)S(1)}, u32[]{:S(2)}, u32[]{:S(2)}) async-start(bf16[16,32,256]{2,1,0:T(8,128)(2,1)} %pad_maximum_fusion.4), calls=%async_computation.1 | async-start | bytes 524288 | tf_op jit(solution)/shard_map/all_to_all | solution.py:311
  25.2 24.3 %copy-start.1 = (s32[1,4096]{1,0:T(1,128)S(1)}, s32[1,4096]{1,0:T(1,128)}, u32[]{:S(2)}) copy-start(s32[1,4096]{1,0:T(1,128)} %param.11) | copy-start | bytes 49156
  38.2 37.4 %all-to-all-start = ((bf16[8,32,1408]{2,1,0:T(8,128)(2,1)}), bf16[8,32,1408]{2,1,0:T(8,128)(2,1)S(1)}, u32[]{:S(2)}, u32[]{:S(2)}) async-start(bf16[8,32,1408]{2,1,0:T(8,128)(2,1)} %pad_maximum_fusion.1), calls=%async_computation | async-start | bytes 1441792 | tf_op jit(solution)/shard_map/all_to_all | solution.py:311
  49.8 11.8 %collective-permute-start = (bf16[512,256]{1,0:T(8,128)(2,1)S(1)}, bf16[512,256]{1,0:T(8,128)(2,1)S(1)}, u32[]{:S(2)}, u32[]{:S(2)}) collective-permute-start(bf16[512,256]{1,0:T(8,128)(2,1)S(1)} %bitcast.80), channel_id=1, source_target_pairs={{0,32},{32,64},{64,96},{96,0},{1,33},{33,65},{65,97},{97,1},{2,34}... | collective-permute-start | bytes 786440 | tf_op jit(solution)/shard_map/ppermute | solution.py:323
  52.9 8.7 %collective-permute-start.1 = (bf16[512,256]{1,0:T(8,128)(2,1)S(1)}, bf16[512,256]{1,0:T(8,128)(2,1)S(1)}, u32[]{:S(2)}, u32[]{:S(2)}) collective-permute-start(bf16[512,256]{1,0:T(8,128)(2,1)S(1)} %bitcast.81), channel_id=1, source_target_pairs={{0,96},{32,0},{64,32},{96,64},{1,97},{33,1},{65,33},{97,65},{2,98}... | collective-permute-start | bytes 786440 | tf_op jit(solution)/shard_map/ppermute | solution.py:323
  56.3 9.6 %collective-permute-start.2 = (bf16[512,256]{1,0:T(8,128)(2,1)S(1)}, bf16[512,256]{1,0:T(8,128)(2,1)S(1)}, u32[]{:S(2)}, u32[]{:S(2)}) collective-permute-start(bf16[512,256]{1,0:T(8,128)(2,1)S(1)} %bitcast.82), channel_id=1, source_target_pairs={{0,64},{32,96},{64,0},{96,32},{1,65},{33,97},{65,1},{97,33},{2,66}... | collective-permute-start | bytes 786440 | tf_op jit(solution)/shard_map/ppermute | solution.py:323
  59.8 10.9 %copy-start.5 = (f32[1,16]{1,0:T(1,128)S(1)}, f32[1,16]{1,0:T(1,128)}, u32[]{:S(2)}) copy-start(f32[1,16]{1,0:T(1,128)} %param.9) | copy-start | bytes 196
  66.0 10.3 %collective-permute-start.3 = (bf16[2048,256]{1,0:T(8,128)(2,1)S(1)}, bf16[2048,256]{1,0:T(8,128)(2,1)S(1)}, u32[]{:S(2)}, u32[]{:S(2)}) collective-permute-start(bf16[2048,256]{1,0:T(8,128)(2,1)S(1)} %pad_maximum_fusion.refs_0_), channel_id=1, source_target_pairs={{0,8},{8,0},{1,9},{9,1},{2,10},{10,2},{3,11},{11,3},{4,12},{12,4},... | collective-permute-start | bytes 3145736 | tf_op jit(solution)/shard_map/ppermute | solution.py:319
  111.7 13.3 %collective-permute-start.4 = (bf16[33,128,128]{2,1,0:T(8,128)(2,1)S(1)}, bf16[33,128,128]{2,1,0:T(8,128)(2,1)S(1)}, u32[]{:S(2)}, u32[]{:S(2)}) collective-permute-start(bf16[33,128,128]{2,1,0:T(8,128)(2,1)S(1)} %get-tuple-element.18), channel_id=1, source_target_pairs={{0,8},{8,0},{1,9},{9,1},{2,10},{10,2},{3,11},{11,3},{4,12},{12,4},... | collective-permute-start | bytes 3244040 | tf_op jit(solution)/shard_map/ppermute | solution.py:319
  126.2 25.3 %all-to-all-start.4 = ((bf16[4,1184,128]{2,1,0:T(8,128)(2,1)}), bf16[4,1184,128]{2,1,0:T(8,128)(2,1)S(1)}, u32[]{:S(2)}, u32[]{:S(2)}) async-start(bf16[4,1184,128]{2,1,0:T(8,128)(2,1)} %chip.1), calls=%async_computation.4 | async-start | bytes 2424832 | tf_op jit(solution)/shard_map/all_to_all | solution.py:311
  135.2 66.4 %all-gather.2.cloned.1.call-start = ((), (), s32[]{:S(2)}) async-start(), calls=%async_computation.6 | async-start | bytes 2162688 | tf_op jit(solution)/shard_map/all_gather | solution.py:377
  151.8 21.3 %collective-permute-start.5 = (bf16[672,128]{1,0:T(8,128)(2,1)S(1)}, bf16[672,128]{1,0:T(8,128)(2,1)S(1)}, u32[]{:S(2)}, u32[]{:S(2)}) collective-permute-start(bf16[672,128]{1,0:T(8,128)(2,1)S(1)} %pad_maximum_fusion.7), channel_id=1, source_target_pairs={{0,16},{16,0},{1,17},{17,1},{2,18},{18,2},{3,19},{19,3},{4,20},{20... | collective-permute-start | bytes 516104 | tf_op jit(solution)/shard_map/ppermute | solution.py:327
  173.3 11.7 %collective-permute-start.6 = (f32[136,128]{1,0:T(8,128)S(1)}, f32[136,128]{1,0:T(8,128)S(1)}, u32[]{:S(2)}, u32[]{:S(2)}) collective-permute-start(f32[136,128]{1,0:T(8,128)S(1)} %select_maximum_fusion.1), channel_id=1, source_target_pairs={{0,128},{128,0},{256,384},{384,256},{1,129},{129,1},{257,385},{385... | collective-permute-start | bytes 208904 | tf_op jit(solution)/shard_map/ppermute | solution.py:327
  176.8 23.8 %all-to-all-start.5 = ((bf16[8,32,640]{2,1,0:T(8,128)(2,1)}), bf16[8,32,640]{2,1,0:T(8,128)(2,1)S(1)}, u32[]{:S(2)}, u32[]{:S(2)}) async-start(bf16[8,32,640]{2,1,0:T(8,128)(2,1)} %pad_maximum_fusion.3), calls=%async_computation.5 | async-start | bytes 655360 | tf_op jit(solution)/shard_map/all_to_all | solution.py:311
  185.0 7.4 %collective-permute-start.7 = (f32[136,256]{1,0:T(8,128)S(1)}, f32[136,256]{1,0:T(8,128)S(1)}, u32[]{:S(2)}, u32[]{:S(2)}) collective-permute-start(f32[136,256]{1,0:T(8,128)S(1)} %select_maximum_fusion), channel_id=1, source_target_pairs={{0,256},{128,384},{256,0},{384,128},{1,257},{129,385},{257,1},{385... | collective-permute-start | bytes 417800 | tf_op jit(solution)/shard_map/ppermute | solution.py:327
  192.5 5.1 %collective-permute-start.8 = (f32[128,512]{1,0:T(8,128)S(1)}, f32[128,512]{1,0:T(8,128)S(1)}, u32[]{:S(2)}, u32[]{:S(2)}) collective-permute-start(f32[128,512]{1,0:T(8,128)S(1)} %pad_maximum_fusion.5), channel_id=1, source_target_pairs={{0,8},{8,0},{1,9},{9,1},{2,10},{10,2},{3,11},{11,3},{4,12},{12,4},... | collective-permute-start | bytes 786440 | tf_op jit(solution)/shard_map/ppermute | solution.py:319
  201.6 1.6 copy-start.2
Sparse Core Ops, SparseCore 0:
  139.7 51.5 all-gather.1
